TPU v7x, 32 devices: a whole 2x2x4 slice. The times are simulated.
32 devices in a mesh: rep: 2 (over x), pool: 8 (over z, y), tp: 2 (over core).
Axes of the slice: x: 2, y: 2, z: 4, core: 2. Of those that a mesh axis runs over, the one named last changes fastest.
Arguments:
- hidden: bfloat16 [1024, 8192], P(('rep', 'pool')), parts along dimension 0, may hold values from -6 to 6
- base_query: bfloat16 [1024, 8192], P(('rep', 'pool'), 'tp'), parts along dimension 0, may hold values from -160 to 160
- key_cache: bfloat16 [1024, 64, 1024], P(('rep', 'pool'), None, 'tp'), parts along dimension 0, may hold values from -12 to 12
- value_cache: bfloat16 [1024, 64, 1024], P(('rep', 'pool'), None, 'tp'), parts along dimension 0, may hold values from -6 to 6
- new_key: bfloat16 [1024, 1024], P(('rep', 'pool'), 'tp'), parts along dimension 0, may hold values from -6 to 6
- new_value: bfloat16 [1024, 1024], P(('rep', 'pool'), 'tp'), parts along dimension 0, may hold values from -6 to 6
- lengths: int32 [1024], P(('rep', 'pool')), parts along dimension 0, may hold values from 2 to 64, as said below
- request_adapter: int32 [1024], P(('rep', 'pool')), parts along dimension 0, may hold values from 0 to 15, as said below
- adapter_store_row: int32 [32], P('rep'), parts along dimension 0, may hold values from 0 to 15, as said below
- adapter_down: bfloat16 [16, 8192, 64], P('pool', 'tp'), may hold values from -0.0625 to 0.0625
- adapter_up: bfloat16 [16, 64, 8192], P('pool', None, 'tp'), may hold values from -0.75 to 0.75
Outputs:
- context: bfloat16 [1024, 8192], P(('rep', 'pool'), 'tp'), parts along dimension 0
There are 2 independent parts, one for each index of `rep`. A program takes and returns all parts, laid end to end along the dimension named above; an argument that names none is the same for every part. Nothing has to cross between parts.
Inputs may be any that keep to these rules, and one draw needn't show every extreme that they name: Each entry of each part is a different store row: a permutation. Adapter a lives with pool index adapter_store_row[a] // 2. `request_adapter`: within one group of 64 requests at most 16 requests have adapters held by one pool index; one pool index receives exactly 16 requests from every group. `lengths`: in every group some request uses all 64 positions.
All inputs are finite; a program needn't handle non-finite values.
Results may differ from a plain program's by a relative error of at most 0.0067.
Values may be sent and summed in bfloat16 or wider, within the bound.
No kernel may reach another device: no remote copies, remote signals or barrier semaphores. Data moves between devices by JAX's collectives and lax.ppermute only.
A program may use at most 64 MiB of HBM per device.

v0:
```python
import math

import jax
import jax.numpy as jnp
from jax import lax
from jax.sharding import PartitionSpec as P

HEAD_SIZE = 128


ADAPTER_SCALE = 2.0
MASKED = -1e30


def served_rows(query_features, store_indices, adapter_down, adapter_up):
    owned_count = adapter_down.shape[0]
    request_selector = store_indices == lax.broadcasted_iota(
        jnp.int32, store_indices.shape[:2] + (owned_count,), 2
    )
    partial_middle = jnp.einsum(
        "zoq,xqe->zoxe", query_features, adapter_down, preferred_element_type=jnp.float32
    )
    adapter_middle = jnp.sum(jnp.where(request_selector[..., None], partial_middle, 0.0), axis=2)
    adapter_middle = lax.psum(adapter_middle, "tp")
    adapter_output = jnp.einsum(
        "bzg,ugm->bzum",
        adapter_middle.astype(jnp.bfloat16),
        adapter_up,
        preferred_element_type=jnp.float32,
    )
    adapter_delta = ADAPTER_SCALE * jnp.sum(
        jnp.where(request_selector[..., None], adapter_output, 0.0), axis=2
    )
    return lax.all_to_all(
        adapter_delta.astype(jnp.bfloat16), "pool", split_axis=0, concat_axis=0, tiled=True
    )


def shards(
    hidden,
    base_query,
    key_cache,
    value_cache,
    new_key,
    new_value,
    lengths,
    request_adapter,
    adapter_store_row,
    adapter_down,
    adapter_up,
):
    request_rows = hidden.shape[0]
    pool_count = lax.axis_size("pool")
    capacity = max(2, 2 * request_rows // pool_count)
    slot_total = pool_count * capacity
    adapters = adapter_store_row.shape[0]
    owned_count = adapter_down.shape[0]
    half_width = adapter_down.shape[1]
    matches = request_adapter[:, None] == lax.broadcasted_iota(
        jnp.int32, (request_rows, adapters), 1
    )
    position = jnp.sum(jnp.where(matches, adapter_store_row[None, :], 0), axis=1)
    owner_of = position // owned_count
    held_slot = position % owned_count
    same_owner = owner_of[:, None] == owner_of[None, :]
    earlier = lax.broadcasted_iota(
        jnp.int32, (request_rows, request_rows), 1
    ) < lax.broadcasted_iota(jnp.int32, (request_rows, request_rows), 0)
    order_rank = jnp.sum(jnp.where(same_owner & earlier, 1, 0), axis=1).astype(jnp.int32)
    target = owner_of * capacity + order_rank
    routing = lax.broadcasted_iota(jnp.int32, (slot_total, request_rows), 0) == target[None, :]
    store_indices = jnp.sum(jnp.where(routing, held_slot[None, :] + 1, 0), axis=1) - 1
    store_indices = store_indices.reshape(pool_count, capacity, 1)
    routing_b = routing.astype(jnp.bfloat16)
    query_features = lax.dynamic_slice_in_dim(
        hidden, lax.axis_index("tp") * half_width, half_width, 1
    )
    packed = jnp.dot(routing_b, query_features, preferred_element_type=jnp.float32).astype(
        jnp.bfloat16
    )
    returned = served_rows(
        lax.all_to_all(
            packed.reshape(pool_count, capacity, half_width),
            "pool",
            split_axis=0,
            concat_axis=0,
            tiled=True,
        ),
        lax.all_to_all(store_indices, "pool", split_axis=0, concat_axis=0, tiled=True),
        adapter_down,
        adapter_up,
    )
    adapter_delta = jnp.einsum(
        "sr,sd->rd",
        routing_b,
        returned.reshape(slot_total, returned.shape[2]),
        preferred_element_type=jnp.float32,
    ).astype(jnp.bfloat16)
    head_count = base_query.shape[1] // HEAD_SIZE
    cached_count = key_cache.shape[2] // HEAD_SIZE
    group_size = head_count // cached_count
    cached_len = key_cache.shape[1]
    factor = 1.0 / math.sqrt(HEAD_SIZE)
    base_heads = base_query.reshape(request_rows, cached_count, group_size, HEAD_SIZE)
    head_delta = adapter_delta.reshape(request_rows, cached_count, group_size, HEAD_SIZE)
    cached_k = key_cache.reshape(request_rows, cached_len, cached_count, HEAD_SIZE)
    cached_v = value_cache.reshape(request_rows, cached_len, cached_count, HEAD_SIZE)
    fresh_k = new_key.reshape(request_rows, cached_count, HEAD_SIZE)
    fresh_v = new_value.reshape(request_rows, cached_count, HEAD_SIZE)
    scores = jnp.einsum("rkgd,rpkd->rkgp", base_heads, cached_k, preferred_element_type=jnp.float32)
    scores = (
        scores
        + jnp.einsum("rkgd,rpkd->rkgp", head_delta, cached_k, preferred_element_type=jnp.float32)
    ) * factor
    usable = lax.broadcasted_iota(jnp.int32, (request_rows, cached_len), 1) < lengths[:, None]
    scores = jnp.where(usable[:, None, None, :], scores, MASKED)
    own_score = jnp.einsum("rkgd,rkd->rkg", base_heads, fresh_k, preferred_element_type=jnp.float32)
    own_score = (
        own_score
        + jnp.einsum("rkgd,rkd->rkg", head_delta, fresh_k, preferred_element_type=jnp.float32)
    ) * factor
    highest = jnp.maximum(jnp.max(scores, axis=-1), own_score)
    weights = jnp.exp(scores - highest[..., None])
    own_weight = jnp.exp(own_score - highest)
    totals = jnp.sum(weights, axis=-1) + own_weight
    weights_b = weights.astype(jnp.bfloat16)
    own_b = own_weight.astype(jnp.bfloat16)
    mixed = jnp.einsum("rkgp,rpkd->rkgd", weights_b, cached_v, preferred_element_type=jnp.float32)
    mixed = (
        mixed + own_b.astype(jnp.float32)[..., None] * fresh_v.astype(jnp.float32)[:, :, None, :]
    )
    mixed = mixed / totals[..., None]
    return mixed.reshape(request_rows, head_count * HEAD_SIZE).astype(jnp.bfloat16)


def solution(mesh):
    placed = (
        P(("rep", "pool"), None),
        P(("rep", "pool"), "tp"),
        P(("rep", "pool"), None, "tp"),
        P(("rep", "pool"), None, "tp"),
        P(("rep", "pool"), "tp"),
        P(("rep", "pool"), "tp"),
        P(("rep", "pool")),
        P(("rep", "pool")),
        P("rep"),
        P("pool", "tp", None),
        P("pool", None, "tp"),
    )
    return jax.shard_map(
        shards, mesh=mesh, in_specs=placed, out_specs=P(("rep", "pool"), "tp"), check_vma=False
    )
```

profile of v0, /device:TPU:0, one launch (start us, length us, event | category | flops | bytes accessed | tf_op | source)
XLA Modules:
  0.0 94.3 jit_solution(3535517643293795077)
XLA Ops:
  0.0 0.0 copy-start
  0.0 0.8 select_reduce_fusion.2
  0.9 0.2 select_reduce_fusion.1
  1.1 0.1 select_reduce_fusion
  1.2 0.7 sub.25
  1.8 7.3 %all-to-all-start = ((s32[8,16,1]{1,2,0:T(1,128)}), s32[8,16,1]{1,2,0:T(1,128)S(1)}, u32[]{:S(2)}, u32[]{:S(2)}) async-start(s32[8,16,1]{1,2,0:T(1,128)} %bitcast), calls=%async_computation | async-start | bytes 8192 | tf_op jit(solution)/shard_map/all_to_all | solution.py:89
  9.1 0.0 copy-done
  9.1 1.5 %convolution_convert_fusion = bf16[128,4096]{1,0:T(8,128)(2,1)} fusion(bf16[64,8192]{1,0:T(8,128)(2,1)S(1)} %copy-done, s32[]{:T(128)S(6)} %select_n.59, s32[64]{0:T(128)S(1)} %multiply_add_fusion), kind=kOutput, calls=%fused_computation.1 | convolution fusion | flops 67641344 | bytes 1573380 | tf_op jit(solution)/shard_map/dot_general | solution.py:78
  10.7 4.8 %all-to-all-done = s32[8,16,1]{1,2,0:T(1,128)S(1)} async-done(((s32[8,16,1]{1,2,0:T(1,128)}), s32[8,16,1]{1,2,0:T(1,128)S(1)}, u32[]{:S(2)}, u32[]{:S(2)}) %all-to-all-start) | async-done | bytes 544 | tf_op jit(solution)/shard_map/all_to_all | solution.py:89
  15.5 3.6 %all-to-all-start.1 = ((bf16[8,16,4096]{2,1,0:T(8,128)(2,1)}), bf16[8,16,4096]{2,1,0:T(8,128)(2,1)S(1)}, u32[]{:S(2)}, u32[]{:S(2)}) async-start(bf16[8,16,4096]{2,1,0:T(8,128)(2,1)} %bitcast.2), calls=%async_computation.1 | async-start | bytes 2097152 | tf_op jit(solution)/shard_map/all_to_all | solution.py:82
  19.1 24.7 %all-to-all-done.1 = bf16[8,16,4096]{2,1,0:T(8,128)(2,1)S(1)} async-done(((bf16[8,16,4096]{2,1,0:T(8,128)(2,1)}), bf16[8,16,4096]{2,1,0:T(8,128)(2,1)S(1)}, u32[]{:S(2)}, u32[]{:S(2)}) %all-to-all-start.1) | async-done | bytes 1048608 | tf_op jit(solution)/shard_map/all_to_all | solution.py:82
  43.8 1.9 %fusion.23 = f32[8,16,64]{2,1,0:T(8,128)S(1)} fusion(bf16[8,16,4096]{2,1,0:T(8,128)(2,1)S(1)} %all-to-all-done.1, bf16[2,4096,64]{1,2,0:T(8,128)(2,1)} %param.20, pred[8,16,2]{1,2,0:T(4,128)(4,1)S(1)} %iota_compare_fusion.5), kind=kOutput, calls=%fused_computation.20 | convolution fusion | flops 134242304 | bytes 2130176 | tf_op jit(solution)/shard_map/zoq,xqe->zoxe/dot_general | solution.py:20
  45.8 3.6 %psum.7 = bf16[8,16,64]{2,1,0:T(8,128)(2,1)S(1)} all-reduce(f32[8,16,64]{2,1,0:T(8,128)S(1)} %fusion.23), channel_id=1, replica_groups=mesh['rep'=2,'pool'=8,'tp'=2] {'tp'}, use_global_device_ids=true, to_apply=%region_4.5 | all-reduce | flops 8192 | bytes 49152 | tf_op jit(solution)/shard_map/psum | solution.py:24
  49.4 0.0 copy-start.2
  49.4 0.0 copy-start.3
  49.4 0.0 copy-start.4
  49.4 2.2 %fusion.9 = f32[8,16,4096]{2,1,0:T(8,128)S(1)} fusion(pred[8,16,2]{1,2,0:T(4,128)(4,1)S(1)} %iota_compare_fusion.5, bf16[2,64,4096]{2,1,0:T(8,128)(2,1)} %param.21, bf16[8,16,64]{2,1,0:T(8,128)(2,1)S(1)} %psum.7), kind=kOutput, calls=%fused_computation.13 | convolution fusion | flops 135790592 | bytes 3162368 | tf_op jit(solution)/shard_map/bzg,ugm->bzum/dot_general | solution.py:25
  51.6 0.0 copy-start.5
  51.7 1.1 %multiply_convert_fusion = bf16[8,16,4096]{2,1,0:T(8,128)(2,1)} fusion(f32[8,16,4096]{2,1,0:T(8,128)S(1)} %fusion.9), kind=kLoop, calls=%fused_computation.12 | loop fusion | flops 1048576 | bytes 3145728 | tf_op jit(solution)/shard_map/convert_element_type | solution.py:35
  52.8 3.6 %all-to-all-start.2 = ((bf16[8,16,4096]{2,1,0:T(8,128)(2,1)}), bf16[8,16,4096]{2,1,0:T(8,128)(2,1)S(1)}, u32[]{:S(2)}, u32[]{:S(2)}) async-start(bf16[8,16,4096]{2,1,0:T(8,128)(2,1)} %multiply_convert_fusion), calls=%async_computation.2 | async-start | bytes 2097152 | tf_op jit(solution)/shard_map/all_to_all | solution.py:34
  56.3 0.0 copy-done.2
  56.4 0.1 copy.32
  56.5 0.0 copy-done.3
  56.5 0.0 copy-done.4
  56.6 0.0 copy-done.5
  56.6 0.1 iota_compare_fusion.4
  56.6 0.4 fusion.48
  57.1 25.7 %all-to-all-done.2 = bf16[8,16,4096]{2,1,0:T(8,128)(2,1)S(1)} async-done(((bf16[8,16,4096]{2,1,0:T(8,128)(2,1)}), bf16[8,16,4096]{2,1,0:T(8,128)(2,1)S(1)}, u32[]{:S(2)}, u32[]{:S(2)}) %all-to-all-start.2) | async-done | bytes 1048608 | tf_op jit(solution)/shard_map/all_to_all | solution.py:34
  82.8 0.3 fusion.22
  83.2 0.0 copy-start.1
  83.2 0.1 copy.33
  83.3 0.4 fusion.49
  83.7 4.7 %fusion.3 = f32[64,4,8,64]{3,2,1,0:T(8,128)S(1)} fusion(bf16[64,4,8,128]{3,2,1,0:T(8,128)(2,1)S(1)} %bitcast.80, bf16[64,64,512]{2,1,0:T(8,128)(2,1)} %param.13), kind=kOutput, calls=%fused_computation.6 | convolution fusion | flops 33554432 | bytes 5242880 | tf_op jit(solution)/shard_map/rkgd,rpkd->rkgp/dot_general | solution.py:113
  88.4 0.0 copy-done.1
  88.4 0.0 copy-start.6
  88.4 2.5 %fusion.47 = (f32[64,4,8]{2,1,0:T(4,128)S(1)}, f32[64,4,8,64]{3,2,1,0:T(8,128)S(1)}) fusion(f32[64,4,8,64]{3,2,1,0:T(8,128)S(1)} %fusion.3, bf16[64,4,8,128]{3,2,1,0:T(8,128)(2,1)S(1)} %bitcast.78, pred[64,64]{1,0:T(8,128)(4,1)S(1)} %iota_compare_fusion.4, bf16[64,64,512]{2,1,0:T(8,128)(2,1)S(1)} %copy-done.1), kind=kOutput, calls=%fused_computation.59 | convolution fusion | flops 34076672 | bytes 5779456 | tf_op jit(solution)/shard_map/rkgd,rpkd->rkgp/dot_general | solution.py:110
  90.9 0.1 fusion.38
  90.9 0.8 fusion.33
  91.7 0.1 convert_convert_fusion
  91.8 0.0 copy-done.6
  91.8 1.5 %fusion.27 = bf16[64,4,8,128]{3,2,1,0:T(8,128)(2,1)S(1)} fusion(f32[64,4,8,64]{3,2,1,0:T(8,128)S(1)} %get-tuple-element.10, f32[64,4,8]{2,1,0:T(4,128)S(1)} %get-tuple-element.6, f32[64,4,128]{2,1,0:T(4,128)S(1)} %reshape.130, f32[64,4,8]{2,1,0:T(4,128)S(1)} %get-tuple-element.5, f32[64,4,8]{2,1,0:T(4,128)S(1)} %fusion.38, ...), kind=kOutput, calls=%fused_computation.22 | convolution fusion | flops 34865152 | bytes 5398528 | tf_op jit(solution)/shard_map/rkgp,rpkd->rkgd/dot_general | solution.py:128
  93.3 1.0 %copy.62 = bf16[8,8,32,128]{3,1,2,0:T(8,128)(2,1)} copy(bf16[8,8,32,128]{3,2,1,0:T(8,128)(2,1)S(1)} %bitcast.82) | data formatting | bytes 1048576
  (6 shorter events, 0.1 us)
Async XLA Ops:
  0.0 9.1 %copy-start = (bf16[64,8192]{1,0:T(8,128)(2,1)S(1)}, bf16[64,8192]{1,0:T(8,128)(2,1)}, u32[]{:S(2)}) copy-start(bf16[64,8192]{1,0:T(8,128)(2,1)} %param.11) | copy-start | bytes 3145732
  1.8 13.7 %all-to-all-start = ((s32[8,16,1]{1,2,0:T(1,128)}), s32[8,16,1]{1,2,0:T(1,128)S(1)}, u32[]{:S(2)}, u32[]{:S(2)}) async-start(s32[8,16,1]{1,2,0:T(1,128)} %bitcast), calls=%async_computation | async-start | bytes 8192 | tf_op jit(solution)/shard_map/all_to_all | solution.py:89
  15.5 28.3 %all-to-all-start.1 = ((bf16[8,16,4096]{2,1,0:T(8,128)(2,1)}), bf16[8,16,4096]{2,1,0:T(8,128)(2,1)S(1)}, u32[]{:S(2)}, u32[]{:S(2)}) async-start(bf16[8,16,4096]{2,1,0:T(8,128)(2,1)} %bitcast.2), calls=%async_computation.1 | async-start | bytes 2097152 | tf_op jit(solution)/shard_map/all_to_all | solution.py:82
  49.4 7.0 %copy-start.2 = (bf16[64,4096]{1,0:T(8,128)(2,1)S(1)}, bf16[64,4096]{1,0:T(8,128)(2,1)}, u32[]{:S(2)}) copy-start(bf16[64,4096]{1,0:T(8,128)(2,1)} %param.12) | copy-start | bytes 1572868
  49.4 7.1 %copy-start.3 = (bf16[64,512]{1,0:T(8,128)(2,1)S(1)}, bf16[64,512]{1,0:T(8,128)(2,1)}, u32[]{:S(2)}) copy-start(bf16[64,512]{1,0:T(8,128)(2,1)} %param.15) | copy-start | bytes 196612
  49.4 7.1 %copy-start.4 = (bf16[64,512]{1,0:T(8,128)(2,1)S(1)}, bf16[64,512]{1,0:T(8,128)(2,1)}, u32[]{:S(2)}) copy-start(bf16[64,512]{1,0:T(8,128)(2,1)} %param.16) | copy-start | bytes 196612
  51.6 4.9 %copy-start.5 = (s32[64]{0:T(128)S(1)}, s32[64]{0:T(128)}, u32[]{:S(2)}) copy-start(s32[64]{0:T(128)} %param.17) | copy-start | bytes 772
  52.8 30.0 %all-to-all-start.2 = ((bf16[8,16,4096]{2,1,0:T(8,128)(2,1)}), bf16[8,16,4096]{2,1,0:T(8,128)(2,1)S(1)}, u32[]{:S(2)}, u32[]{:S(2)}) async-start(bf16[8,16,4096]{2,1,0:T(8,128)(2,1)} %multiply_convert_fusion), calls=%async_computation.2 | async-start | bytes 2097152 | tf_op jit(solution)/shard_map/all_to_all | solution.py:34
  83.2 5.2 %copy-start.1 = (bf16[64,64,512]{2,1,0:T(8,128)(2,1)S(1)}, bf16[64,64,512]{2,1,0:T(8,128)(2,1)}, u32[]{:S(2)}) copy-start(bf16[64,64,512]{2,1,0:T(8,128)(2,1)} %param.13) | copy-start | bytes 12582916
  88.4 3.4 %copy-start.6 = (bf16[64,64,512]{2,1,0:T(8,128)(2,1)S(1)}, bf16[64,64,512]{2,1,0:T(8,128)(2,1)}, u32[]{:S(2)}) copy-start(bf16[64,64,512]{2,1,0:T(8,128)(2,1)} %param.14) | copy-start | bytes 12582916
where the time goes:
time: 94.7 us; the launch traced here: 94.3 us
  waiting for transfers between devices  55.3 us (58%)
  matrix products  15.5 us (16%)
  starting transfers between devices  14.4 us (15%)
  blocking collectives  3.62 us (4%)
  other arithmetic  3.27 us (3%)
  local copies, waits for them, and re-layouts  1.98 us (2%)
    all_to_all x1, waiting for transfers between devices, served_rows(): lax.all_to_all(adapter_delta.astype(jnp.bfloat16), 'pool', split_axis=0,...  25.7 us
    all_to_all x1, waiting for transfers between devices, shards(): lax.all_to_all(packed.reshape(pool_count, capacity, half_width), 'pool',...  24.7 us
    all_to_all x1, starting transfers between devices, shards(): lax.all_to_all(store_indices, 'pool', split_axis=0, concat_axis=0, tiled=...  7.28 us
    all_to_all x1, waiting for transfers between devices, shards(): lax.all_to_all(store_indices, 'pool', split_axis=0, concat_axis=0, tiled=...  4.84 us
    dot_general x1, matrix products, shards(): jnp.einsum('rkgd,rpkd->rkgp', head_delta, cached_k, preferred_element_typ...  4.7 us
    psum x1, blocking collectives, served_rows(): adapter_middle = lax.psum(adapter_middle, 'tp')  3.62 us
    all_to_all x1, starting transfers between devices, shards(): lax.all_to_all(packed.reshape(pool_count, capacity, half_width), 'pool',...  3.56 us
    all_to_all x1, starting transfers between devices, served_rows(): lax.all_to_all(adapter_delta.astype(jnp.bfloat16), 'pool', split_axis=0,...  3.56 us
  transfers between devices with their start and end apart: 3, of which 3 were waited for; matrix products, arithmetic and copies ran while one was open for 2% of the time, Pallas kernels for 0%

commit v1 on v0

v1 whole, which is shorter than its diff:
```python
import functools
import math

import jax
import jax.numpy as jnp
from jax import lax
from jax.experimental import pallas as pl
from jax.experimental.pallas import tpu as pltpu
from jax.sharding import PartitionSpec as P

HEAD_SIZE = 128
ADAPTER_SCALE = 2.0
MASKED = -1e30
LANES = 128
ROWS = 16
MIB = 1024 * 1024

VMEM = pl.BlockSpec(memory_space=pltpu.VMEM)
ANYWHERE = pl.BlockSpec(memory_space=pl.ANY)


def grant(mib):
    return pltpu.CompilerParams(vmem_limit_bytes=mib * MIB)


def column_of(row):
    count = row.shape[1]
    here = lax.broadcasted_iota(jnp.int32, (count, count), 0)
    there = lax.broadcasted_iota(jnp.int32, (count, count), 1)
    spread = jnp.broadcast_to(row, (count, count))
    return jnp.sum(jnp.where(here == there, spread, 0), axis=1, keepdims=True)


def as_bf16(mask):
    return mask.astype(jnp.float32).astype(jnp.bfloat16)


def pack_kernel(pool_count, capacity, owned_count, splits, adapter_hbm, store_hbm, hidden_hbm, *refs):
    outs = refs[: len(splits)]
    routing_ref, adapter_ref, store_ref, held_ref, sems, index_sems = refs[len(splits) :]
    width = held_ref.shape[1]
    chunks = sems.shape[0]
    step = width // chunks
    start = lax.axis_index("tp") * width
    small = [
        pltpu.make_async_copy(adapter_hbm, adapter_ref, index_sems.at[0]),
        pltpu.make_async_copy(store_hbm, store_ref, index_sems.at[1]),
    ]
    copies = [
        pltpu.make_async_copy(
            hidden_hbm.at[:, pl.ds(pl.multiple_of(start + c * step, LANES), step)],
            held_ref.at[:, pl.ds(c * step, step)],
            sems.at[c],
        )
        for c in range(chunks)
    ]
    for copy in small + copies:
        copy.start()
    for copy in small:
        copy.wait()
    adapters = store_ref.shape[1]
    requests = adapter_ref.shape[1]
    matches = lax.broadcasted_iota(jnp.int32, (adapters, requests), 0) == adapter_ref[...]
    position = jnp.sum(jnp.where(matches, column_of(store_ref[...]), 0), axis=0, keepdims=True)
    owner = lax.div(position, jnp.int32(owned_count))
    held = position - owner * owned_count
    distance = lax.bitwise_xor(owner, jnp.broadcast_to(lax.axis_index("pool"), owner.shape))
    earlier = lax.broadcasted_iota(jnp.int32, (requests, requests), 0) < lax.broadcasted_iota(
        jnp.int32, (requests, requests), 1
    )
    same = column_of(owner) == owner
    rank = jnp.sum(jnp.where(same & earlier, 1, 0), axis=0, keepdims=True)
    target = distance * capacity + rank
    slot_total = pool_count * capacity
    routing = lax.broadcasted_iota(jnp.int32, (slot_total, requests), 0) == target
    held_slot = jnp.sum(jnp.where(routing, held, 0), axis=1, keepdims=True)
    tags = jnp.broadcast_to(held_slot, (slot_total, LANES)).astype(jnp.float32).astype(jnp.bfloat16)
    routing_b = as_bf16(routing)
    back = lax.broadcasted_iota(jnp.int32, (requests, slot_total), 1) == column_of(target)
    routing_ref[...] = as_bf16(back)
    for out, (first, size) in zip(outs, splits):
        out[:, width:] = tags[first : first + size]
    for c, copy in enumerate(copies):
        copy.wait()
        columns = slice(c * step, (c + 1) * step)
        packed = jnp.dot(
            routing_b, held_ref[:, columns], preferred_element_type=jnp.float32
        ).astype(jnp.bfloat16)
        for out, (first, size) in zip(outs, splits):
            out[:, columns] = packed[first : first + size]


def pack(hidden, request_adapter, adapter_store_row, pool_count, capacity, owned_count, width, splits):
    requests = hidden.shape[0]
    adapters = adapter_store_row.shape[0]
    slot_total = pool_count * capacity
    chunks = 4
    return pl.pallas_call(
        functools.partial(pack_kernel, pool_count, capacity, owned_count, splits),
        out_shape=[jax.ShapeDtypeStruct((size, width + LANES), jnp.bfloat16) for _, size in splits]
        + [jax.ShapeDtypeStruct((requests, slot_total), jnp.bfloat16)],
        in_specs=[ANYWHERE] * 3,
        out_specs=[VMEM] * (len(splits) + 1),
        scratch_shapes=[
            pltpu.VMEM((1, requests), jnp.int32),
            pltpu.VMEM((1, adapters), jnp.int32),
            pltpu.VMEM((requests, width), jnp.bfloat16),
            pltpu.SemaphoreType.DMA((chunks,)),
            pltpu.SemaphoreType.DMA((2,)),
        ],
        compiler_params=grant(8),
        name="pack",
    )(request_adapter.reshape(1, requests), adapter_store_row.reshape(1, adapters), hidden)


def down_kernel(count, *refs):
    rows, down_ref, out_ref = refs[:count], refs[count], refs[count + 1]
    owned_count, _, width = down_ref.shape
    features = jnp.concatenate([row[:, :width] for row in rows], axis=0)
    tags = jnp.concatenate([row[:, width : width + 1] for row in rows], axis=0).astype(jnp.float32)
    total = jnp.zeros(out_ref.shape, jnp.float32)
    for slot in range(owned_count):
        partial = lax.dot_general(
            features,
            down_ref[slot],
            (((1,), (1,)), ((), ())),
            preferred_element_type=jnp.float32,
        )
        total = total + jnp.where(tags == float(slot), partial, 0.0)
    out_ref[...] = total


def down(rows, adapter_down):
    total = sum(row.shape[0] for row in rows)
    rank = adapter_down.shape[1]
    return pl.pallas_call(
        functools.partial(down_kernel, len(rows)),
        out_shape=jax.ShapeDtypeStruct((total, rank), jnp.float32),
        in_specs=[VMEM] * (len(rows) + 1),
        out_specs=VMEM,
        compiler_params=grant(8),
        cost_estimate=pl.CostEstimate(
            flops=2 * total * adapter_down.size, bytes_accessed=2 * adapter_down.size, transcendentals=0
        ),
        name="down",
    )(*rows, adapter_down)


def up_kernel(count, mine_ref, other_ref, up_ref, *refs):
    rows, outs = refs[:count], refs[count:]
    owned_count, _, width = up_ref.shape
    tags = jnp.concatenate([row[:, :1] for row in rows], axis=0).astype(jnp.float32)
    middle = (mine_ref[...] + other_ref[...]).astype(jnp.bfloat16).astype(jnp.float32)
    chosen = jnp.concatenate(
        [jnp.where(tags == float(slot), middle, 0.0) for slot in range(owned_count)], axis=1
    ).astype(jnp.bfloat16)
    step = min(width, 1024)
    for c in range(width // step):
        columns = slice(c * step, (c + 1) * step)
        factors = jnp.concatenate([up_ref[slot, :, columns] for slot in range(owned_count)], axis=0)
        total = jnp.dot(chosen, factors, preferred_element_type=jnp.float32)
        total = (ADAPTER_SCALE * total).astype(jnp.bfloat16)
        at = 0
        for out in outs:
            out[:, columns] = total[at : at + out.shape[0]]
            at += out.shape[0]


def up(mine, other, rows, adapter_up):
    width = adapter_up.shape[2]
    total = mine.shape[0]
    tag_at = rows[0].shape[1] // LANES - 1
    return pl.pallas_call(
        functools.partial(up_kernel, len(rows)),
        grid=(1,),
        out_shape=[jax.ShapeDtypeStruct((row.shape[0], width), jnp.bfloat16) for row in rows],
        in_specs=[VMEM] * 3
        + [pl.BlockSpec((row.shape[0], LANES), lambda i: (0, tag_at)) for row in rows],
        out_specs=[VMEM] * len(rows),
        compiler_params=grant(8),
        cost_estimate=pl.CostEstimate(
            flops=2 * total * adapter_up.size, bytes_accessed=2 * adapter_up.size, transcendentals=0
        ),
        name="up",
    )(mine, other, adapter_up, *rows)


def serve(rows, adapter_down, adapter_up, tp_count):
    mine = down(rows, adapter_down)
    other = lax.ppermute(mine, "tp", [(i, tp_count - 1 - i) for i in range(tp_count)])
    return up(mine, other, rows, adapter_up)


def prepare_kernel(base_ref, lengths_ref, heads_ref, valid_ref):
    requests = base_ref.shape[0]
    cached_count, rows, _ = heads_ref.shape
    group_size = rows // requests
    for j in range(cached_count):
        for h in range(group_size):
            at = (j * group_size + h) * HEAD_SIZE
            heads_ref[j, pl.ds(h, requests, stride=group_size), :] = base_ref[
                :, at : at + HEAD_SIZE
            ].astype(jnp.float32)
    cached_len = valid_ref.shape[1] - requests
    place = lax.broadcasted_iota(jnp.int32, (requests, cached_len + requests), 1)
    own = place - cached_len == lax.broadcasted_iota(jnp.int32, place.shape, 0)
    inside = (place < column_of(lengths_ref[...])) & (place < cached_len)
    allowed = (inside | own).astype(jnp.float32)
    for h in range(group_size):
        valid_ref[pl.ds(h, requests, stride=group_size), :] = allowed


def prepare(base_query, lengths, cached_len, cached_count):
    requests, features = base_query.shape
    rows = requests * features // (HEAD_SIZE * cached_count)
    return pl.pallas_call(
        prepare_kernel,
        out_shape=[
            jax.ShapeDtypeStruct((cached_count, rows, HEAD_SIZE), jnp.float32),
            jax.ShapeDtypeStruct((rows, cached_len + requests), jnp.float32),
        ],
        in_specs=[VMEM] * 2,
        out_specs=[VMEM] * 2,
        compiler_params=grant(8),
        name="prepare",
    )(base_query, lengths.reshape(1, requests))


def attend_kernel(
    count, heads_ref, valid_ref, routing_ref, key_ref, value_ref, fresh_k_ref, fresh_v_ref, *refs
):
    returned, out_ref, delta_ref, score_ref, mixed_ref = refs[:count], *refs[count:]
    requests, cached_len, _ = key_ref.shape
    cached_count, rows, _ = heads_ref.shape
    group_size = rows // requests
    factor = 1.0 / math.sqrt(HEAD_SIZE)
    across = (((1,), (1,)), ((), ()))
    for j in range(cached_count):
        lanes = slice(j * HEAD_SIZE, (j + 1) * HEAD_SIZE)
        wide = slice(j * group_size * HEAD_SIZE, (j + 1) * group_size * HEAD_SIZE)
        arrived = jnp.concatenate([piece[:, wide] for piece in returned], axis=0)
        delta = jnp.dot(routing_ref[...], arrived, preferred_element_type=jnp.float32)
        for h in range(group_size):
            delta_ref[pl.ds(h, requests, stride=group_size), :] = delta[
                :, h * HEAD_SIZE : (h + 1) * HEAD_SIZE
            ]
        for r in range(requests):
            here = slice(r * group_size, (r + 1) * group_size)
            pair = jnp.concatenate([heads_ref[j, here, :], delta_ref[here, :]], axis=0)
            both = lax.dot_general(
                pair.astype(jnp.bfloat16),
                key_ref[r, :, lanes],
                across,
                preferred_element_type=jnp.float32,
            )
            score_ref[here, :cached_len] = both[:group_size] + both[group_size:]
        own = lax.dot_general(
            heads_ref[j].astype(jnp.bfloat16),
            fresh_k_ref[:, lanes],
            across,
            preferred_element_type=jnp.float32,
        ) + lax.dot_general(
            delta_ref[...].astype(jnp.bfloat16),
            fresh_k_ref[:, lanes],
            across,
            preferred_element_type=jnp.float32,
        )
        score_ref[:, cached_len:] = own
        scores = jnp.where(valid_ref[...] > 0.0, score_ref[...] * factor, MASKED)
        highest = jnp.max(scores, axis=1, keepdims=True)
        weights = jnp.exp(scores - highest)
        totals = jnp.sum(weights, axis=1, keepdims=True)
        weights_b = weights.astype(jnp.bfloat16)
        score_ref[...] = weights_b.astype(jnp.float32)
        own_mixed = jnp.dot(
            weights_b[:, cached_len:], fresh_v_ref[:, lanes], preferred_element_type=jnp.float32
        )
        for r in range(requests):
            here = slice(r * group_size, (r + 1) * group_size)
            mixed_ref[here, :] = jnp.dot(
                score_ref[here, :cached_len].astype(jnp.bfloat16),
                value_ref[r, :, lanes],
                preferred_element_type=jnp.float32,
            )
        mixed_ref[...] = (mixed_ref[...] + own_mixed) / totals
        for h in range(group_size):
            at = (j * group_size + h) * HEAD_SIZE
            out_ref[:, at : at + HEAD_SIZE] = mixed_ref[
                pl.ds(h, requests, stride=group_size), :
            ].astype(jnp.bfloat16)


def attend(heads, valid, routing_b, key_cache, value_cache, new_key, new_value, returned):
    requests, cached_len, _ = key_cache.shape
    cached_count, rows, _ = heads.shape
    features = cached_count * rows // requests * HEAD_SIZE
    return pl.pallas_call(
        functools.partial(attend_kernel, len(returned)),
        out_shape=jax.ShapeDtypeStruct((requests, features), jnp.bfloat16),
        in_specs=[VMEM] * (7 + len(returned)),
        out_specs=VMEM,
        scratch_shapes=[
            pltpu.VMEM((rows, HEAD_SIZE), jnp.float32),
            pltpu.VMEM((rows, cached_len + requests), jnp.float32),
            pltpu.VMEM((rows, HEAD_SIZE), jnp.float32),
        ],
        compiler_params=grant(20),
        name="attend",
    )(heads, valid, routing_b, key_cache, value_cache, new_key, new_value, *returned)


def after(arrays, *tokens):
    return lax.optimization_barrier((tuple(arrays), tokens))[0]


def shards(
    hidden,
    base_query,
    key_cache,
    value_cache,
    new_key,
    new_value,
    lengths,
    request_adapter,
    adapter_store_row,
    adapter_down,
    adapter_up,
):
    request_rows = hidden.shape[0]
    pool_count = lax.axis_size("pool")
    tp_count = lax.axis_size("tp")
    capacity = max(2, 2 * request_rows // pool_count)
    slot_total = pool_count * capacity
    owned_count, half_width, _ = adapter_down.shape
    cached_len = key_cache.shape[1]
    cached_count = key_cache.shape[2] // HEAD_SIZE
    per_group = max(1, ROWS // capacity)
    group_rows = per_group * capacity
    group_count = slot_total // group_rows
    splits = [(g * group_rows, group_rows) for g in range(group_count)]
    adapter_down = jnp.swapaxes(adapter_down, 1, 2)

    def travel(g, rows):
        parts = []
        for k in range(per_group):
            distance = g * per_group + k
            part = rows[k * capacity : (k + 1) * capacity] if per_group > 1 else rows
            if distance:
                part = lax.ppermute(part, "pool", [(i, i ^ distance) for i in range(pool_count)])
            parts.append(part)
        return parts[0] if per_group == 1 else jnp.concatenate(parts, axis=0)

    near = list(range(group_count // 2))
    far = list(range(group_count // 2, group_count))
    first, second = far[: len(far) // 2], far[len(far) // 2 :]
    *groups, routing_b = pack(
        hidden, request_adapter, adapter_store_row, pool_count, capacity, owned_count, half_width, splits
    )
    heads, valid = prepare(base_query, lengths, cached_len, cached_count)
    arrived = {g: travel(g, groups[g]) for g in first + near}
    late = after([groups[g] for g in second], arrived[near[1]])
    arrived |= {g: travel(g, rows) for g, rows in zip(second, late)}
    returned = {}
    for chosen in (first + near, second):
        served = serve([arrived[g] for g in chosen], adapter_down, adapter_up, tp_count)
        returned |= {g: travel(g, rows) for g, rows in zip(chosen, served)}
    return attend(
        heads,
        valid,
        routing_b,
        key_cache,
        value_cache,
        new_key,
        new_value,
        [returned[g] for g in range(group_count)],
    )


def solution(mesh):
    placed = (
        P(("rep", "pool"), None),
        P(("rep", "pool"), "tp"),
        P(("rep", "pool"), None, "tp"),
        P(("rep", "pool"), None, "tp"),
        P(("rep", "pool"), "tp"),
        P(("rep", "pool"), "tp"),
        P(("rep", "pool")),
        P(("rep", "pool")),
        P("rep"),
        P("pool", "tp", None),
        P("pool", None, "tp"),
    )
    return jax.shard_map(
        shards, mesh=mesh, in_specs=placed, out_specs=P(("rep", "pool"), "tp"), check_vma=False
    )
```

time: 94.7 us -> 77.5 us (0.82)
  the two profiles are of different devices: /device:TPU:0 before, /device:TPU:19 now
where the time goes in v1:
time: 77.5 us; the launch traced here: 76.7 us
  waiting for transfers between devices  33.8 us (44%)
  starting transfers between devices  22 us (28%)
  Pallas kernels  10.8 us (14%)
  local copies, waits for them, and re-layouts  9.98 us (13%)
    ppermute x14, waiting for transfers between devices, travel(): lax.ppermute(part, 'pool', [(i, i ^ distance) for i in range(pool_count)])  33.8 us
    ppermute x14, starting transfers between devices, travel(): lax.ppermute(part, 'pool', [(i, i ^ distance) for i in range(pool_count)])  18.5 us
    unnamed x26, local copies, waits for them, and re-layouts  9.98 us
    pallas_call x1, Pallas kernels, attend(): pl.pallas_call(functools.partial(attend_kernel, len(returned)), out_shape...  7.36 us
    ppermute x2, starting transfers between devices, serve(): lax.ppermute(mine, 'tp', [(i, tp_count - 1 - i) for i in range(tp_count)])  3.5 us
  transfers between devices with their start and end apart: 16, of which 8 were waited for; matrix products, arithmetic and copies ran while one was open for 0% of the time, Pallas kernels for 2%

profile of v1, /device:TPU:19, one launch (start us, length us, event | category | flops | bytes accessed | tf_op | source)
XLA Modules:
  0.0 76.7 jit_solution(3765946206808272285)
XLA Ops:
  0.0 0.0 copy-start
  0.0 0.0 copy-start.6
  0.0 1.4 %copy-done.6 = bf16[64,8192]{1,0:T(8,128)(2,1)S(1)} copy-done((bf16[64,8192]{1,0:T(8,128)(2,1)S(1)}, bf16[64,8192]{1,0:T(8,128)(2,1)}, u32[]{:S(2)}) %copy-start.6) | copy-done | bytes 1048600
  1.4 0.0 copy-start.10
  1.4 0.9 %copy-done.10 = s32[64]{0:T(128)S(1)} copy-done((s32[64]{0:T(128)S(1)}, s32[64]{0:T(128)}, u32[]{:S(2)}) %copy-start.10) | copy-done | bytes 280
  2.2 0.0 copy-start.11
  2.2 0.7 copy-done.11
  2.9 1.3 %pack.1 = (bf16[16,4224]{1,0:T(8,128)(2,1)S(1)}, bf16[16,4224]{1,0:T(8,128)(2,1)S(1)}, bf16[16,4224]{1,0:T(8,128)(2,1)S(1)}, bf16[16,4224]{1,0:T(8,128)(2,1)S(1)...) custom-call(s32[1,64]{1,0:T(1,128)S(1)} %bitcast.6, ...), custom_call_target="tpu_custom_call" | custom-call | tf_op jit(solution)/shard_map/pack/pallas_call | solution.py:98
  4.2 0.1 collective-permute-start
  4.3 3.2 %collective-permute-start.1 = (bf16[16,4224]{1,0:T(8,128)(2,1)S(1)}, bf16[16,4224]{1,0:T(8,128)(2,1)S(1)}, u32[]{:S(2)}, u32[]{:S(2)}) collective-permute-start(bf16[16,4224]{1,0:T(8,128)(2,1)S(1)} %get-tuple-element.30), channel_id=1, source_target_pairs={{0,10},{2,8},{4,14},{6,12},{8,2},{10,0},{12,6},{14,4},{1,11},{3,9}... | collective-permute-start | bytes 405512 | tf_op jit(solution)/shard_map/ppermute | solution.py:349
  7.6 0.2 collective-permute-start.2
  7.8 1.3 %collective-permute-start.3 = (bf16[16,4224]{1,0:T(8,128)(2,1)S(1)}, bf16[16,4224]{1,0:T(8,128)(2,1)S(1)}, u32[]{:S(2)}, u32[]{:S(2)}) collective-permute-start(bf16[16,4224]{1,0:T(8,128)(2,1)S(1)} %get-tuple-element.33), channel_id=1, source_target_pairs={{0,4},{2,6},{4,0},{6,2},{8,12},{10,14},{12,8},{14,10},{1,5},{3,7},... | collective-permute-start | bytes 405512 | tf_op jit(solution)/shard_map/ppermute | solution.py:349
  9.1 1.1 %collective-permute-start.4 = (bf16[16,4224]{1,0:T(8,128)(2,1)S(1)}, bf16[16,4224]{1,0:T(8,128)(2,1)S(1)}, u32[]{:S(2)}, u32[]{:S(2)}) collective-permute-start(bf16[16,4224]{1,0:T(8,128)(2,1)S(1)} %get-tuple-element.34), channel_id=1, source_target_pairs={{0,6},{2,4},{4,2},{6,0},{8,14},{10,12},{12,10},{14,8},{1,7},{3,5},... | collective-permute-start | bytes 405512 | tf_op jit(solution)/shard_map/ppermute | solution.py:349
  10.2 0.7 collective-permute-done.refs_0_
  10.9 4.4 %collective-permute-done.1.refs_1_ = bf16[16,4224]{1,0:T(8,128)(2,1)S(1)} collective-permute-done((bf16[16,4224]{1,0:T(8,128)(2,1)S(1)}, bf16[16,4224]{1,0:T(8,128)(2,1)S(1)}, u32[]{:S(2)}, u32[]{:S(2)}) %collective-permute-start.1) | collective-permute-done | bytes 135200 | tf_op jit(solution)/shard_map/ppermute | solution.py:349
  15.3 0.0 collective-permute-done.2.refs_3_
  15.3 0.0 collective-permute-done.3.refs_4_
  15.3 3.6 %collective-permute-done.4.refs_5_ = bf16[16,4224]{1,0:T(8,128)(2,1)S(1)} collective-permute-done((bf16[16,4224]{1,0:T(8,128)(2,1)S(1)}, bf16[16,4224]{1,0:T(8,128)(2,1)S(1)}, u32[]{:S(2)}, u32[]{:S(2)}) %collective-permute-start.4) | collective-permute-done | bytes 135200 | tf_op jit(solution)/shard_map/ppermute | solution.py:349
  18.9 0.0 copy-start.2
  18.9 1.2 %copy-done.2 = bf16[2,4096,64]{1,2,0:T(8,128)(2,1)S(1)} copy-done((bf16[2,4096,64]{1,2,0:T(8,128)(2,1)S(1)}, bf16[2,4096,64]{1,2,0:T(8,128)(2,1)}, u32[]{:S(2)}) %copy-start.2) | copy-done | bytes 1048600
  20.2 0.6 down.2.mine_ref
  20.7 2.6 %collective-permute-start.5 = (f32[96,64]{1,0:T(8,128)S(1)}, f32[96,64]{1,0:T(8,128)S(1)}, u32[]{:S(2)}, u32[]{:S(2)}) collective-permute-start(f32[96,64]{1,0:T(8,128)S(1)} %down.2.mine_ref), channel_id=1, source_target_pairs={{0,1},{1,0},{2,3},{3,2},{4,5},{5,4},{6,7},{7,6},{8,9},{9,8},{10,11... | collective-permute-start | bytes 73736 | tf_op jit(solution)/shard_map/ppermute | solution.py:190
  23.4 0.0 collective-permute-start.11
  23.4 2.4 %collective-permute-start.12 = (bf16[16,4224]{1,0:T(8,128)(2,1)S(1)}, bf16[16,4224]{1,0:T(8,128)(2,1)S(1)}, u32[]{:S(2)}, u32[]{:S(2)}) collective-permute-start(bf16[16,4224]{1,0:T(8,128)(2,1)S(1)} %get-tuple-element.44), channel_id=1, source_target_pairs={{0,14},{2,12},{4,10},{6,8},{8,6},{10,4},{12,2},{14,0},{1,15},{3,13... | collective-permute-start | bytes 405512 | tf_op jit(solution)/shard_map/ppermute | solution.py:349
  25.8 0.0 collective-permute-done.5.other_ref
  25.8 0.0 copy-start.4
  25.8 1.2 %copy-done.4 = bf16[2,64,4096]{2,1,0:T(8,128)(2,1)S(1)} copy-done((bf16[2,64,4096]{2,1,0:T(8,128)(2,1)S(1)}, bf16[2,64,4096]{2,1,0:T(8,128)(2,1)}, u32[]{:S(2)}) %copy-start.4) | copy-done | bytes 1048600
  27.0 0.0 copy-start.7
  27.0 0.0 copy-start.12
  27.0 0.0 copy-start.8
  27.0 0.0 copy-start.9
  27.0 0.5 up.2
  27.5 0.3 collective-permute-start.6
  27.8 4.9 %collective-permute-start.7 = (bf16[16,4096]{1,0:T(8,128)(2,1)S(1)}, bf16[16,4096]{1,0:T(8,128)(2,1)S(1)}, u32[]{:S(2)}, u32[]{:S(2)}) collective-permute-start(bf16[16,4096]{1,0:T(8,128)(2,1)S(1)} %get-tuple-element.37), channel_id=1, source_target_pairs={{0,4},{2,6},{4,0},{6,2},{8,12},{10,14},{12,8},{14,10},{1,5},{3,7},... | collective-permute-start | bytes 393224 | tf_op jit(solution)/shard_map/ppermute | solution.py:349
  32.8 0.0 collective-permute-done.11.refs_0_
  32.8 5.4 %collective-permute-done.12.refs_1_ = bf16[16,4224]{1,0:T(8,128)(2,1)S(1)} collective-permute-done((bf16[16,4224]{1,0:T(8,128)(2,1)S(1)}, bf16[16,4224]{1,0:T(8,128)(2,1)S(1)}, u32[]{:S(2)}, u32[]{:S(2)}) %collective-permute-start.12) | collective-permute-done | bytes 135200 | tf_op jit(solution)/shard_map/ppermute | solution.py:349
  38.2 1.2 %copy-done.3 = bf16[2,4096,64]{1,2,0:T(8,128)(2,1)S(1)} copy-done((bf16[2,4096,64]{1,2,0:T(8,128)(2,1)S(1)}, bf16[2,4096,64]{1,2,0:T(8,128)(2,1)}, u32[]{:S(2)}) %copy-start.3) | copy-done | bytes 1048600
  39.4 0.4 down.3.mine_ref
  39.8 0.9 %collective-permute-start.13 = (f32[32,64]{1,0:T(8,128)S(1)}, f32[32,64]{1,0:T(8,128)S(1)}, u32[]{:S(2)}, u32[]{:S(2)}) collective-permute-start(f32[32,64]{1,0:T(8,128)S(1)} %down.3.mine_ref), channel_id=1, source_target_pairs={{0,1},{1,0},{2,3},{3,2},{4,5},{5,4},{6,7},{7,6},{8,9},{9,8},{10,11... | collective-permute-start | bytes 24584 | tf_op jit(solution)/shard_map/ppermute | solution.py:190
  40.6 0.0 collective-permute-start.8
  40.7 1.1 %collective-permute-start.9 = (bf16[16,4096]{1,0:T(8,128)(2,1)S(1)}, bf16[16,4096]{1,0:T(8,128)(2,1)S(1)}, u32[]{:S(2)}, u32[]{:S(2)}) collective-permute-start(bf16[16,4096]{1,0:T(8,128)(2,1)S(1)} %get-tuple-element.39), channel_id=1, source_target_pairs={{0,8},{2,10},{4,12},{6,14},{8,0},{10,2},{12,4},{14,6},{1,9},{3,11}... | collective-permute-start | bytes 393224 | tf_op jit(solution)/shard_map/ppermute | solution.py:349
  41.8 0.0 collective-permute-done.13.other_ref
  41.8 1.2 %collective-permute-start.10 = (bf16[16,4096]{1,0:T(8,128)(2,1)S(1)}, bf16[16,4096]{1,0:T(8,128)(2,1)S(1)}, u32[]{:S(2)}, u32[]{:S(2)}) collective-permute-start(bf16[16,4096]{1,0:T(8,128)(2,1)S(1)} %get-tuple-element.40), channel_id=1, source_target_pairs={{0,10},{2,8},{4,14},{6,12},{8,2},{10,0},{12,6},{14,4},{1,11},{3,9}... | collective-permute-start | bytes 393224 | tf_op jit(solution)/shard_map/ppermute | solution.py:349
  43.0 0.0 copy-start.5
  43.0 1.2 %copy-done.5 = bf16[2,64,4096]{2,1,0:T(8,128)(2,1)S(1)} copy-done((bf16[2,64,4096]{2,1,0:T(8,128)(2,1)S(1)}, bf16[2,64,4096]{2,1,0:T(8,128)(2,1)}, u32[]{:S(2)}) %copy-start.5) | copy-done | bytes 1048600
  44.2 0.4 up.3
  44.6 0.0 collective-permute-done.6.refs_1_
  44.6 1.3 %collective-permute-start.14 = (bf16[16,4096]{1,0:T(8,128)(2,1)S(1)}, bf16[16,4096]{1,0:T(8,128)(2,1)S(1)}, u32[]{:S(2)}, u32[]{:S(2)}) collective-permute-start(bf16[16,4096]{1,0:T(8,128)(2,1)S(1)} %get-tuple-element.45), channel_id=1, source_target_pairs={{0,12},{2,14},{4,8},{6,10},{8,4},{10,6},{12,0},{14,2},{1,13},{3,15... | collective-permute-start | bytes 393224 | tf_op jit(solution)/shard_map/ppermute | solution.py:349
  45.9 0.0 collective-permute-done.7.refs_2_
  45.9 1.2 %collective-permute-start.15 = (bf16[16,4096]{1,0:T(8,128)(2,1)S(1)}, bf16[16,4096]{1,0:T(8,128)(2,1)S(1)}, u32[]{:S(2)}, u32[]{:S(2)}) collective-permute-start(bf16[16,4096]{1,0:T(8,128)(2,1)S(1)} %get-tuple-element.46), channel_id=1, source_target_pairs={{0,14},{2,12},{4,10},{6,8},{8,6},{10,4},{12,2},{14,0},{1,15},{3,13... | collective-permute-start | bytes 393224 | tf_op jit(solution)/shard_map/ppermute | solution.py:349
  47.1 0.0 copy-done.7
  47.1 0.0 copy-done.12
  47.1 0.3 prepare.1
  47.4 0.0 collective-permute-done.8.refs_3_
  47.4 0.8 %collective-permute-done.9.refs_4_ = bf16[16,4096]{1,0:T(8,128)(2,1)S(1)} collective-permute-done((bf16[16,4096]{1,0:T(8,128)(2,1)S(1)}, bf16[16,4096]{1,0:T(8,128)(2,1)S(1)}, u32[]{:S(2)}, u32[]{:S(2)}) %collective-permute-start.9) | collective-permute-done | bytes 131104 | tf_op jit(solution)/shard_map/ppermute | solution.py:349
  48.2 10.2 %collective-permute-done.10.refs_5_ = bf16[16,4096]{1,0:T(8,128)(2,1)S(1)} collective-permute-done((bf16[16,4096]{1,0:T(8,128)(2,1)S(1)}, bf16[16,4096]{1,0:T(8,128)(2,1)S(1)}, u32[]{:S(2)}, u32[]{:S(2)}) %collective-permute-start.10) | collective-permute-done | bytes 131104 | tf_op jit(solution)/shard_map/ppermute | solution.py:349
  58.4 5.0 %collective-permute-done.14.refs_6_ = bf16[16,4096]{1,0:T(8,128)(2,1)S(1)} collective-permute-done((bf16[16,4096]{1,0:T(8,128)(2,1)S(1)}, bf16[16,4096]{1,0:T(8,128)(2,1)S(1)}, u32[]{:S(2)}, u32[]{:S(2)}) %collective-permute-start.14) | collective-permute-done | bytes 131104 | tf_op jit(solution)/shard_map/ppermute | solution.py:349
  63.4 3.8 %collective-permute-done.15.refs_7_ = bf16[16,4096]{1,0:T(8,128)(2,1)S(1)} collective-permute-done((bf16[16,4096]{1,0:T(8,128)(2,1)S(1)}, bf16[16,4096]{1,0:T(8,128)(2,1)S(1)}, u32[]{:S(2)}, u32[]{:S(2)}) %collective-permute-start.15) | collective-permute-done | bytes 131104 | tf_op jit(solution)/shard_map/ppermute | solution.py:349
  67.1 0.0 copy-done
  67.1 0.0 copy-done.8
  67.1 0.0 copy-done.9
  67.1 0.0 copy-start.1
  67.1 2.2 %copy-done.1 = bf16[64,64,512]{2,1,0:T(8,128)(2,1)S(1)} copy-done((bf16[64,64,512]{2,1,0:T(8,128)(2,1)S(1)}, bf16[64,64,512]{2,1,0:T(8,128)(2,1)}, u32[]{:S(2)}) %copy-start.1) | copy-done | bytes 4194328
  69.3 7.4 %attend.1 = bf16[64,4096]{1,0:T(8,128)(2,1)} custom-call(f32[4,512,128]{2,1,0:T(8,128)S(1)} %get-tuple-element.26.heads_ref, f32[512,128]{1,0:T(8,128)S(1)} %get-tuple-element.27.valid_ref, bf16[64,128]{1,0:T(8,128)(2,1)S(1)} %get-tuple-element.28.routing_ref, bf16[64,64,512]{2,1,0:T(8,128)(2,1)S(1)} %copy-done, bf16[64,64,512]{2,1,0:T(8,128)(2,1)S(1)} %copy-done.1, ...), custom_call_target="tpu_custom_call" | custom-call | tf_op jit(solution)/shard_map/attend/pallas_call | solution.py:297
  (1 shorter events, 0.0 us)
Async XLA Ops:
  0.0 67.1 %copy-start = (bf16[64,64,512]{2,1,0:T(8,128)(2,1)S(1)}, bf16[64,64,512]{2,1,0:T(8,128)(2,1)}, u32[]{:S(2)}) copy-start(bf16[64,64,512]{2,1,0:T(8,128)(2,1)} %key_ref.1) | copy-start | bytes 12582916
  0.0 1.4 %copy-start.6 = (bf16[64,8192]{1,0:T(8,128)(2,1)S(1)}, bf16[64,8192]{1,0:T(8,128)(2,1)}, u32[]{:S(2)}) copy-start(bf16[64,8192]{1,0:T(8,128)(2,1)} %hidden_hbm.1) | copy-start | bytes 3145732
  1.4 0.9 %copy-start.10 = (s32[64]{0:T(128)S(1)}, s32[64]{0:T(128)}, u32[]{:S(2)}) copy-start(s32[64]{0:T(128)} %param.18) | copy-start | bytes 772
  2.2 0.7 copy-start.11
  4.2 6.7 %collective-permute-start = (bf16[16,4224]{1,0:T(8,128)(2,1)S(1)}, bf16[16,4224]{1,0:T(8,128)(2,1)S(1)}, u32[]{:S(2)}, u32[]{:S(2)}) collective-permute-start(bf16[16,4224]{1,0:T(8,128)(2,1)S(1)} %get-tuple-element.29), channel_id=1, source_target_pairs={{0,8},{2,10},{4,12},{6,14},{8,0},{10,2},{12,4},{14,6},{1,9},{3,11}... | collective-permute-start | bytes 405512 | tf_op jit(solution)/shard_map/ppermute | solution.py:349
  4.3 11.0 %collective-permute-start.1 = (bf16[16,4224]{1,0:T(8,128)(2,1)S(1)}, bf16[16,4224]{1,0:T(8,128)(2,1)S(1)}, u32[]{:S(2)}, u32[]{:S(2)}) collective-permute-start(bf16[16,4224]{1,0:T(8,128)(2,1)S(1)} %get-tuple-element.30), channel_id=1, source_target_pairs={{0,10},{2,8},{4,14},{6,12},{8,2},{10,0},{12,6},{14,4},{1,11},{3,9}... | collective-permute-start | bytes 405512 | tf_op jit(solution)/shard_map/ppermute | solution.py:349
  7.6 7.7 %collective-permute-start.2 = (bf16[16,4224]{1,0:T(8,128)(2,1)S(1)}, bf16[16,4224]{1,0:T(8,128)(2,1)S(1)}, u32[]{:S(2)}, u32[]{:S(2)}) collective-permute-start(bf16[16,4224]{1,0:T(8,128)(2,1)S(1)} %get-tuple-element.32), channel_id=1, source_target_pairs={{0,2},{2,0},{4,6},{6,4},{8,10},{10,8},{12,14},{14,12},{1,3},{3,1},... | collective-permute-start | bytes 405512 | tf_op jit(solution)/shard_map/ppermute | solution.py:349
  7.8 7.5 %collective-permute-start.3 = (bf16[16,4224]{1,0:T(8,128)(2,1)S(1)}, bf16[16,4224]{1,0:T(8,128)(2,1)S(1)}, u32[]{:S(2)}, u32[]{:S(2)}) collective-permute-start(bf16[16,4224]{1,0:T(8,128)(2,1)S(1)} %get-tuple-element.33), channel_id=1, source_target_pairs={{0,4},{2,6},{4,0},{6,2},{8,12},{10,14},{12,8},{14,10},{1,5},{3,7},... | collective-permute-start | bytes 405512 | tf_op jit(solution)/shard_map/ppermute | solution.py:349
  9.1 9.8 %collective-permute-start.4 = (bf16[16,4224]{1,0:T(8,128)(2,1)S(1)}, bf16[16,4224]{1,0:T(8,128)(2,1)S(1)}, u32[]{:S(2)}, u32[]{:S(2)}) collective-permute-start(bf16[16,4224]{1,0:T(8,128)(2,1)S(1)} %get-tuple-element.34), channel_id=1, source_target_pairs={{0,6},{2,4},{4,2},{6,0},{8,14},{10,12},{12,10},{14,8},{1,7},{3,5},... | collective-permute-start | bytes 405512 | tf_op jit(solution)/shard_map/ppermute | solution.py:349
  18.9 1.2 %copy-start.2 = (bf16[2,4096,64]{1,2,0:T(8,128)(2,1)S(1)}, bf16[2,4096,64]{1,2,0:T(8,128)(2,1)}, u32[]{:S(2)}) copy-start(bf16[2,4096,64]{1,2,0:T(8,128)(2,1)} %param.20) | copy-start | bytes 3145732
  20.7 5.1 %collective-permute-start.5 = (f32[96,64]{1,0:T(8,128)S(1)}, f32[96,64]{1,0:T(8,128)S(1)}, u32[]{:S(2)}, u32[]{:S(2)}) collective-permute-start(f32[96,64]{1,0:T(8,128)S(1)} %down.2.mine_ref), channel_id=1, source_target_pairs={{0,1},{1,0},{2,3},{3,2},{4,5},{5,4},{6,7},{7,6},{8,9},{9,8},{10,11... | collective-permute-start | bytes 73736 | tf_op jit(solution)/shard_map/ppermute | solution.py:190
  23.4 9.4 %collective-permute-start.11 = (bf16[16,4224]{1,0:T(8,128)(2,1)S(1)}, bf16[16,4224]{1,0:T(8,128)(2,1)S(1)}, u32[]{:S(2)}, u32[]{:S(2)}) collective-permute-start(bf16[16,4224]{1,0:T(8,128)(2,1)S(1)} %get-tuple-element.43), channel_id=1, source_target_pairs={{0,12},{2,14},{4,8},{6,10},{8,4},{10,6},{12,0},{14,2},{1,13},{3,15... | collective-permute-start | bytes 405512 | tf_op jit(solution)/shard_map/ppermute | solution.py:349
  23.4 14.8 %collective-permute-start.12 = (bf16[16,4224]{1,0:T(8,128)(2,1)S(1)}, bf16[16,4224]{1,0:T(8,128)(2,1)S(1)}, u32[]{:S(2)}, u32[]{:S(2)}) collective-permute-start(bf16[16,4224]{1,0:T(8,128)(2,1)S(1)} %get-tuple-element.44), channel_id=1, source_target_pairs={{0,14},{2,12},{4,10},{6,8},{8,6},{10,4},{12,2},{14,0},{1,15},{3,13... | collective-permute-start | bytes 405512 | tf_op jit(solution)/shard_map/ppermute | solution.py:349
  25.8 1.2 %copy-start.4 = (bf16[2,64,4096]{2,1,0:T(8,128)(2,1)S(1)}, bf16[2,64,4096]{2,1,0:T(8,128)(2,1)}, u32[]{:S(2)}) copy-start(bf16[2,64,4096]{2,1,0:T(8,128)(2,1)} %up_ref.3) | copy-start | bytes 3145732
  27.0 20.1 %copy-start.7 = (bf16[64,4096]{1,0:T(8,128)(2,1)S(1)}, bf16[64,4096]{1,0:T(8,128)(2,1)}, u32[]{:S(2)}) copy-start(bf16[64,4096]{1,0:T(8,128)(2,1)} %base_ref.1) | copy-start | bytes 1572868
  27.0 20.1 %copy-start.12 = (s32[64]{0:T(128)S(1)}, s32[64]{0:T(128)}, u32[]{:S(2)}) copy-start(s32[64]{0:T(128)} %param.17) | copy-start | bytes 772
  27.0 40.1 %copy-start.8 = (bf16[64,512]{1,0:T(8,128)(2,1)S(1)}, bf16[64,512]{1,0:T(8,128)(2,1)}, u32[]{:S(2)}) copy-start(bf16[64,512]{1,0:T(8,128)(2,1)} %fresh_k_ref.1) | copy-start | bytes 196612
  27.0 40.1 %copy-start.9 = (bf16[64,512]{1,0:T(8,128)(2,1)S(1)}, bf16[64,512]{1,0:T(8,128)(2,1)}, u32[]{:S(2)}) copy-start(bf16[64,512]{1,0:T(8,128)(2,1)} %fresh_v_ref.1) | copy-start | bytes 196612
  27.5 17.1 %collective-permute-start.6 = (bf16[16,4096]{1,0:T(8,128)(2,1)S(1)}, bf16[16,4096]{1,0:T(8,128)(2,1)S(1)}, u32[]{:S(2)}, u32[]{:S(2)}) collective-permute-start(bf16[16,4096]{1,0:T(8,128)(2,1)S(1)} %get-tuple-element.36), channel_id=1, source_target_pairs={{0,2},{2,0},{4,6},{6,4},{8,10},{10,8},{12,14},{14,12},{1,3},{3,1},... | collective-permute-start | bytes 393224 | tf_op jit(solution)/shard_map/ppermute | solution.py:349
  27.8 18.1 %collective-permute-start.7 = (bf16[16,4096]{1,0:T(8,128)(2,1)S(1)}, bf16[16,4096]{1,0:T(8,128)(2,1)S(1)}, u32[]{:S(2)}, u32[]{:S(2)}) collective-permute-start(bf16[16,4096]{1,0:T(8,128)(2,1)S(1)} %get-tuple-element.37), channel_id=1, source_target_pairs={{0,4},{2,6},{4,0},{6,2},{8,12},{10,14},{12,8},{14,10},{1,5},{3,7},... | collective-permute-start | bytes 393224 | tf_op jit(solution)/shard_map/ppermute | solution.py:349
  38.2 1.2 %copy-start.3 = (bf16[2,4096,64]{1,2,0:T(8,128)(2,1)S(1)}, bf16[2,4096,64]{1,2,0:T(8,128)(2,1)}, u32[]{:S(2)}) copy-start(bf16[2,4096,64]{1,2,0:T(8,128)(2,1)} %param.20) | copy-start | bytes 3145732
  39.8 2.0 %collective-permute-start.13 = (f32[32,64]{1,0:T(8,128)S(1)}, f32[32,64]{1,0:T(8,128)S(1)}, u32[]{:S(2)}, u32[]{:S(2)}) collective-permute-start(f32[32,64]{1,0:T(8,128)S(1)} %down.3.mine_ref), channel_id=1, source_target_pairs={{0,1},{1,0},{2,3},{3,2},{4,5},{5,4},{6,7},{7,6},{8,9},{9,8},{10,11... | collective-permute-start | bytes 24584 | tf_op jit(solution)/shard_map/ppermute | solution.py:190
  40.6 6.7 %collective-permute-start.8 = (bf16[16,4096]{1,0:T(8,128)(2,1)S(1)}, bf16[16,4096]{1,0:T(8,128)(2,1)S(1)}, u32[]{:S(2)}, u32[]{:S(2)}) collective-permute-start(bf16[16,4096]{1,0:T(8,128)(2,1)S(1)} %get-tuple-element.38), channel_id=1, source_target_pairs={{0,6},{2,4},{4,2},{6,0},{8,14},{10,12},{12,10},{14,8},{1,7},{3,5},... | collective-permute-start | bytes 393224 | tf_op jit(solution)/shard_map/ppermute | solution.py:349
  40.7 7.6 %collective-permute-start.9 = (bf16[16,4096]{1,0:T(8,128)(2,1)S(1)}, bf16[16,4096]{1,0:T(8,128)(2,1)S(1)}, u32[]{:S(2)}, u32[]{:S(2)}) collective-permute-start(bf16[16,4096]{1,0:T(8,128)(2,1)S(1)} %get-tuple-element.39), channel_id=1, source_target_pairs={{0,8},{2,10},{4,12},{6,14},{8,0},{10,2},{12,4},{14,6},{1,9},{3,11}... | collective-permute-start | bytes 393224 | tf_op jit(solution)/shard_map/ppermute | solution.py:349
  41.8 16.6 %collective-permute-start.10 = (bf16[16,4096]{1,0:T(8,128)(2,1)S(1)}, bf16[16,4096]{1,0:T(8,128)(2,1)S(1)}, u32[]{:S(2)}, u32[]{:S(2)}) collective-permute-start(bf16[16,4096]{1,0:T(8,128)(2,1)S(1)} %get-tuple-element.40), channel_id=1, source_target_pairs={{0,10},{2,8},{4,14},{6,12},{8,2},{10,0},{12,6},{14,4},{1,11},{3,9}... | collective-permute-start | bytes 393224 | tf_op jit(solution)/shard_map/ppermute | solution.py:349
  43.0 1.2 %copy-start.5 = (bf16[2,64,4096]{2,1,0:T(8,128)(2,1)S(1)}, bf16[2,64,4096]{2,1,0:T(8,128)(2,1)}, u32[]{:S(2)}) copy-start(bf16[2,64,4096]{2,1,0:T(8,128)(2,1)} %up_ref.3) | copy-start | bytes 3145732
  44.6 18.8 %collective-permute-start.14 = (bf16[16,4096]{1,0:T(8,128)(2,1)S(1)}, bf16[16,4096]{1,0:T(8,128)(2,1)S(1)}, u32[]{:S(2)}, u32[]{:S(2)}) collective-permute-start(bf16[16,4096]{1,0:T(8,128)(2,1)S(1)} %get-tuple-element.45), channel_id=1, source_target_pairs={{0,12},{2,14},{4,8},{6,10},{8,4},{10,6},{12,0},{14,2},{1,13},{3,15... | collective-permute-start | bytes 393224 | tf_op jit(solution)/shard_map/ppermute | solution.py:349
  45.9 21.2 %collective-permute-start.15 = (bf16[16,4096]{1,0:T(8,128)(2,1)S(1)}, bf16[16,4096]{1,0:T(8,128)(2,1)S(1)}, u32[]{:S(2)}, u32[]{:S(2)}) collective-permute-start(bf16[16,4096]{1,0:T(8,128)(2,1)S(1)} %get-tuple-element.46), channel_id=1, source_target_pairs={{0,14},{2,12},{4,10},{6,8},{8,6},{10,4},{12,2},{14,0},{1,15},{3,13... | collective-permute-start | bytes 393224 | tf_op jit(solution)/shard_map/ppermute | solution.py:349
  67.1 2.2 %copy-start.1 = (bf16[64,64,512]{2,1,0:T(8,128)(2,1)S(1)}, bf16[64,64,512]{2,1,0:T(8,128)(2,1)}, u32[]{:S(2)}) copy-start(bf16[64,64,512]{2,1,0:T(8,128)(2,1)} %value_ref.1) | copy-start | bytes 12582916

commit v2 on v1

v2 whole, which is shorter than its diff:
```python
import functools
import math

import jax
import jax.numpy as jnp
from jax import lax
from jax.experimental import pallas as pl
from jax.experimental.pallas import tpu as pltpu
from jax.sharding import PartitionSpec as P

HEAD_SIZE = 128
ADAPTER_SCALE = 2.0
MASKED = -1e30
LANES = 128
ROWS = 16
MIB = 1024 * 1024

VMEM = pl.BlockSpec(memory_space=pltpu.VMEM)
ANYWHERE = pl.BlockSpec(memory_space=pl.ANY)


def grant(mib):
    return pltpu.CompilerParams(vmem_limit_bytes=mib * MIB)


def column_of(row):
    count = row.shape[1]
    here = lax.broadcasted_iota(jnp.int32, (count, count), 0)
    there = lax.broadcasted_iota(jnp.int32, (count, count), 1)
    spread = jnp.broadcast_to(row, (count, count))
    return jnp.sum(jnp.where(here == there, spread, 0), axis=1, keepdims=True)


def in_hbm(array):
    return pltpu.with_memory_space_constraint(array, pltpu.HBM)


def as_bf16(mask):
    return mask.astype(jnp.float32).astype(jnp.bfloat16)


def pack_kernel(pool_count, tp_count, capacity, owned_count, adapter_hbm, store_hbm, hidden_hbm, *refs):
    *outs, routing_ref, adapter_ref, store_ref, held_ref, sems, index_sems = refs
    width = held_ref.shape[1]
    chunks = sems.shape[0]
    step = width // chunks
    small = [
        pltpu.make_async_copy(adapter_hbm, adapter_ref, index_sems.at[0]),
        pltpu.make_async_copy(store_hbm, store_ref, index_sems.at[1]),
    ]
    copies = [
        pltpu.make_async_copy(
            hidden_hbm.at[:, pl.ds(c * step, step)], held_ref.at[:, pl.ds(c * step, step)], sems.at[c]
        )
        for c in range(chunks)
    ]
    for copy in small + copies:
        copy.start()
    for copy in small:
        copy.wait()
    adapters = store_ref.shape[1]
    requests = adapter_ref.shape[1]
    slot_total = pool_count // tp_count * capacity
    matches = lax.broadcasted_iota(jnp.int32, (adapters, requests), 0) == adapter_ref[...]
    position = jnp.sum(jnp.where(matches, column_of(store_ref[...]), 0), axis=0, keepdims=True)
    owner = lax.div(position, jnp.int32(owned_count))
    held = position - owner * owned_count
    distance = lax.bitwise_xor(owner, jnp.broadcast_to(lax.axis_index("pool"), owner.shape))
    step_of = lax.div(distance, jnp.int32(tp_count))
    mine = distance - step_of * tp_count == lax.axis_index("tp")
    earlier = lax.broadcasted_iota(jnp.int32, (requests, requests), 0) < lax.broadcasted_iota(
        jnp.int32, (requests, requests), 1
    )
    same = column_of(owner) == owner
    rank = jnp.sum(jnp.where(same & earlier, 1, 0), axis=0, keepdims=True)
    target = step_of * capacity + rank + jnp.where(mine, 0, slot_total)
    routing = lax.broadcasted_iota(jnp.int32, (slot_total, requests), 0) == target
    held_slot = jnp.sum(jnp.where(routing, held, 0), axis=1, keepdims=True)
    tags = jnp.broadcast_to(held_slot, (slot_total, LANES)).astype(jnp.float32).astype(jnp.bfloat16)
    routing_b = as_bf16(routing)
    back = lax.broadcasted_iota(jnp.int32, (requests, tp_count * slot_total), 1) == column_of(target)
    routing_ref[...] = as_bf16(back)
    for g, out in enumerate(outs):
        out[:, width:] = tags[g * out.shape[0] : (g + 1) * out.shape[0]]
    for c, copy in enumerate(copies):
        copy.wait()
        columns = slice(c * step, (c + 1) * step)
        packed = jnp.dot(
            routing_b, held_ref[:, columns], preferred_element_type=jnp.float32
        ).astype(jnp.bfloat16)
        for g, out in enumerate(outs):
            out[:, columns] = packed[g * out.shape[0] : (g + 1) * out.shape[0]]


def pack(hidden, request_adapter, adapter_store_row, pool_count, tp_count, capacity, owned_count, group_rows):
    requests, width = hidden.shape
    adapters = adapter_store_row.shape[0]
    slot_total = pool_count // tp_count * capacity
    group_count = slot_total // group_rows
    chunks = 4
    return pl.pallas_call(
        functools.partial(pack_kernel, pool_count, tp_count, capacity, owned_count),
        out_shape=[pltpu.VMEM((group_rows, width + LANES), jnp.bfloat16)] * group_count
        + [pltpu.VMEM((requests, tp_count * slot_total), jnp.bfloat16)],
        in_specs=[ANYWHERE] * 3,
        out_specs=[VMEM] * (group_count + 1),
        scratch_shapes=[
            pltpu.VMEM((1, requests), jnp.int32),
            pltpu.VMEM((1, adapters), jnp.int32),
            pltpu.VMEM((requests, width), jnp.bfloat16),
            pltpu.SemaphoreType.DMA((chunks,)),
            pltpu.SemaphoreType.DMA((2,)),
        ],
        compiler_params=grant(8),
        name="pack",
    )(
        in_hbm(request_adapter.reshape(1, requests)),
        in_hbm(adapter_store_row.reshape(1, adapters)),
        in_hbm(hidden),
    )


def serve_kernel(count, *refs):
    rows, (down_ref, down_far_ref, up_ref, up_far_ref), outs = (
        refs[:count],
        refs[count : count + 4],
        refs[count + 4 :],
    )
    owned_count, rank, width = down_ref.shape
    here = lax.axis_index("tp")
    there = 1 - here
    tags = jnp.concatenate([row[:, 2 * width : 2 * width + 1] for row in rows], axis=0)
    tags = tags.astype(jnp.float32)
    middle = jnp.zeros((tags.shape[0], rank), jnp.float32)
    for half, factors in ((here, down_ref), (there, down_far_ref)):
        columns = pl.ds(pl.multiple_of(half * width, LANES), width)
        features = jnp.concatenate([row[:, columns] for row in rows], axis=0)
        for slot in range(owned_count):
            partial = lax.dot_general(
                features,
                factors[slot],
                (((1,), (1,)), ((), ())),
                preferred_element_type=jnp.float32,
            )
            middle = middle + jnp.where(tags == float(slot), partial, 0.0)
    middle = middle.astype(jnp.bfloat16).astype(jnp.float32)
    chosen = jnp.concatenate(
        [jnp.where(tags == float(slot), middle, 0.0) for slot in range(owned_count)], axis=1
    ).astype(jnp.bfloat16)
    step = min(width, 1024)
    for half, factors in ((here, up_ref), (there, up_far_ref)):
        for c in range(width // step):
            columns = slice(c * step, (c + 1) * step)
            stacked = jnp.concatenate([factors[slot, :, columns] for slot in range(owned_count)], axis=0)
            total = jnp.dot(chosen, stacked, preferred_element_type=jnp.float32)
            total = (ADAPTER_SCALE * total).astype(jnp.bfloat16)
            at = 0
            for out in outs:
                out[half, :, columns] = total[at : at + out.shape[1]]
                at += out.shape[1]


def serve(rows, factors):
    width = factors[0].shape[2]
    return pl.pallas_call(
        functools.partial(serve_kernel, len(rows)),
        out_shape=[pltpu.VMEM((2, row.shape[0], width), jnp.bfloat16) for row in rows],
        in_specs=[VMEM] * (len(rows) + 4),
        out_specs=[VMEM] * len(rows),
        compiler_params=grant(8),
        name="serve",
    )(*rows, *factors)


def prepare_kernel(
    base_hbm,
    lengths_hbm,
    down_hbm,
    up_hbm,
    key_hbm,
    value_hbm,
    heads_ref,
    valid_ref,
    down_ref,
    up_ref,
    key_ref,
    value_ref,
    base_ref,
    lengths_ref,
    sems,
):
    pairs = [
        (lengths_hbm, lengths_ref),
        (base_hbm, base_ref),
        (down_hbm, down_ref),
        (up_hbm, up_ref),
        (key_hbm, key_ref),
        (value_hbm, value_ref),
    ]
    copies = [pltpu.make_async_copy(*pair, sems.at[i]) for i, pair in enumerate(pairs)]
    for copy in copies:
        copy.start()
    copies[0].wait()
    copies[1].wait()
    requests = base_ref.shape[0]
    cached_count, rows, _ = heads_ref.shape
    group_size = rows // requests
    for j in range(cached_count):
        for h in range(group_size):
            at = (j * group_size + h) * HEAD_SIZE
            heads_ref[j, pl.ds(h, requests, stride=group_size), :] = base_ref[
                :, at : at + HEAD_SIZE
            ].astype(jnp.float32)
    cached_len = valid_ref.shape[1] - requests
    place = lax.broadcasted_iota(jnp.int32, (requests, cached_len + requests), 1)
    own = place - cached_len == lax.broadcasted_iota(jnp.int32, place.shape, 0)
    inside = (place < column_of(lengths_ref[...])) & (place < cached_len)
    allowed = (inside | own).astype(jnp.float32)
    for h in range(group_size):
        valid_ref[pl.ds(h, requests, stride=group_size), :] = allowed
    for copy in copies[2:]:
        copy.wait()


def prepare(base_query, lengths, adapter_down, adapter_up, key_cache, value_cache):
    requests, features = base_query.shape
    cached_len = key_cache.shape[1]
    cached_count = key_cache.shape[2] // HEAD_SIZE
    rows = requests * features // (HEAD_SIZE * cached_count)
    held = [adapter_down, adapter_up, key_cache, value_cache]
    return pl.pallas_call(
        prepare_kernel,
        out_shape=[
            pltpu.VMEM((cached_count, rows, HEAD_SIZE), jnp.float32),
            pltpu.VMEM((rows, cached_len + requests), jnp.float32),
        ]
        + [pltpu.VMEM(array.shape, array.dtype) for array in held],
        in_specs=[ANYWHERE] * 6,
        out_specs=[VMEM] * 6,
        scratch_shapes=[
            pltpu.VMEM((requests, features), base_query.dtype),
            pltpu.VMEM((1, requests), jnp.int32),
            pltpu.SemaphoreType.DMA((6,)),
        ],
        compiler_params=grant(8),
        cost_estimate=pl.CostEstimate(
            flops=0, bytes_accessed=4 * key_cache.size + 4 * adapter_up.size, transcendentals=0
        ),
        name="prepare",
    )(*[in_hbm(array) for array in [base_query, lengths.reshape(1, requests)] + held])


def attend_kernel(
    count, heads_ref, valid_ref, routing_ref, key_ref, value_ref, fresh_k_ref, fresh_v_ref, *refs
):
    returned, out_ref, delta_ref, score_ref, mixed_ref = refs[:count], *refs[count:]
    requests, cached_len, _ = key_ref.shape
    cached_count, rows, _ = heads_ref.shape
    group_size = rows // requests
    factor = 1.0 / math.sqrt(HEAD_SIZE)
    across = (((1,), (1,)), ((), ()))
    half = lax.axis_index("tp")
    for j in range(cached_count):
        lanes = slice(j * HEAD_SIZE, (j + 1) * HEAD_SIZE)
        wide = slice(j * group_size * HEAD_SIZE, (j + 1) * group_size * HEAD_SIZE)
        arrived = jnp.concatenate([piece[half, :, wide] for piece in returned], axis=0)
        delta = jnp.dot(routing_ref[...], arrived, preferred_element_type=jnp.float32)
        for h in range(group_size):
            delta_ref[pl.ds(h, requests, stride=group_size), :] = delta[
                :, h * HEAD_SIZE : (h + 1) * HEAD_SIZE
            ]
        for r in range(requests):
            here = slice(r * group_size, (r + 1) * group_size)
            pair = jnp.concatenate([heads_ref[j, here, :], delta_ref[here, :]], axis=0)
            both = lax.dot_general(
                pair.astype(jnp.bfloat16),
                key_ref[r, :, lanes],
                across,
                preferred_element_type=jnp.float32,
            )
            score_ref[here, :cached_len] = both[:group_size] + both[group_size:]
        own = lax.dot_general(
            heads_ref[j].astype(jnp.bfloat16),
            fresh_k_ref[:, lanes],
            across,
            preferred_element_type=jnp.float32,
        ) + lax.dot_general(
            delta_ref[...].astype(jnp.bfloat16),
            fresh_k_ref[:, lanes],
            across,
            preferred_element_type=jnp.float32,
        )
        score_ref[:, cached_len:] = own
        scores = jnp.where(valid_ref[...] > 0.0, score_ref[...] * factor, MASKED)
        highest = jnp.max(scores, axis=1, keepdims=True)
        weights = jnp.exp(scores - highest)
        totals = jnp.sum(weights, axis=1, keepdims=True)
        weights_b = weights.astype(jnp.bfloat16)
        score_ref[...] = weights_b.astype(jnp.float32)
        own_mixed = jnp.dot(
            weights_b[:, cached_len:], fresh_v_ref[:, lanes], preferred_element_type=jnp.float32
        )
        for r in range(requests):
            here = slice(r * group_size, (r + 1) * group_size)
            mixed_ref[here, :] = jnp.dot(
                score_ref[here, :cached_len].astype(jnp.bfloat16),
                value_ref[r, :, lanes],
                preferred_element_type=jnp.float32,
            )
        mixed_ref[...] = (mixed_ref[...] + own_mixed) / totals
        for h in range(group_size):
            at = (j * group_size + h) * HEAD_SIZE
            out_ref[:, at : at + HEAD_SIZE] = mixed_ref[
                pl.ds(h, requests, stride=group_size), :
            ].astype(jnp.bfloat16)


def attend(heads, valid, routing_b, key_cache, value_cache, new_key, new_value, returned):
    requests, cached_len, _ = key_cache.shape
    cached_count, rows, _ = heads.shape
    features = cached_count * rows // requests * HEAD_SIZE
    return pl.pallas_call(
        functools.partial(attend_kernel, len(returned)),
        out_shape=jax.ShapeDtypeStruct((requests, features), jnp.bfloat16),
        in_specs=[VMEM] * (7 + len(returned)),
        out_specs=VMEM,
        scratch_shapes=[
            pltpu.VMEM((rows, HEAD_SIZE), jnp.float32),
            pltpu.VMEM((rows, cached_len + requests), jnp.float32),
            pltpu.VMEM((rows, HEAD_SIZE), jnp.float32),
        ],
        compiler_params=grant(20),
        name="attend",
    )(heads, valid, routing_b, key_cache, value_cache, new_key, new_value, *returned)


def after(arrays, *tokens):
    return lax.optimization_barrier((tuple(arrays), tokens))[0]


def shards(
    hidden,
    base_query,
    key_cache,
    value_cache,
    new_key,
    new_value,
    lengths,
    request_adapter,
    adapter_store_row,
    adapter_down,
    adapter_up,
):
    request_rows = hidden.shape[0]
    pool_count = lax.axis_size("pool")
    tp_count = lax.axis_size("tp")
    capacity = max(2, 2 * request_rows // pool_count)
    owned_count = adapter_down.shape[0]
    step_count = pool_count // tp_count
    per_group = max(1, ROWS // capacity)
    group_count = step_count // per_group
    adapter_down = jnp.swapaxes(adapter_down, 1, 2)

    def move(g, rows):
        parts = []
        for k in range(per_group):
            step = g * per_group + k
            part = rows
            if per_group > 1:
                part = lax.slice_in_dim(rows, k * capacity, (k + 1) * capacity, axis=rows.ndim - 2)
            pairs = [
                (i * tp_count + c, (i ^ (tp_count * step + c)) * tp_count + c)
                for i in range(pool_count)
                for c in range(tp_count)
            ]
            parts.append(lax.ppermute(part, ("pool", "tp"), pairs))
        return parts[0] if per_group == 1 else jnp.concatenate(parts, axis=rows.ndim - 2)

    def swap(array):
        return lax.ppermute(array, "tp", [(0, 1), (1, 0)])

    *groups, routing_b = pack(
        hidden, request_adapter, adapter_store_row, pool_count, tp_count, capacity, owned_count, per_group * capacity
    )
    factors = [adapter_down, swap(adapter_down), adapter_up, swap(adapter_up)]
    heads, valid, factors[0], factors[2], key_cache, value_cache = prepare(
        *after([base_query, lengths, adapter_down, adapter_up, key_cache, value_cache], routing_b)
    )
    near = list(range(group_count // 2))
    far = list(range(group_count // 2, group_count))
    arrived = {g: move(g, groups[g]) for g in far + near}
    returned = {}
    for chosen in (near, *[[g] for g in far]):
        served = serve([arrived[g] for g in chosen], factors)
        returned |= {g: move(g, rows) for g, rows in zip(chosen, served)}
    returned = [returned[g] for g in range(group_count)]
    others = [swap(rows) for rows in returned]
    return attend(
        heads, valid, routing_b, key_cache, value_cache, new_key, new_value, returned + others
    )


def solution(mesh):
    placed = (
        P(("rep", "pool"), None),
        P(("rep", "pool"), "tp"),
        P(("rep", "pool"), None, "tp"),
        P(("rep", "pool"), None, "tp"),
        P(("rep", "pool"), "tp"),
        P(("rep", "pool"), "tp"),
        P(("rep", "pool")),
        P(("rep", "pool")),
        P("rep"),
        P("pool", "tp", None),
        P("pool", None, "tp"),
    )
    return jax.shard_map(
        shards, mesh=mesh, in_specs=placed, out_specs=P(("rep", "pool"), "tp"), check_vma=False
    )
```

time: 77.5 us -> 63.8 us (0.82)
  local copies, waits for them, and re-layouts: 9.98 us -> 0.01 us
  waiting for transfers between devices: 33.8 us -> 27.3 us
  Pallas kernels: 10.8 us -> 17.1 us
  starting transfers between devices: 22 us -> 19.2 us
    unnamed x26 -> x4, local copies, waits for them, and re-layouts: 9.98 us -> 0.01 us
    ppermute x16 -> x14, waiting for transfers between devices: 33.8 us -> 27.3 us  [the longest x8 25.7 us: move(): parts.append(lax.ppermute(part, ('pool', 'tp'), pairs))]
    pallas_call x6 -> x5, Pallas kernels: 3.43 us -> 9.71 us  [the longest x1 4.26 us: prepare(): pl.pallas_call(prepare_kernel, out_shape=[pltpu.VMEM((cached_count, rows,...]
    ppermute x16 -> x14, starting transfers between devices: 22 us -> 19.2 us  [the longest x8 18 us: move(): parts.append(lax.ppermute(part, ('pool', 'tp'), pairs))]
  transfers between devices with their start and end apart: 16 -> 14, of which waited for: 8 -> 6; matrix products, arithmetic and copies ran while one was open for 0% -> 0% of each run, Pallas kernels for 2% -> 15%
where the time goes in v2:
time: 63.8 us; the launch traced here: 63.6 us
  waiting for transfers between devices  27.3 us (43%)
  starting transfers between devices  19.2 us (30%)
  Pallas kernels  17.1 us (27%)
    ppermute x8, waiting for transfers between devices, move(): parts.append(lax.ppermute(part, ('pool', 'tp'), pairs))  25.7 us
    ppermute x8, starting transfers between devices, move(): parts.append(lax.ppermute(part, ('pool', 'tp'), pairs))  18 us
    pallas_call x1, Pallas kernels, attend(): pl.pallas_call(functools.partial(attend_kernel, len(returned)), out_shape...  7.36 us
    pallas_call x1, Pallas kernels, prepare(): pl.pallas_call(prepare_kernel, out_shape=[pltpu.VMEM((cached_count, rows,...  4.26 us
    pallas_call x3, Pallas kernels, serve(): pl.pallas_call(functools.partial(serve_kernel, len(rows)), out_shape=[plt...  3.33 us
    pallas_call x1, Pallas kernels, pack(): pl.pallas_call(functools.partial(pack_kernel, pool_count, tp_count, capac...  2.11 us
    ppermute x6, waiting for transfers between devices, swap(): return lax.ppermute(array, 'tp', [(0, 1), (1, 0)])  1.53 us
  transfers between devices with their start and end apart: 14, of which 6 were waited for; matrix products, arithmetic and copies ran while one was open for 0% of the time, Pallas kernels for 15%

profile of v2, /device:TPU:19, one launch (start us, length us, event | category | flops | bytes accessed | tf_op | source)
XLA Modules:
  0.0 63.6 jit_solution(1209343859784079777)
XLA Ops:
  0.0 0.7 %collective-permute-start.2 = (bf16[2,64,4096]{2,1,0:T(8,128)(2,1)}, bf16[2,64,4096]{2,1,0:T(8,128)(2,1)S(1)}, u32[]{:S(2)}, u32[]{:S(2)}) collective-permute-start(bf16[2,64,4096]{2,1,0:T(8,128)(2,1)} %bitcast.4), channel_id=1, source_target_pairs={{0,1},{1,0},{2,3},{3,2},{4,5},{5,4},{6,7},{7,6},{8,9},{9,8},{10,11... | collective-permute-start | bytes 3145736 | tf_op jit(solution)/shard_map/ppermute | solution.py:380
  0.7 0.0 collective-permute-start.3
  0.7 2.1 %pack.1 = (bf16[16,8320]{1,0:T(8,128)(2,1)S(1)}, bf16[16,8320]{1,0:T(8,128)(2,1)S(1)}, bf16[16,8320]{1,0:T(8,128)(2,1)S(1)}, bf16[16,8320]{1,0:T(8,128)(2,1)S(1)}, bf16[64,128]{1,0:T(8,128)(2,1)S(1)}) custom-call(s32[1,64]{1,0:T(1,128)} %bitcast.6, s32[1,16]{1,0:T(1,128)} %bitcast.7, bf16[64,8192]{1,0:T(8,128)(2,1)} %hidden_hbm.1), custom_call_target="tpu_custom_call" | custom-call | tf_op jit(solution)/shard_map/pack/pallas_call | solution.py:101
  2.8 3.1 %collective-permute-start = (bf16[16,8320]{1,0:T(8,128)(2,1)S(1)}, bf16[16,8320]{1,0:T(8,128)(2,1)S(1)}, u32[]{:S(2)}, u32[]{:S(2)}) collective-permute-start(bf16[16,8320]{1,0:T(8,128)(2,1)S(1)} %get-tuple-element.35), channel_id=1, source_target_pairs={{0,0},{1,3},{2,2},{3,1},{4,4},{5,7},{6,6},{7,5},{8,8},{9,11},{10,1... | collective-permute-start | bytes 798728 | tf_op jit(solution)/shard_map/ppermute | solution.py:376
  6.0 1.3 %collective-permute-start.1 = (bf16[16,8320]{1,0:T(8,128)(2,1)S(1)}, bf16[16,8320]{1,0:T(8,128)(2,1)S(1)}, u32[]{:S(2)}, u32[]{:S(2)}) collective-permute-start(bf16[16,8320]{1,0:T(8,128)(2,1)S(1)} %get-tuple-element.36), channel_id=1, source_target_pairs={{0,4},{1,7},{2,6},{3,5},{4,0},{5,3},{6,2},{7,1},{8,12},{9,15},{10,... | collective-permute-start | bytes 798728 | tf_op jit(solution)/shard_map/ppermute | solution.py:376
  7.3 1.0 %collective-permute-start.6 = (bf16[16,8320]{1,0:T(8,128)(2,1)S(1)}, bf16[16,8320]{1,0:T(8,128)(2,1)S(1)}, u32[]{:S(2)}, u32[]{:S(2)}) collective-permute-start(bf16[16,8320]{1,0:T(8,128)(2,1)S(1)} %get-tuple-element.41), channel_id=1, source_target_pairs={{0,8},{1,11},{2,10},{3,9},{4,12},{5,15},{6,14},{7,13},{8,0},{9,3},... | collective-permute-start | bytes 798728 | tf_op jit(solution)/shard_map/ppermute | solution.py:376
  8.3 2.5 %collective-permute-done.refs_0_ = bf16[16,8320]{1,0:T(8,128)(2,1)S(1)} collective-permute-done((bf16[16,8320]{1,0:T(8,128)(2,1)S(1)}, bf16[16,8320]{1,0:T(8,128)(2,1)S(1)}, u32[]{:S(2)}, u32[]{:S(2)}) %collective-permute-start) | collective-permute-done | bytes 266272 | tf_op jit(solution)/shard_map/ppermute | solution.py:376
  10.8 1.8 %collective-permute-start.8 = (bf16[16,8320]{1,0:T(8,128)(2,1)S(1)}, bf16[16,8320]{1,0:T(8,128)(2,1)S(1)}, u32[]{:S(2)}, u32[]{:S(2)}) collective-permute-start(bf16[16,8320]{1,0:T(8,128)(2,1)S(1)} %get-tuple-element.42), channel_id=1, source_target_pairs={{0,12},{1,15},{2,14},{3,13},{4,8},{5,11},{6,10},{7,9},{8,4},{9,7},... | collective-permute-start | bytes 798728 | tf_op jit(solution)/shard_map/ppermute | solution.py:376
  12.7 4.3 %prepare.1 = (f32[4,512,128]{2,1,0:T(8,128)S(1)}, f32[512,128]{1,0:T(8,128)S(1)}, bf16[2,64,4096]{2,1,0:T(8,128)(2,1)S(1)}, bf16[2,64,4096]{2,1,0:T(8,128)(2,1)S...) custom-call(bf16[64,4096]{1,0:T(8,128)(2,1)} %base_hbm, s32[1,64]{1,0:T(1,128)} %bitcast.8, ...), custom_call_target="tpu_custom_call" | custom-call | bytes 10485760 | tf_op jit(solution)/shard_map/prepare/pallas_call | solution.py:231
  16.9 0.0 collective-permute-done.1.refs_1_
  16.9 0.0 collective-permute-done.2.refs_3_.refs_2_
  17.0 0.0 collective-permute-done.3.refs_5_.refs_4_
  17.0 1.1 %serve.3 = (bf16[2,16,4096]{2,1,0:T(8,128)(2,1)S(1)}, bf16[2,16,4096]{2,1,0:T(8,128)(2,1)S(1)}) custom-call(bf16[16,8320]{1,0:T(8,128)(2,1)S(1)} %collective-permute-done.refs_0_, bf16[16,8320]{1,0:T(8,128)(2,1)S(1)} %collective-permute-done.1.refs_1_, bf16[2,64,4096]{2,1,0:T(8,128)(2,1)S(1)} %get-tuple-element.37.refs_2_.refs_1_, ...), custom_call_target="tpu_custom_call" | custom-call | tf_op jit(solution)/shard_map/serve/pallas_call | solution.py:165
  18.1 2.4 %collective-permute-start.4 = (bf16[2,16,4096]{2,1,0:T(8,128)(2,1)S(1)}, bf16[2,16,4096]{2,1,0:T(8,128)(2,1)S(1)}, u32[]{:S(2)}, u32[]{:S(2)}) collective-permute-start(bf16[2,16,4096]{2,1,0:T(8,128)(2,1)S(1)} %get-tuple-element.39), channel_id=1, source_target_pairs={{0,0},{1,3},{2,2},{3,1},{4,4},{5,7},{6,6},{7,5},{8,8},{9,11},{10,1... | collective-permute-start | bytes 786440 | tf_op jit(solution)/shard_map/ppermute | solution.py:376
  20.5 0.0 copy-start
  20.5 0.0 copy-start.1
  20.5 3.3 %collective-permute-start.5 = (bf16[2,16,4096]{2,1,0:T(8,128)(2,1)S(1)}, bf16[2,16,4096]{2,1,0:T(8,128)(2,1)S(1)}, u32[]{:S(2)}, u32[]{:S(2)}) collective-permute-start(bf16[2,16,4096]{2,1,0:T(8,128)(2,1)S(1)} %get-tuple-element.40), channel_id=1, source_target_pairs={{0,4},{1,7},{2,6},{3,5},{4,0},{5,3},{6,2},{7,1},{8,12},{9,15},{10,... | collective-permute-start | bytes 786440 | tf_op jit(solution)/shard_map/ppermute | solution.py:376
  23.8 2.2 %collective-permute-done.6.refs_0_ = bf16[16,8320]{1,0:T(8,128)(2,1)S(1)} collective-permute-done((bf16[16,8320]{1,0:T(8,128)(2,1)S(1)}, bf16[16,8320]{1,0:T(8,128)(2,1)S(1)}, u32[]{:S(2)}, u32[]{:S(2)}) %collective-permute-start.6) | collective-permute-done | bytes 266272 | tf_op jit(solution)/shard_map/ppermute | solution.py:376
  26.0 1.1 %serve.4 = bf16[2,16,4096]{2,1,0:T(8,128)(2,1)S(1)} custom-call(bf16[16,8320]{1,0:T(8,128)(2,1)S(1)} %collective-permute-done.6.refs_0_, bf16[2,64,4096]{2,1,0:T(8,128)(2,1)S(1)} %get-tuple-element.37.refs_2_.refs_1_, bf16[2,64,4096]{2,1,0:T(8,128)(2,1)S(1)} %collective-permute-done.2.refs_3_.refs_2_, ...), custom_call_target="tpu_custom_call" | custom-call | tf_op jit(solution)/shard_map/serve/pallas_call | solution.py:165
  27.1 3.8 %collective-permute-start.7 = (bf16[2,16,4096]{2,1,0:T(8,128)(2,1)S(1)}, bf16[2,16,4096]{2,1,0:T(8,128)(2,1)S(1)}, u32[]{:S(2)}, u32[]{:S(2)}) collective-permute-start(bf16[2,16,4096]{2,1,0:T(8,128)(2,1)S(1)} %serve.4), channel_id=1, source_target_pairs={{0,8},{1,11},{2,10},{3,9},{4,12},{5,15},{6,14},{7,13},{8,0},{9,3},... | collective-permute-start | bytes 786440 | tf_op jit(solution)/shard_map/ppermute | solution.py:376
  30.9 13.7 %collective-permute-done.8.refs_0_ = bf16[16,8320]{1,0:T(8,128)(2,1)S(1)} collective-permute-done((bf16[16,8320]{1,0:T(8,128)(2,1)S(1)}, bf16[16,8320]{1,0:T(8,128)(2,1)S(1)}, u32[]{:S(2)}, u32[]{:S(2)}) %collective-permute-start.8) | collective-permute-done | bytes 266272 | tf_op jit(solution)/shard_map/ppermute | solution.py:376
  44.6 1.1 %serve.5 = bf16[2,16,4096]{2,1,0:T(8,128)(2,1)S(1)} custom-call(bf16[16,8320]{1,0:T(8,128)(2,1)S(1)} %collective-permute-done.8.refs_0_, bf16[2,64,4096]{2,1,0:T(8,128)(2,1)S(1)} %get-tuple-element.37.refs_2_.refs_1_, bf16[2,64,4096]{2,1,0:T(8,128)(2,1)S(1)} %collective-permute-done.2.refs_3_.refs_2_, ...), custom_call_target="tpu_custom_call" | custom-call | tf_op jit(solution)/shard_map/serve/pallas_call | solution.py:165
  45.7 1.2 %collective-permute-start.9 = (bf16[2,16,4096]{2,1,0:T(8,128)(2,1)S(1)}, bf16[2,16,4096]{2,1,0:T(8,128)(2,1)S(1)}, u32[]{:S(2)}, u32[]{:S(2)}) collective-permute-start(bf16[2,16,4096]{2,1,0:T(8,128)(2,1)S(1)} %serve.5), channel_id=1, source_target_pairs={{0,12},{1,15},{2,14},{3,13},{4,8},{5,11},{6,10},{7,9},{8,4},{9,7},... | collective-permute-start | bytes 786440 | tf_op jit(solution)/shard_map/ppermute | solution.py:376
  46.9 0.0 collective-permute-done.4.refs_0_
  46.9 0.0 collective-permute-start.10
  46.9 0.0 collective-permute-done.5.refs_1_
  46.9 0.5 collective-permute-start.11
  47.4 1.1 %collective-permute-done.7.refs_2_ = bf16[2,16,4096]{2,1,0:T(8,128)(2,1)S(1)} collective-permute-done((bf16[2,16,4096]{2,1,0:T(8,128)(2,1)S(1)}, bf16[2,16,4096]{2,1,0:T(8,128)(2,1)S(1)}, u32[]{:S(2)}, u32[]{:S(2)}) %collective-permute-start.7) | collective-permute-done | bytes 262176 | tf_op jit(solution)/shard_map/ppermute | solution.py:376
  48.6 0.0 collective-permute-start.12
  48.6 6.2 %collective-permute-done.9.refs_3_ = bf16[2,16,4096]{2,1,0:T(8,128)(2,1)S(1)} collective-permute-done((bf16[2,16,4096]{2,1,0:T(8,128)(2,1)S(1)}, bf16[2,16,4096]{2,1,0:T(8,128)(2,1)S(1)}, u32[]{:S(2)}, u32[]{:S(2)}) %collective-permute-start.9) | collective-permute-done | bytes 262176 | tf_op jit(solution)/shard_map/ppermute | solution.py:376
  54.7 0.0 collective-permute-start.13
  54.7 0.0 collective-permute-done.10.refs_4_
  54.7 0.0 collective-permute-done.11.refs_5_
  54.7 0.0 collective-permute-done.12.refs_6_
  54.8 1.5 %collective-permute-done.13.refs_7_ = bf16[2,16,4096]{2,1,0:T(8,128)(2,1)S(1)} collective-permute-done((bf16[2,16,4096]{2,1,0:T(8,128)(2,1)S(1)}, bf16[2,16,4096]{2,1,0:T(8,128)(2,1)S(1)}, u32[]{:S(2)}, u32[]{:S(2)}) %collective-permute-start.13) | collective-permute-done | bytes 262176 | tf_op jit(solution)/shard_map/ppermute | solution.py:380
  56.3 0.0 copy-done
  56.3 0.0 copy-done.1
  56.3 7.4 %attend.1 = bf16[64,4096]{1,0:T(8,128)(2,1)} custom-call(f32[4,512,128]{2,1,0:T(8,128)S(1)} %get-tuple-element.31.heads_ref, f32[512,128]{1,0:T(8,128)S(1)} %get-tuple-element.32.valid_ref, bf16[64,128]{1,0:T(8,128)(2,1)S(1)} %get-tuple-element.24.routing_ref, bf16[64,64,512]{2,1,0:T(8,128)(2,1)S(1)} %get-tuple-element.33.key_ref, ...), custom_call_target="tpu_custom_call" | custom-call | tf_op jit(solution)/shard_map/attend/pallas_call | solution.py:322
Async XLA Ops:
  0.0 16.9 %collective-permute-start.2 = (bf16[2,64,4096]{2,1,0:T(8,128)(2,1)}, bf16[2,64,4096]{2,1,0:T(8,128)(2,1)S(1)}, u32[]{:S(2)}, u32[]{:S(2)}) collective-permute-start(bf16[2,64,4096]{2,1,0:T(8,128)(2,1)} %bitcast.4), channel_id=1, source_target_pairs={{0,1},{1,0},{2,3},{3,2},{4,5},{5,4},{6,7},{7,6},{8,9},{9,8},{10,11... | collective-permute-start | bytes 3145736 | tf_op jit(solution)/shard_map/ppermute | solution.py:380
  0.7 16.3 %collective-permute-start.3 = (bf16[2,64,4096]{2,1,0:T(8,128)(2,1)}, bf16[2,64,4096]{2,1,0:T(8,128)(2,1)S(1)}, u32[]{:S(2)}, u32[]{:S(2)}) collective-permute-start(bf16[2,64,4096]{2,1,0:T(8,128)(2,1)} %up_hbm), channel_id=1, source_target_pairs={{0,1},{1,0},{2,3},{3,2},{4,5},{5,4},{6,7},{7,6},{8,9},{9,8},{10,11... | collective-permute-start | bytes 3145736 | tf_op jit(solution)/shard_map/ppermute | solution.py:380
  2.8 8.0 %collective-permute-start = (bf16[16,8320]{1,0:T(8,128)(2,1)S(1)}, bf16[16,8320]{1,0:T(8,128)(2,1)S(1)}, u32[]{:S(2)}, u32[]{:S(2)}) collective-permute-start(bf16[16,8320]{1,0:T(8,128)(2,1)S(1)} %get-tuple-element.35), channel_id=1, source_target_pairs={{0,0},{1,3},{2,2},{3,1},{4,4},{5,7},{6,6},{7,5},{8,8},{9,11},{10,1... | collective-permute-start | bytes 798728 | tf_op jit(solution)/shard_map/ppermute | solution.py:376
  6.0 11.0 %collective-permute-start.1 = (bf16[16,8320]{1,0:T(8,128)(2,1)S(1)}, bf16[16,8320]{1,0:T(8,128)(2,1)S(1)}, u32[]{:S(2)}, u32[]{:S(2)}) collective-permute-start(bf16[16,8320]{1,0:T(8,128)(2,1)S(1)} %get-tuple-element.36), channel_id=1, source_target_pairs={{0,4},{1,7},{2,6},{3,5},{4,0},{5,3},{6,2},{7,1},{8,12},{9,15},{10,... | collective-permute-start | bytes 798728 | tf_op jit(solution)/shard_map/ppermute | solution.py:376
  7.3 18.7 %collective-permute-start.6 = (bf16[16,8320]{1,0:T(8,128)(2,1)S(1)}, bf16[16,8320]{1,0:T(8,128)(2,1)S(1)}, u32[]{:S(2)}, u32[]{:S(2)}) collective-permute-start(bf16[16,8320]{1,0:T(8,128)(2,1)S(1)} %get-tuple-element.41), channel_id=1, source_target_pairs={{0,8},{1,11},{2,10},{3,9},{4,12},{5,15},{6,14},{7,13},{8,0},{9,3},... | collective-permute-start | bytes 798728 | tf_op jit(solution)/shard_map/ppermute | solution.py:376
  10.8 33.8 %collective-permute-start.8 = (bf16[16,8320]{1,0:T(8,128)(2,1)S(1)}, bf16[16,8320]{1,0:T(8,128)(2,1)S(1)}, u32[]{:S(2)}, u32[]{:S(2)}) collective-permute-start(bf16[16,8320]{1,0:T(8,128)(2,1)S(1)} %get-tuple-element.42), channel_id=1, source_target_pairs={{0,12},{1,15},{2,14},{3,13},{4,8},{5,11},{6,10},{7,9},{8,4},{9,7},... | collective-permute-start | bytes 798728 | tf_op jit(solution)/shard_map/ppermute | solution.py:376
  18.1 28.8 %collective-permute-start.4 = (bf16[2,16,4096]{2,1,0:T(8,128)(2,1)S(1)}, bf16[2,16,4096]{2,1,0:T(8,128)(2,1)S(1)}, u32[]{:S(2)}, u32[]{:S(2)}) collective-permute-start(bf16[2,16,4096]{2,1,0:T(8,128)(2,1)S(1)} %get-tuple-element.39), channel_id=1, source_target_pairs={{0,0},{1,3},{2,2},{3,1},{4,4},{5,7},{6,6},{7,5},{8,8},{9,11},{10,1... | collective-permute-start | bytes 786440 | tf_op jit(solution)/shard_map/ppermute | solution.py:376
  20.5 35.7 %copy-start = (bf16[64,512]{1,0:T(8,128)(2,1)S(1)}, bf16[64,512]{1,0:T(8,128)(2,1)}, u32[]{:S(2)}) copy-start(bf16[64,512]{1,0:T(8,128)(2,1)} %fresh_k_ref.1) | copy-start | bytes 196612
  20.5 35.7 %copy-start.1 = (bf16[64,512]{1,0:T(8,128)(2,1)S(1)}, bf16[64,512]{1,0:T(8,128)(2,1)}, u32[]{:S(2)}) copy-start(bf16[64,512]{1,0:T(8,128)(2,1)} %fresh_v_ref.1) | copy-start | bytes 196612
  20.5 26.4 %collective-permute-start.5 = (bf16[2,16,4096]{2,1,0:T(8,128)(2,1)S(1)}, bf16[2,16,4096]{2,1,0:T(8,128)(2,1)S(1)}, u32[]{:S(2)}, u32[]{:S(2)}) collective-permute-start(bf16[2,16,4096]{2,1,0:T(8,128)(2,1)S(1)} %get-tuple-element.40), channel_id=1, source_target_pairs={{0,4},{1,7},{2,6},{3,5},{4,0},{5,3},{6,2},{7,1},{8,12},{9,15},{10,... | collective-permute-start | bytes 786440 | tf_op jit(solution)/shard_map/ppermute | solution.py:376
  27.1 21.5 %collective-permute-start.7 = (bf16[2,16,4096]{2,1,0:T(8,128)(2,1)S(1)}, bf16[2,16,4096]{2,1,0:T(8,128)(2,1)S(1)}, u32[]{:S(2)}, u32[]{:S(2)}) collective-permute-start(bf16[2,16,4096]{2,1,0:T(8,128)(2,1)S(1)} %serve.4), channel_id=1, source_target_pairs={{0,8},{1,11},{2,10},{3,9},{4,12},{5,15},{6,14},{7,13},{8,0},{9,3},... | collective-permute-start | bytes 786440 | tf_op jit(solution)/shard_map/ppermute | solution.py:376
  45.7 9.1 %collective-permute-start.9 = (bf16[2,16,4096]{2,1,0:T(8,128)(2,1)S(1)}, bf16[2,16,4096]{2,1,0:T(8,128)(2,1)S(1)}, u32[]{:S(2)}, u32[]{:S(2)}) collective-permute-start(bf16[2,16,4096]{2,1,0:T(8,128)(2,1)S(1)} %serve.5), channel_id=1, source_target_pairs={{0,12},{1,15},{2,14},{3,13},{4,8},{5,11},{6,10},{7,9},{8,4},{9,7},... | collective-permute-start | bytes 786440 | tf_op jit(solution)/shard_map/ppermute | solution.py:376
  46.9 7.8 %collective-permute-start.10 = (bf16[2,16,4096]{2,1,0:T(8,128)(2,1)S(1)}, bf16[2,16,4096]{2,1,0:T(8,128)(2,1)S(1)}, u32[]{:S(2)}, u32[]{:S(2)}) collective-permute-start(bf16[2,16,4096]{2,1,0:T(8,128)(2,1)S(1)} %collective-permute-done.4.refs_0_), channel_id=1, source_target_pairs={{0,1},{1,0},{2,3},{3,2},{4,5},{5,4},{6,7},{7,6},{8,9},{9,8},{10,11... | collective-permute-start | bytes 786440 | tf_op jit(solution)/shard_map/ppermute | solution.py:380
  46.9 7.8 %collective-permute-start.11 = (bf16[2,16,4096]{2,1,0:T(8,128)(2,1)S(1)}, bf16[2,16,4096]{2,1,0:T(8,128)(2,1)S(1)}, u32[]{:S(2)}, u32[]{:S(2)}) collective-permute-start(bf16[2,16,4096]{2,1,0:T(8,128)(2,1)S(1)} %collective-permute-done.5.refs_1_), channel_id=1, source_target_pairs={{0,1},{1,0},{2,3},{3,2},{4,5},{5,4},{6,7},{7,6},{8,9},{9,8},{10,11... | collective-permute-start | bytes 786440 | tf_op jit(solution)/shard_map/ppermute | solution.py:380
  48.6 6.2 %collective-permute-start.12 = (bf16[2,16,4096]{2,1,0:T(8,128)(2,1)S(1)}, bf16[2,16,4096]{2,1,0:T(8,128)(2,1)S(1)}, u32[]{:S(2)}, u32[]{:S(2)}) collective-permute-start(bf16[2,16,4096]{2,1,0:T(8,128)(2,1)S(1)} %collective-permute-done.7.refs_2_), channel_id=1, source_target_pairs={{0,1},{1,0},{2,3},{3,2},{4,5},{5,4},{6,7},{7,6},{8,9},{9,8},{10,11... | collective-permute-start | bytes 786440 | tf_op jit(solution)/shard_map/ppermute | solution.py:380
  54.7 1.5 %collective-permute-start.13 = (bf16[2,16,4096]{2,1,0:T(8,128)(2,1)S(1)}, bf16[2,16,4096]{2,1,0:T(8,128)(2,1)S(1)}, u32[]{:S(2)}, u32[]{:S(2)}) collective-permute-start(bf16[2,16,4096]{2,1,0:T(8,128)(2,1)S(1)} %collective-permute-done.9.refs_3_), channel_id=1, source_target_pairs={{0,1},{1,0},{2,3},{3,2},{4,5},{5,4},{6,7},{7,6},{8,9},{9,8},{10,11... | collective-permute-start | bytes 786440 | tf_op jit(solution)/shard_map/ppermute | solution.py:380

commit v3 on v2

v3 whole, which is shorter than its diff:
```python
import functools
import math

import jax
import jax.numpy as jnp
from jax import lax
from jax.experimental import pallas as pl
from jax.experimental.pallas import tpu as pltpu
from jax.sharding import PartitionSpec as P

HEAD_SIZE = 128
ADAPTER_SCALE = 2.0
MASKED = -1e30
FACTOR = 1.0 / math.sqrt(HEAD_SIZE)
LANES = 128
ROWS = 16
MIB = 1024 * 1024

VMEM = pl.BlockSpec(memory_space=pltpu.VMEM)
ANYWHERE = pl.BlockSpec(memory_space=pl.ANY)


def grant(mib):
    return pltpu.CompilerParams(vmem_limit_bytes=mib * MIB)


def column_of(row):
    count = row.shape[1]
    here = lax.broadcasted_iota(jnp.int32, (count, count), 0)
    there = lax.broadcasted_iota(jnp.int32, (count, count), 1)
    spread = jnp.broadcast_to(row, (count, count))
    return jnp.sum(jnp.where(here == there, spread, 0), axis=1, keepdims=True)


def in_hbm(array):
    return pltpu.with_memory_space_constraint(array, pltpu.HBM)


def as_bf16(mask):
    return mask.astype(jnp.float32).astype(jnp.bfloat16)


def pack_kernel(pool_count, tp_count, capacity, owned_count, adapter_hbm, store_hbm, hidden_hbm, *refs):
    *outs, routing_ref, place_ref, held_ref, adapter_ref, store_ref, sems, index_sems = refs
    chunks = sems.shape[0]
    step = held_ref.shape[1] // chunks
    small = [
        pltpu.make_async_copy(adapter_hbm, adapter_ref, index_sems.at[0]),
        pltpu.make_async_copy(store_hbm, store_ref, index_sems.at[1]),
    ]
    copies = [
        pltpu.make_async_copy(
            hidden_hbm.at[:, pl.ds(c * step, step)], held_ref.at[:, pl.ds(c * step, step)], sems.at[c]
        )
        for c in range(chunks)
    ]
    for copy in small + copies:
        copy.start()
    for copy in small:
        copy.wait()
    adapters = store_ref.shape[1]
    requests = adapter_ref.shape[1]
    slot_total = pool_count // tp_count * capacity
    matches = lax.broadcasted_iota(jnp.int32, (adapters, requests), 0) == adapter_ref[...]
    position = jnp.sum(jnp.where(matches, column_of(store_ref[...]), 0), axis=0, keepdims=True)
    owner = lax.div(position, jnp.int32(owned_count))
    held = position - owner * owned_count
    distance = lax.bitwise_xor(owner, jnp.broadcast_to(lax.axis_index("pool"), owner.shape))
    step_of = lax.div(distance, jnp.int32(tp_count))
    mine = distance - step_of * tp_count == lax.axis_index("tp")
    earlier = lax.broadcasted_iota(jnp.int32, (requests, requests), 0) < lax.broadcasted_iota(
        jnp.int32, (requests, requests), 1
    )
    same = column_of(owner) == owner
    rank = jnp.sum(jnp.where(same & earlier, 1, 0), axis=0, keepdims=True)
    target = step_of * capacity + rank + jnp.where(mine, 0, slot_total)
    place_ref[0:1, :] = target
    place_ref[1:2, :] = held
    for copy in copies:
        copy.wait()
    pack_rows(target, held, held_ref, slot_total // 2, outs)
    back = lax.broadcasted_iota(jnp.int32, (requests, tp_count * slot_total), 1) == column_of(target)
    routing_ref[...] = as_bf16(back)


def pack_rows(target, held, held_ref, first, outs):
    width = held_ref.shape[1]
    requests = held_ref.shape[0]
    count = sum(out.shape[0] for out in outs)
    routing = lax.broadcasted_iota(jnp.int32, (count, requests), 0) + first == target
    held_slot = jnp.sum(jnp.where(routing, held, 0), axis=1, keepdims=True)
    tags = jnp.broadcast_to(held_slot, (count, LANES)).astype(jnp.float32).astype(jnp.bfloat16)
    routing_b = as_bf16(routing)
    chunks = 4
    step = width // chunks
    for c in range(chunks):
        columns = slice(c * step, (c + 1) * step)
        packed = jnp.dot(
            routing_b, held_ref[:, columns], preferred_element_type=jnp.float32
        ).astype(jnp.bfloat16)
        for g, out in enumerate(outs):
            out[:, columns] = packed[g * out.shape[0] : (g + 1) * out.shape[0]]
    for g, out in enumerate(outs):
        out[:, width:] = tags[g * out.shape[0] : (g + 1) * out.shape[0]]


def pack_near_kernel(place_ref, held_ref, *outs):
    pack_rows(place_ref[0:1, :], place_ref[1:2, :], held_ref, 0, outs)


def pack(hidden, request_adapter, adapter_store_row, pool_count, tp_count, capacity, owned_count, group_rows):
    requests, width = hidden.shape
    adapters = adapter_store_row.shape[0]
    slot_total = pool_count // tp_count * capacity
    group_count = slot_total // group_rows // 2
    chunks = 4
    rows = [pltpu.VMEM((group_rows, width + LANES), jnp.bfloat16)] * group_count
    *far, routing_b, place, held = pl.pallas_call(
        functools.partial(pack_kernel, pool_count, tp_count, capacity, owned_count),
        out_shape=rows
        + [
            pltpu.VMEM((requests, tp_count * slot_total), jnp.bfloat16),
            pltpu.VMEM((2, requests), jnp.int32),
            pltpu.VMEM((requests, width), jnp.bfloat16),
        ],
        in_specs=[ANYWHERE] * 3,
        out_specs=[VMEM] * (group_count + 3),
        scratch_shapes=[
            pltpu.VMEM((1, requests), jnp.int32),
            pltpu.VMEM((1, adapters), jnp.int32),
            pltpu.SemaphoreType.DMA((chunks,)),
            pltpu.SemaphoreType.DMA((2,)),
        ],
        compiler_params=grant(8),
        name="pack",
    )(
        in_hbm(request_adapter.reshape(1, requests)),
        in_hbm(adapter_store_row.reshape(1, adapters)),
        in_hbm(hidden),
    )
    return far, routing_b, place, held


def pack_near(place, held, like):
    return pl.pallas_call(
        pack_near_kernel,
        out_shape=[pltpu.VMEM(row.shape, row.dtype) for row in like],
        in_specs=[VMEM] * 2,
        out_specs=[VMEM] * len(like),
        compiler_params=grant(8),
        name="pack_near",
    )(place, held)


def serve_kernel(count, parts, *refs):
    rows, (down_ref, down_far_ref, up_ref, up_far_ref), outs = (
        refs[:count],
        refs[count : count + 4],
        refs[count + 4 :],
    )
    owned_count, rank, width = down_ref.shape
    here = lax.axis_index("tp")
    there = 1 - here
    tags = jnp.concatenate([row[:, 2 * width : 2 * width + 1] for row in rows], axis=0)
    tags = tags.astype(jnp.float32)
    middle = jnp.zeros((tags.shape[0], rank), jnp.float32)
    for half, factors in ((here, down_ref), (there, down_far_ref)):
        columns = pl.ds(pl.multiple_of(half * width, LANES), width)
        features = jnp.concatenate([row[:, columns] for row in rows], axis=0)
        for slot in range(owned_count):
            partial = lax.dot_general(
                features,
                factors[slot],
                (((1,), (1,)), ((), ())),
                preferred_element_type=jnp.float32,
            )
            middle = middle + jnp.where(tags == float(slot), partial, 0.0)
    middle = middle.astype(jnp.bfloat16).astype(jnp.float32)
    chosen = jnp.concatenate(
        [jnp.where(tags == float(slot), middle, 0.0) for slot in range(owned_count)], axis=1
    ).astype(jnp.bfloat16)
    step = min(width, 1024)
    for half, factors in ((here, up_ref), (there, up_far_ref)):
        for c in range(width // step):
            columns = slice(c * step, (c + 1) * step)
            stacked = jnp.concatenate([factors[slot, :, columns] for slot in range(owned_count)], axis=0)
            total = jnp.dot(chosen, stacked, preferred_element_type=jnp.float32)
            total = (ADAPTER_SCALE * total).astype(jnp.bfloat16)
            at = 0
            for k in range(len(rows)):
                part, column = divmod(c * step, width // parts)
                out = outs[k * parts + part]
                out[half, :, column : column + step] = total[at : at + out.shape[1]]
                at += out.shape[1]


def serve(rows, factors, parts=1):
    width = factors[0].shape[2]
    return pl.pallas_call(
        functools.partial(serve_kernel, len(rows), parts),
        out_shape=[
            pltpu.VMEM((2, row.shape[0], width // parts), jnp.bfloat16) for row in rows for _ in range(parts)
        ],
        in_specs=[VMEM] * (len(rows) + 4),
        out_specs=[VMEM] * (len(rows) * parts),
        compiler_params=grant(8),
        name="serve",
    )(*rows, *factors)


def prepare_kernel(
    base_hbm,
    lengths_hbm,
    fresh_k_hbm,
    fresh_v_hbm,
    down_hbm,
    up_hbm,
    key_hbm,
    value_hbm,
    heads_ref,
    score_ref,
    fresh_k_ref,
    fresh_v_ref,
    down_ref,
    up_ref,
    key_ref,
    value_ref,
    base_in,
    lengths_in,
    fresh_k_in,
    fresh_v_in,
    sems,
):
    pairs = [
        (lengths_hbm, lengths_in),
        (base_hbm, base_in),
        (fresh_k_hbm, fresh_k_in),
        (fresh_v_hbm, fresh_v_in),
        (key_hbm, key_ref),
        (down_hbm, down_ref),
        (up_hbm, up_ref),
        (value_hbm, value_ref),
    ]
    copies = [pltpu.make_async_copy(*pair, sems.at[i]) for i, pair in enumerate(pairs)]
    for copy in copies:
        copy.start()
    for copy in copies[:4]:
        copy.wait()
    requests = base_in.shape[0]
    cached_count, rows, _ = heads_ref.shape
    group_size = rows // requests
    for j in range(cached_count):
        lanes = slice(j * HEAD_SIZE, (j + 1) * HEAD_SIZE)
        for h in range(group_size):
            at = (j * group_size + h) * HEAD_SIZE
            here = pl.ds(h, requests, stride=group_size)
            heads_ref[j, here, :] = base_in[:, at : at + HEAD_SIZE].astype(jnp.float32)
            fresh_k_ref[j, here, :] = fresh_k_in[:, lanes].astype(jnp.float32)
            fresh_v_ref[j, here, :] = fresh_v_in[:, lanes].astype(jnp.float32)
    pair_count, places, _ = key_ref.shape
    cached_len = places * pair_count // requests
    side = requests // pair_count
    request = lax.broadcasted_iota(jnp.int32, (requests, places), 0)
    place = lax.broadcasted_iota(jnp.int32, (requests, places), 1)
    place = place - lax.rem(request, jnp.int32(side)) * cached_len
    allowed = (place >= 0) & (place < column_of(lengths_in[...]))
    allowed = allowed.astype(jnp.float32)
    for h in range(group_size):
        score_ref[0, pl.ds(h, requests, stride=group_size), :] = allowed
    valid = score_ref[0] > 0.0
    copies[4].wait()
    block = side * group_size
    for j in range(cached_count):
        lanes = slice(j * HEAD_SIZE, (j + 1) * HEAD_SIZE)
        for p in range(pair_count):
            here = slice(p * block, (p + 1) * block)
            score_ref[j, here, :] = lax.dot_general(
                heads_ref[j, here, :].astype(jnp.bfloat16),
                key_ref[p, :, lanes],
                (((1,), (1,)), ((), ())),
                preferred_element_type=jnp.float32,
            )
        score_ref[j] = jnp.where(valid, score_ref[j] * FACTOR, MASKED)
    for copy in copies[5:]:
        copy.wait()


def prepare(base_query, lengths, new_key, new_value, adapter_down, adapter_up, key_cache, value_cache):
    requests, features = base_query.shape
    cached_count = new_key.shape[1] // HEAD_SIZE
    rows = requests * features // (HEAD_SIZE * cached_count)
    places = key_cache.shape[1]
    held = [adapter_down, adapter_up, key_cache, value_cache]
    moved = [base_query, lengths.reshape(1, requests), new_key, new_value]
    return pl.pallas_call(
        prepare_kernel,
        out_shape=[
            pltpu.VMEM((cached_count, rows, HEAD_SIZE), jnp.float32),
            pltpu.VMEM((cached_count, rows, places), jnp.float32),
            pltpu.VMEM((cached_count, rows, HEAD_SIZE), jnp.float32),
            pltpu.VMEM((cached_count, rows, HEAD_SIZE), jnp.float32),
        ]
        + [pltpu.VMEM(array.shape, array.dtype) for array in held],
        in_specs=[ANYWHERE] * 8,
        out_specs=[VMEM] * 8,
        scratch_shapes=[pltpu.VMEM(array.shape, array.dtype) for array in moved]
        + [pltpu.SemaphoreType.DMA((8,))],
        compiler_params=grant(8),
        cost_estimate=pl.CostEstimate(
            flops=0, bytes_accessed=4 * key_cache.size + 4 * adapter_up.size, transcendentals=0
        ),
        name="prepare",
    )(*[in_hbm(array) for array in moved + held])


def attend_kernel(
    first,
    counts,
    heads_ref,
    score_ref,
    fresh_k_ref,
    fresh_v_ref,
    key_ref,
    value_ref,
    routing_ref,
    *refs,
):
    count = len(counts)
    returned = refs[:count]
    out_hbm, delta_ref, weight_ref, mixed_ref, out_ref, sems = refs[-6:]
    pair_count, _, _ = key_ref.shape
    _, rows, _ = heads_ref.shape
    requests = out_hbm.shape[0]
    group_size = rows // requests
    block = rows // pair_count
    half = lax.axis_index("tp")
    width = group_size * HEAD_SIZE
    copies = []
    for k in range(out_ref.shape[0]):
        j = first + k
        lanes = slice(j * HEAD_SIZE, (j + 1) * HEAD_SIZE)
        arrived = jnp.concatenate(
            [piece[half, :, (j - at) * width : (j - at + 1) * width] for piece, at in zip(returned, counts)],
            axis=0,
        )
        delta = jnp.dot(routing_ref[...], arrived, preferred_element_type=jnp.float32)
        for h in range(group_size):
            delta_ref[pl.ds(h, requests, stride=group_size), :] = delta[
                :, h * HEAD_SIZE : (h + 1) * HEAD_SIZE
            ]
        for p in range(pair_count):
            here = slice(p * block, (p + 1) * block)
            weight_ref[here, :] = lax.dot_general(
                delta_ref[here, :].astype(jnp.bfloat16),
                key_ref[p, :, lanes],
                (((1,), (1,)), ((), ())),
                preferred_element_type=jnp.float32,
            )
        scores = score_ref[j] + weight_ref[...] * FACTOR
        own = (heads_ref[j] + delta_ref[...]) * fresh_k_ref[j]
        own = jnp.sum(own, axis=1, keepdims=True) * FACTOR
        highest = jnp.maximum(jnp.max(scores, axis=1, keepdims=True), own)
        weights = jnp.exp(scores - highest)
        own_weight = jnp.exp(own - highest)
        totals = jnp.sum(weights, axis=1, keepdims=True) + own_weight
        weight_ref[...] = weights
        own_b = own_weight.astype(jnp.bfloat16).astype(jnp.float32)
        for p in range(pair_count):
            here = slice(p * block, (p + 1) * block)
            mixed_ref[here, :] = jnp.dot(
                weight_ref[here, :].astype(jnp.bfloat16),
                value_ref[p, :, lanes],
                preferred_element_type=jnp.float32,
            )
        mixed_ref[...] = (mixed_ref[...] + own_b * fresh_v_ref[j]) / totals
        for h in range(group_size):
            out_ref[k, :, h * HEAD_SIZE : (h + 1) * HEAD_SIZE] = mixed_ref[
                pl.ds(h, requests, stride=group_size), :
            ].astype(jnp.bfloat16)
        copy = pltpu.make_async_copy(
            out_ref.at[k], out_hbm.at[:, pl.ds(j * width, width)], sems.at[k]
        )
        copy.start()
        copies.append(copy)
    for copy in copies:
        copy.wait()


def attend(held, routing_b, returned, first, span, counts, out=None):
    cached_count, rows, _ = held[0].shape
    requests = routing_b.shape[0]
    width = rows // requests * HEAD_SIZE
    operands = [*held, routing_b, *returned]
    aliases = {}
    if out is not None:
        aliases = {len(operands): 0}
        operands.append(out)
    return pl.pallas_call(
        functools.partial(attend_kernel, first, counts),
        out_shape=jax.ShapeDtypeStruct((requests, cached_count * width), jnp.bfloat16),
        in_specs=[VMEM] * (len(held) + 1 + len(returned)) + [ANYWHERE] * len(aliases),
        out_specs=ANYWHERE,
        input_output_aliases=aliases,
        scratch_shapes=[
            pltpu.VMEM((rows, HEAD_SIZE), jnp.float32),
            pltpu.VMEM((rows, held[1].shape[2]), jnp.float32),
            pltpu.VMEM((rows, HEAD_SIZE), jnp.float32),
            pltpu.VMEM((span, requests, width), jnp.bfloat16),
            pltpu.SemaphoreType.DMA((span,)),
        ],
        compiler_params=grant(8),
        name="attend",
    )(*operands)


def after(arrays, *tokens):
    return lax.optimization_barrier((tuple(arrays), tokens))[0]


def shards(
    hidden,
    base_query,
    key_cache,
    value_cache,
    new_key,
    new_value,
    lengths,
    request_adapter,
    adapter_store_row,
    adapter_down,
    adapter_up,
):
    request_rows = hidden.shape[0]
    pool_count = lax.axis_size("pool")
    tp_count = lax.axis_size("tp")
    capacity = max(2, 2 * request_rows // pool_count)
    owned_count = adapter_down.shape[0]
    step_count = pool_count // tp_count
    per_group = max(1, ROWS // capacity)
    group_count = step_count // per_group
    adapter_down = jnp.swapaxes(adapter_down, 1, 2)

    def move(g, rows):
        parts = []
        for k in range(per_group):
            step = g * per_group + k
            part = rows
            if per_group > 1:
                part = lax.slice_in_dim(rows, k * capacity, (k + 1) * capacity, axis=rows.ndim - 2)
            pairs = [
                (i * tp_count + c, (i ^ (tp_count * step + c)) * tp_count + c)
                for i in range(pool_count)
                for c in range(tp_count)
            ]
            parts.append(lax.ppermute(part, ("pool", "tp"), pairs))
        return parts[0] if per_group == 1 else jnp.concatenate(parts, axis=rows.ndim - 2)

    def swap(array):
        return lax.ppermute(array, "tp", [(0, 1), (1, 0)])

    far_rows, routing_b, place, spread = pack(
        hidden, request_adapter, adapter_store_row, pool_count, tp_count, capacity, owned_count, per_group * capacity
    )
    factors = [adapter_down, swap(adapter_down), adapter_up, swap(adapter_up)]
    cached_len, features = key_cache.shape[1:]
    pairs = (request_rows // 2, 2 * cached_len, features)
    *held, factors[0], factors[2], key_cache, value_cache = prepare(
        *after(
            [
                base_query,
                lengths,
                new_key,
                new_value,
                adapter_down,
                adapter_up,
                key_cache.reshape(pairs),
                value_cache.reshape(pairs),
            ],
            routing_b,
        )
    )
    held = [*held, key_cache, value_cache]
    *far, last = list(range(group_count // 2, group_count))
    near = list(range(group_count // 2))
    ready = after([place, spread], factors[1], factors[3])
    groups = [*pack_near(*ready, far_rows), *far_rows]
    arrived = {g: move(g, groups[g]) for g in [*far, last, *near]}
    early = serve([arrived[g] for g in far], factors)
    served = serve(after([arrived[g] for g in near], early[0]), factors)
    returned = {g: move(g, rows) for g, rows in zip(near, served)}
    returned |= {g: move(g, rows) for g, rows in zip(far, after(early, served[0]))}
    final = serve(after([arrived[last]], served[0]), factors, parts=2)
    final = [move(last, rows) for rows in final]
    whole = [returned[g] for g in range(last)]
    others = [swap(rows) for rows in whole]
    cached_count = features // HEAD_SIZE
    span = cached_count // len(final)
    out = None
    for k, rows in enumerate(final):
        first = k * span
        pieces = [*whole, rows, *others, swap(rows)]
        counts = [*[0] * last, first] * 2
        out = attend(held, routing_b, pieces, first, span, counts, out)
    return out


def solution(mesh):
    placed = (
        P(("rep", "pool"), None),
        P(("rep", "pool"), "tp"),
        P(("rep", "pool"), None, "tp"),
        P(("rep", "pool"), None, "tp"),
        P(("rep", "pool"), "tp"),
        P(("rep", "pool"), "tp"),
        P(("rep", "pool")),
        P(("rep", "pool")),
        P("rep"),
        P("pool", "tp", None),
        P("pool", None, "tp"),
    )
    return jax.shard_map(
        shards, mesh=mesh, in_specs=placed, out_specs=P(("rep", "pool"), "tp"), check_vma=False
    )
```

time: 63.8 us -> 59.3 us (0.929)
  the two profiles are of different devices: /device:TPU:19 before, /device:TPU:1 now
where the time goes in v3:
time: 59.3 us; the launch traced here: 59.1 us
  starting transfers between devices  25 us (42%)
  waiting for transfers between devices  18.6 us (31%)
  Pallas kernels  15.5 us (26%)
    ppermute x9, starting transfers between devices, move(): parts.append(lax.ppermute(part, ('pool', 'tp'), pairs))  22.6 us
    ppermute x9, waiting for transfers between devices, move(): parts.append(lax.ppermute(part, ('pool', 'tp'), pairs))  18.6 us
    pallas_call x2, Pallas kernels, attend(): pl.pallas_call(functools.partial(attend_kernel, first, counts), out_shape...  5.53 us
    pallas_call x1, Pallas kernels, prepare(): pl.pallas_call(prepare_kernel, out_shape=[pltpu.VMEM((cached_count, rows,...  4.78 us
    pallas_call x3, Pallas kernels, serve(): pl.pallas_call(functools.partial(serve_kernel, len(rows), parts), out_sha...  3.33 us
    ppermute x7, starting transfers between devices, swap(): return lax.ppermute(array, 'tp', [(0, 1), (1, 0)])  2.36 us
    pallas_call x1, Pallas kernels, pack(): pl.pallas_call(functools.partial(pack_kernel, pool_count, tp_count, capac...  1.57 us
  transfers between devices with their start and end apart: 16, of which 3 were waited for; matrix products, arithmetic and copies ran while one was open for 0% of the time, Pallas kernels for 22%

profile of v3, /device:TPU:1, one launch (start us, length us, event | category | flops | bytes accessed | tf_op | source)
XLA Modules:
  0.0 59.1 jit_solution(4505343863751042256)
XLA Ops:
  0.0 0.1 collective-permute-start
  0.1 0.5 collective-permute-start.1
  0.5 1.6 %pack.1 = (bf16[16,8320]{1,0:T(8,128)(2,1)S(1)}, bf16[16,8320]{1,0:T(8,128)(2,1)S(1)}, bf16[64,128]{1,0:T(8,128)(2,1)S(1)}, s32[2,64]{1,0:T(2,128)S(1)}, bf16[64,8192]{1,0:T(8,128)(2,1)S(1)}) custom-call(s32[1,64]{1,0:T(1,128)} %bitcast.10, s32[1,16]{1,0:T(1,128)} %bitcast.11, bf16[64,8192]{1,0:T(8,128)(2,1)} %hidden_hbm.1), custom_call_target="tpu_custom_call" | custom-call | tf_op jit(solution)/shard_map/pack/pallas_call | solution.py:118
  2.1 4.3 %collective-permute-start.4 = (bf16[16,8320]{1,0:T(8,128)(2,1)S(1)}, bf16[16,8320]{1,0:T(8,128)(2,1)S(1)}, u32[]{:S(2)}, u32[]{:S(2)}) collective-permute-start(bf16[16,8320]{1,0:T(8,128)(2,1)S(1)} %get-tuple-element.59), channel_id=1, source_target_pairs={{0,8},{1,11},{2,10},{3,9},{4,12},{5,15},{6,14},{7,13},{8,0},{9,3},... | collective-permute-start | bytes 798728 | tf_op jit(solution)/shard_map/ppermute | solution.py:455
  6.4 0.0 collective-permute-done.refs_2_.refs_3_
  6.4 0.0 collective-permute-done.1.refs_4_.refs_5_
  6.4 0.3 pack_near.1
  6.7 2.2 %collective-permute-start.2 = (bf16[16,8320]{1,0:T(8,128)(2,1)S(1)}, bf16[16,8320]{1,0:T(8,128)(2,1)S(1)}, u32[]{:S(2)}, u32[]{:S(2)}) collective-permute-start(bf16[16,8320]{1,0:T(8,128)(2,1)S(1)} %get-tuple-element.57), channel_id=1, source_target_pairs={{0,0},{1,3},{2,2},{3,1},{4,4},{5,7},{6,6},{7,5},{8,8},{9,11},{10,1... | collective-permute-start | bytes 798728 | tf_op jit(solution)/shard_map/ppermute | solution.py:455
  8.9 2.2 %collective-permute-start.3 = (bf16[16,8320]{1,0:T(8,128)(2,1)S(1)}, bf16[16,8320]{1,0:T(8,128)(2,1)S(1)}, u32[]{:S(2)}, u32[]{:S(2)}) collective-permute-start(bf16[16,8320]{1,0:T(8,128)(2,1)S(1)} %get-tuple-element.58), channel_id=1, source_target_pairs={{0,4},{1,7},{2,6},{3,5},{4,0},{5,3},{6,2},{7,1},{8,12},{9,15},{10,... | collective-permute-start | bytes 798728 | tf_op jit(solution)/shard_map/ppermute | solution.py:455
  11.2 2.2 %collective-permute-start.8 = (bf16[16,8320]{1,0:T(8,128)(2,1)S(1)}, bf16[16,8320]{1,0:T(8,128)(2,1)S(1)}, u32[]{:S(2)}, u32[]{:S(2)}) collective-permute-start(bf16[16,8320]{1,0:T(8,128)(2,1)S(1)} %get-tuple-element.67), channel_id=1, source_target_pairs={{0,12},{1,15},{2,14},{3,13},{4,8},{5,11},{6,10},{7,9},{8,4},{9,7},... | collective-permute-start | bytes 798728 | tf_op jit(solution)/shard_map/ppermute | solution.py:455
  13.4 4.8 %prepare.1 = (f32[4,512,128]{2,1,0:T(8,128)S(1)}, f32[4,512,128]{2,1,0:T(8,128)S(1)}, f32[4,512,128]{2,1,0:T(8,128)S(1)}, f32[4,512,128]{2,1,0:T(8,128)S(1)}, bf...) custom-call(bf16[64,4096]{1,0:T(8,128)(2,1)} %base_hbm, ...), custom_call_target="tpu_custom_call" | custom-call | bytes 10485760 | tf_op jit(solution)/shard_map/prepare/pallas_call | solution.py:295
  18.2 0.0 collective-permute-done.4.refs_0_
  18.2 1.1 %serve.3 = bf16[2,16,4096]{2,1,0:T(8,128)(2,1)S(1)} custom-call(bf16[16,8320]{1,0:T(8,128)(2,1)S(1)} %collective-permute-done.4.refs_0_, bf16[2,64,4096]{2,1,0:T(8,128)(2,1)S(1)} %get-tuple-element.60.refs_1_.refs_2_, bf16[2,64,4096]{2,1,0:T(8,128)(2,1)S(1)} %collective-permute-done.refs_2_.refs_3_, ...), custom_call_target="tpu_custom_call" | custom-call | tf_op jit(solution)/shard_map/serve/pallas_call | solution.py:199
  19.3 0.0 collective-permute-done.2.refs_0_
  19.3 7.8 %collective-permute-done.3.refs_1_ = bf16[16,8320]{1,0:T(8,128)(2,1)S(1)} collective-permute-done((bf16[16,8320]{1,0:T(8,128)(2,1)S(1)}, bf16[16,8320]{1,0:T(8,128)(2,1)S(1)}, u32[]{:S(2)}, u32[]{:S(2)}) %collective-permute-start.3) | collective-permute-done | bytes 266272 | tf_op jit(solution)/shard_map/ppermute | solution.py:455
  27.1 1.1 %serve.4 = (bf16[2,16,4096]{2,1,0:T(8,128)(2,1)S(1)}, bf16[2,16,4096]{2,1,0:T(8,128)(2,1)S(1)}) custom-call(bf16[16,8320]{1,0:T(8,128)(2,1)S(1)} %collective-permute-done.2.refs_0_, bf16[16,8320]{1,0:T(8,128)(2,1)S(1)} %collective-permute-done.3.refs_1_, bf16[2,64,4096]{2,1,0:T(8,128)(2,1)S(1)} %get-tuple-element.60.refs_1_.refs_2_, ...), custom_call_target="tpu_custom_call" | custom-call | tf_op jit(solution)/shard_map/serve/pallas_call | solution.py:199
  28.3 2.4 %collective-permute-start.7 = (bf16[2,16,4096]{2,1,0:T(8,128)(2,1)S(1)}, bf16[2,16,4096]{2,1,0:T(8,128)(2,1)S(1)}, u32[]{:S(2)}, u32[]{:S(2)}) collective-permute-start(bf16[2,16,4096]{2,1,0:T(8,128)(2,1)S(1)} %serve.3), channel_id=1, source_target_pairs={{0,8},{1,11},{2,10},{3,9},{4,12},{5,15},{6,14},{7,13},{8,0},{9,3},... | collective-permute-start | bytes 786440 | tf_op jit(solution)/shard_map/ppermute | solution.py:455
  30.7 2.8 %collective-permute-start.6 = (bf16[2,16,4096]{2,1,0:T(8,128)(2,1)S(1)}, bf16[2,16,4096]{2,1,0:T(8,128)(2,1)S(1)}, u32[]{:S(2)}, u32[]{:S(2)}) collective-permute-start(bf16[2,16,4096]{2,1,0:T(8,128)(2,1)S(1)} %get-tuple-element.65), channel_id=1, source_target_pairs={{0,4},{1,7},{2,6},{3,5},{4,0},{5,3},{6,2},{7,1},{8,12},{9,15},{10,... | collective-permute-start | bytes 786440 | tf_op jit(solution)/shard_map/ppermute | solution.py:455
  33.5 2.1 %collective-permute-start.5 = (bf16[2,16,4096]{2,1,0:T(8,128)(2,1)S(1)}, bf16[2,16,4096]{2,1,0:T(8,128)(2,1)S(1)}, u32[]{:S(2)}, u32[]{:S(2)}) collective-permute-start(bf16[2,16,4096]{2,1,0:T(8,128)(2,1)S(1)} %get-tuple-element.64), channel_id=1, source_target_pairs={{0,0},{1,3},{2,2},{3,1},{4,4},{5,7},{6,6},{7,5},{8,8},{9,11},{10,1... | collective-permute-start | bytes 786440 | tf_op jit(solution)/shard_map/ppermute | solution.py:455
  35.6 0.0 collective-permute-done.8.refs_0_
  35.6 1.1 %serve.5 = (bf16[2,16,2048]{2,1,0:T(8,128)(2,1)S(1)}, bf16[2,16,2048]{2,1,0:T(8,128)(2,1)S(1)}) custom-call(bf16[16,8320]{1,0:T(8,128)(2,1)S(1)} %collective-permute-done.8.refs_0_, bf16[2,64,4096]{2,1,0:T(8,128)(2,1)S(1)} %get-tuple-element.60.refs_1_.refs_2_, bf16[2,64,4096]{2,1,0:T(8,128)(2,1)S(1)} %collective-permute-done.refs_2_.refs_3_, ...), custom_call_target="tpu_custom_call" | custom-call | tf_op jit(solution)/shard_map/serve/pallas_call | solution.py:199
  36.7 0.3 collective-permute-start.14
  37.0 7.4 %collective-permute-done.7.refs_2_ = bf16[2,16,4096]{2,1,0:T(8,128)(2,1)S(1)} collective-permute-done((bf16[2,16,4096]{2,1,0:T(8,128)(2,1)S(1)}, bf16[2,16,4096]{2,1,0:T(8,128)(2,1)S(1)}, u32[]{:S(2)}, u32[]{:S(2)}) %collective-permute-start.7) | collective-permute-done | bytes 262176 | tf_op jit(solution)/shard_map/ppermute | solution.py:455
  44.5 0.0 collective-permute-start.12
  44.5 0.0 collective-permute-done.6.refs_1_
  44.5 0.5 collective-permute-start.11
  45.0 0.0 collective-permute-done.5.refs_0_
  45.0 0.1 collective-permute-start.10
  45.1 4.0 %collective-permute-start.9 = (bf16[2,16,2048]{2,1,0:T(8,128)(2,1)S(1)}, bf16[2,16,2048]{2,1,0:T(8,128)(2,1)S(1)}, u32[]{:S(2)}, u32[]{:S(2)}) collective-permute-start(bf16[2,16,2048]{2,1,0:T(8,128)(2,1)S(1)} %get-tuple-element.69), channel_id=1, source_target_pairs={{0,12},{1,15},{2,14},{3,13},{4,8},{5,11},{6,10},{7,9},{8,4},{9,7},... | collective-permute-start | bytes 393224 | tf_op jit(solution)/shard_map/ppermute | solution.py:455
  49.0 0.0 collective-permute-done.14.refs_3_
  49.0 0.1 collective-permute-start.15
  49.2 3.3 %collective-permute-done.9.refs_3_ = bf16[2,16,2048]{2,1,0:T(8,128)(2,1)S(1)} collective-permute-done((bf16[2,16,2048]{2,1,0:T(8,128)(2,1)S(1)}, bf16[2,16,2048]{2,1,0:T(8,128)(2,1)S(1)}, u32[]{:S(2)}, u32[]{:S(2)}) %collective-permute-start.9) | collective-permute-done | bytes 131104 | tf_op jit(solution)/shard_map/ppermute | solution.py:455
  52.4 1.1 %collective-permute-start.13 = (bf16[2,16,2048]{2,1,0:T(8,128)(2,1)S(1)}, bf16[2,16,2048]{2,1,0:T(8,128)(2,1)S(1)}, u32[]{:S(2)}, u32[]{:S(2)}) collective-permute-start(bf16[2,16,2048]{2,1,0:T(8,128)(2,1)S(1)} %collective-permute-done.9.refs_3_), channel_id=1, source_target_pairs={{0,1},{1,0},{2,3},{3,2},{4,5},{5,4},{6,7},{7,6},{8,9},{9,8},{10,11... | collective-permute-start | bytes 393224 | tf_op jit(solution)/shard_map/ppermute | solution.py:459
  53.6 0.0 collective-permute-done.15.refs_7_
  53.6 0.0 collective-permute-done.12.refs_6_
  53.6 0.0 collective-permute-done.11.refs_5_
  53.6 0.0 collective-permute-done.10.refs_4_
  53.6 2.8 %attend.2.refs_8_ = bf16[64,4096]{1,0:T(8,128)(2,1)} custom-call(f32[4,512,128]{2,1,0:T(8,128)S(1)} %get-tuple-element.47.heads_ref, f32[4,512,128]{2,1,0:T(8,128)S(1)} %get-tuple-element.48.score_ref, f32[4,512,128]{2,1,0:T(8,128)S(1)} %get-tuple-element.49.fresh_k_ref, f32[4,512,128]{2,1,0:T(8,128)S(1)} %get-tuple-element.50.fresh_v_ref, ...), custom_call_target="tpu_custom_call" | custom-call | tf_op jit(solution)/shard_map/attend/pallas_call | solution.py:398
  56.4 0.0 collective-permute-done.13.refs_7_
  56.4 2.8 %attend.3 = bf16[64,4096]{1,0:T(8,128)(2,1)} custom-call(f32[4,512,128]{2,1,0:T(8,128)S(1)} %get-tuple-element.47.heads_ref, f32[4,512,128]{2,1,0:T(8,128)S(1)} %get-tuple-element.48.score_ref, f32[4,512,128]{2,1,0:T(8,128)S(1)} %get-tuple-element.49.fresh_k_ref, f32[4,512,128]{2,1,0:T(8,128)S(1)} %get-tuple-element.50.fresh_v_ref, ...), custom_call_target="tpu_custom_call", output_to_operand_aliasing={{}: (15, {})} | custom-call | tf_op jit(solution)/shard_map/attend/pallas_call | solution.py:398
Async XLA Ops:
  0.0 6.4 %collective-permute-start = (bf16[2,64,4096]{2,1,0:T(8,128)(2,1)}, bf16[2,64,4096]{2,1,0:T(8,128)(2,1)S(1)}, u32[]{:S(2)}, u32[]{:S(2)}) collective-permute-start(bf16[2,64,4096]{2,1,0:T(8,128)(2,1)} %bitcast.8), channel_id=1, source_target_pairs={{0,1},{1,0},{2,3},{3,2},{4,5},{5,4},{6,7},{7,6},{8,9},{9,8},{10,11... | collective-permute-start | bytes 3145736 | tf_op jit(solution)/shard_map/ppermute | solution.py:459
  0.1 6.4 %collective-permute-start.1 = (bf16[2,64,4096]{2,1,0:T(8,128)(2,1)}, bf16[2,64,4096]{2,1,0:T(8,128)(2,1)S(1)}, u32[]{:S(2)}, u32[]{:S(2)}) collective-permute-start(bf16[2,64,4096]{2,1,0:T(8,128)(2,1)} %up_hbm), channel_id=1, source_target_pairs={{0,1},{1,0},{2,3},{3,2},{4,5},{5,4},{6,7},{7,6},{8,9},{9,8},{10,11... | collective-permute-start | bytes 3145736 | tf_op jit(solution)/shard_map/ppermute | solution.py:459
  2.1 16.1 %collective-permute-start.4 = (bf16[16,8320]{1,0:T(8,128)(2,1)S(1)}, bf16[16,8320]{1,0:T(8,128)(2,1)S(1)}, u32[]{:S(2)}, u32[]{:S(2)}) collective-permute-start(bf16[16,8320]{1,0:T(8,128)(2,1)S(1)} %get-tuple-element.59), channel_id=1, source_target_pairs={{0,8},{1,11},{2,10},{3,9},{4,12},{5,15},{6,14},{7,13},{8,0},{9,3},... | collective-permute-start | bytes 798728 | tf_op jit(solution)/shard_map/ppermute | solution.py:455
  6.7 12.6 %collective-permute-start.2 = (bf16[16,8320]{1,0:T(8,128)(2,1)S(1)}, bf16[16,8320]{1,0:T(8,128)(2,1)S(1)}, u32[]{:S(2)}, u32[]{:S(2)}) collective-permute-start(bf16[16,8320]{1,0:T(8,128)(2,1)S(1)} %get-tuple-element.57), channel_id=1, source_target_pairs={{0,0},{1,3},{2,2},{3,1},{4,4},{5,7},{6,6},{7,5},{8,8},{9,11},{10,1... | collective-permute-start | bytes 798728 | tf_op jit(solution)/shard_map/ppermute | solution.py:455
  8.9 18.2 %collective-permute-start.3 = (bf16[16,8320]{1,0:T(8,128)(2,1)S(1)}, bf16[16,8320]{1,0:T(8,128)(2,1)S(1)}, u32[]{:S(2)}, u32[]{:S(2)}) collective-permute-start(bf16[16,8320]{1,0:T(8,128)(2,1)S(1)} %get-tuple-element.58), channel_id=1, source_target_pairs={{0,4},{1,7},{2,6},{3,5},{4,0},{5,3},{6,2},{7,1},{8,12},{9,15},{10,... | collective-permute-start | bytes 798728 | tf_op jit(solution)/shard_map/ppermute | solution.py:455
  11.2 24.4 %collective-permute-start.8 = (bf16[16,8320]{1,0:T(8,128)(2,1)S(1)}, bf16[16,8320]{1,0:T(8,128)(2,1)S(1)}, u32[]{:S(2)}, u32[]{:S(2)}) collective-permute-start(bf16[16,8320]{1,0:T(8,128)(2,1)S(1)} %get-tuple-element.67), channel_id=1, source_target_pairs={{0,12},{1,15},{2,14},{3,13},{4,8},{5,11},{6,10},{7,9},{8,4},{9,7},... | collective-permute-start | bytes 798728 | tf_op jit(solution)/shard_map/ppermute | solution.py:455
  28.3 16.2 %collective-permute-start.7 = (bf16[2,16,4096]{2,1,0:T(8,128)(2,1)S(1)}, bf16[2,16,4096]{2,1,0:T(8,128)(2,1)S(1)}, u32[]{:S(2)}, u32[]{:S(2)}) collective-permute-start(bf16[2,16,4096]{2,1,0:T(8,128)(2,1)S(1)} %serve.3), channel_id=1, source_target_pairs={{0,8},{1,11},{2,10},{3,9},{4,12},{5,15},{6,14},{7,13},{8,0},{9,3},... | collective-permute-start | bytes 786440 | tf_op jit(solution)/shard_map/ppermute | solution.py:455
  30.7 13.8 %collective-permute-start.6 = (bf16[2,16,4096]{2,1,0:T(8,128)(2,1)S(1)}, bf16[2,16,4096]{2,1,0:T(8,128)(2,1)S(1)}, u32[]{:S(2)}, u32[]{:S(2)}) collective-permute-start(bf16[2,16,4096]{2,1,0:T(8,128)(2,1)S(1)} %get-tuple-element.65), channel_id=1, source_target_pairs={{0,4},{1,7},{2,6},{3,5},{4,0},{5,3},{6,2},{7,1},{8,12},{9,15},{10,... | collective-permute-start | bytes 786440 | tf_op jit(solution)/shard_map/ppermute | solution.py:455
  33.5 11.5 %collective-permute-start.5 = (bf16[2,16,4096]{2,1,0:T(8,128)(2,1)S(1)}, bf16[2,16,4096]{2,1,0:T(8,128)(2,1)S(1)}, u32[]{:S(2)}, u32[]{:S(2)}) collective-permute-start(bf16[2,16,4096]{2,1,0:T(8,128)(2,1)S(1)} %get-tuple-element.64), channel_id=1, source_target_pairs={{0,0},{1,3},{2,2},{3,1},{4,4},{5,7},{6,6},{7,5},{8,8},{9,11},{10,1... | collective-permute-start | bytes 786440 | tf_op jit(solution)/shard_map/ppermute | solution.py:455
  36.7 12.3 %collective-permute-start.14 = (bf16[2,16,2048]{2,1,0:T(8,128)(2,1)S(1)}, bf16[2,16,2048]{2,1,0:T(8,128)(2,1)S(1)}, u32[]{:S(2)}, u32[]{:S(2)}) collective-permute-start(bf16[2,16,2048]{2,1,0:T(8,128)(2,1)S(1)} %get-tuple-element.70), channel_id=1, source_target_pairs={{0,12},{1,15},{2,14},{3,13},{4,8},{5,11},{6,10},{7,9},{8,4},{9,7},... | collective-permute-start | bytes 393224 | tf_op jit(solution)/shard_map/ppermute | solution.py:455
  44.5 9.1 %collective-permute-start.12 = (bf16[2,16,4096]{2,1,0:T(8,128)(2,1)S(1)}, bf16[2,16,4096]{2,1,0:T(8,128)(2,1)S(1)}, u32[]{:S(2)}, u32[]{:S(2)}) collective-permute-start(bf16[2,16,4096]{2,1,0:T(8,128)(2,1)S(1)} %collective-permute-done.7.refs_2_), channel_id=1, source_target_pairs={{0,1},{1,0},{2,3},{3,2},{4,5},{5,4},{6,7},{7,6},{8,9},{9,8},{10,11... | collective-permute-start | bytes 786440 | tf_op jit(solution)/shard_map/ppermute | solution.py:459
  44.5 9.1 %collective-permute-start.11 = (bf16[2,16,4096]{2,1,0:T(8,128)(2,1)S(1)}, bf16[2,16,4096]{2,1,0:T(8,128)(2,1)S(1)}, u32[]{:S(2)}, u32[]{:S(2)}) collective-permute-start(bf16[2,16,4096]{2,1,0:T(8,128)(2,1)S(1)} %collective-permute-done.6.refs_1_), channel_id=1, source_target_pairs={{0,1},{1,0},{2,3},{3,2},{4,5},{5,4},{6,7},{7,6},{8,9},{9,8},{10,11... | collective-permute-start | bytes 786440 | tf_op jit(solution)/shard_map/ppermute | solution.py:459
  45.0 8.6 %collective-permute-start.10 = (bf16[2,16,4096]{2,1,0:T(8,128)(2,1)S(1)}, bf16[2,16,4096]{2,1,0:T(8,128)(2,1)S(1)}, u32[]{:S(2)}, u32[]{:S(2)}) collective-permute-start(bf16[2,16,4096]{2,1,0:T(8,128)(2,1)S(1)} %collective-permute-done.5.refs_0_), channel_id=1, source_target_pairs={{0,1},{1,0},{2,3},{3,2},{4,5},{5,4},{6,7},{7,6},{8,9},{9,8},{10,11... | collective-permute-start | bytes 786440 | tf_op jit(solution)/shard_map/ppermute | solution.py:459
  45.1 7.4 %collective-permute-start.9 = (bf16[2,16,2048]{2,1,0:T(8,128)(2,1)S(1)}, bf16[2,16,2048]{2,1,0:T(8,128)(2,1)S(1)}, u32[]{:S(2)}, u32[]{:S(2)}) collective-permute-start(bf16[2,16,2048]{2,1,0:T(8,128)(2,1)S(1)} %get-tuple-element.69), channel_id=1, source_target_pairs={{0,12},{1,15},{2,14},{3,13},{4,8},{5,11},{6,10},{7,9},{8,4},{9,7},... | collective-permute-start | bytes 393224 | tf_op jit(solution)/shard_map/ppermute | solution.py:455
  49.0 4.5 %collective-permute-start.15 = (bf16[2,16,2048]{2,1,0:T(8,128)(2,1)S(1)}, bf16[2,16,2048]{2,1,0:T(8,128)(2,1)S(1)}, u32[]{:S(2)}, u32[]{:S(2)}) collective-permute-start(bf16[2,16,2048]{2,1,0:T(8,128)(2,1)S(1)} %collective-permute-done.14.refs_3_), channel_id=1, source_target_pairs={{0,1},{1,0},{2,3},{3,2},{4,5},{5,4},{6,7},{7,6},{8,9},{9,8},{10,11... | collective-permute-start | bytes 393224 | tf_op jit(solution)/shard_map/ppermute | solution.py:459
  52.4 3.9 %collective-permute-start.13 = (bf16[2,16,2048]{2,1,0:T(8,128)(2,1)S(1)}, bf16[2,16,2048]{2,1,0:T(8,128)(2,1)S(1)}, u32[]{:S(2)}, u32[]{:S(2)}) collective-permute-start(bf16[2,16,2048]{2,1,0:T(8,128)(2,1)S(1)} %collective-permute-done.9.refs_3_), channel_id=1, source_target_pairs={{0,1},{1,0},{2,3},{3,2},{4,5},{5,4},{6,7},{7,6},{8,9},{9,8},{10,11... | collective-permute-start | bytes 393224 | tf_op jit(solution)/shard_map/ppermute | solution.py:459

commit v4 on v3

--- a/solution.py
+++ b/solution.py
@@ -221,14 +221,15 @@
     score_ref,
     fresh_k_ref,
     fresh_v_ref,
+    turned_ref,
     down_ref,
     up_ref,
-    key_ref,
     value_ref,
     base_in,
     lengths_in,
     fresh_k_in,
     fresh_v_in,
+    key_ref,
     sems,
 ):
     pairs = [
@@ -274,11 +275,10 @@
         lanes = slice(j * HEAD_SIZE, (j + 1) * HEAD_SIZE)
         for p in range(pair_count):
             here = slice(p * block, (p + 1) * block)
-            score_ref[j, here, :] = lax.dot_general(
-                heads_ref[j, here, :].astype(jnp.bfloat16),
-                key_ref[p, :, lanes],
-                (((1,), (1,)), ((), ())),
-                preferred_element_type=jnp.float32,
+            turned = key_ref[p, :, lanes].T
+            turned_ref[j, p] = turned
+            score_ref[j, here, :] = jnp.dot(
+                heads_ref[j, here, :].astype(jnp.bfloat16), turned, preferred_element_type=jnp.float32
             )
         score_ref[j] = jnp.where(valid, score_ref[j] * FACTOR, MASKED)
     for copy in copies[5:]:
@@ -290,7 +290,7 @@
     cached_count = new_key.shape[1] // HEAD_SIZE
     rows = requests * features // (HEAD_SIZE * cached_count)
     places = key_cache.shape[1]
-    held = [adapter_down, adapter_up, key_cache, value_cache]
+    held = [adapter_down, adapter_up, value_cache]
     moved = [base_query, lengths.reshape(1, requests), new_key, new_value]
     return pl.pallas_call(
         prepare_kernel,
@@ -299,23 +299,23 @@
             pltpu.VMEM((cached_count, rows, places), jnp.float32),
             pltpu.VMEM((cached_count, rows, HEAD_SIZE), jnp.float32),
             pltpu.VMEM((cached_count, rows, HEAD_SIZE), jnp.float32),
+            pltpu.VMEM((cached_count, key_cache.shape[0], HEAD_SIZE, places), key_cache.dtype),
         ]
         + [pltpu.VMEM(array.shape, array.dtype) for array in held],
         in_specs=[ANYWHERE] * 8,
         out_specs=[VMEM] * 8,
-        scratch_shapes=[pltpu.VMEM(array.shape, array.dtype) for array in moved]
+        scratch_shapes=[pltpu.VMEM(array.shape, array.dtype) for array in [*moved, key_cache]]
         + [pltpu.SemaphoreType.DMA((8,))],
-        compiler_params=grant(8),
+        compiler_params=grant(12),
         cost_estimate=pl.CostEstimate(
             flops=0, bytes_accessed=4 * key_cache.size + 4 * adapter_up.size, transcendentals=0
         ),
         name="prepare",
-    )(*[in_hbm(array) for array in moved + held])
+    )(*[in_hbm(array) for array in [*moved, adapter_down, adapter_up, key_cache, value_cache]])
 
 
 def attend_kernel(
-    first,
-    counts,
+    parts,
     heads_ref,
     score_ref,
     fresh_k_ref,
@@ -325,10 +325,9 @@
     routing_ref,
     *refs,
 ):
-    count = len(counts)
-    returned = refs[:count]
+    returned = refs[:-6]
     out_hbm, delta_ref, weight_ref, mixed_ref, out_ref, sems = refs[-6:]
-    pair_count, _, _ = key_ref.shape
+    _, pair_count, _, _ = key_ref.shape
     _, rows, _ = heads_ref.shape
     requests = out_hbm.shape[0]
     group_size = rows // requests
@@ -336,13 +335,15 @@
     half = lax.axis_index("tp")
     width = group_size * HEAD_SIZE
     copies = []
-    for k in range(out_ref.shape[0]):
-        j = first + k
+    cached_count = out_ref.shape[0]
+    for j in range(cached_count):
         lanes = slice(j * HEAD_SIZE, (j + 1) * HEAD_SIZE)
-        arrived = jnp.concatenate(
-            [piece[half, :, (j - at) * width : (j - at + 1) * width] for piece, at in zip(returned, counts)],
-            axis=0,
-        )
+        arrived = []
+        for piece in parts:
+            part, at = divmod(j * len(piece), cached_count)
+            at = at // len(piece) * width
+            arrived.append(returned[piece[part]][half, :, at : at + width])
+        arrived = jnp.concatenate(arrived, axis=0)
         delta = jnp.dot(routing_ref[...], arrived, preferred_element_type=jnp.float32)
         for h in range(group_size):
             delta_ref[pl.ds(h, requests, stride=group_size), :] = delta[
@@ -350,11 +351,8 @@
             ]
         for p in range(pair_count):
             here = slice(p * block, (p + 1) * block)
-            weight_ref[here, :] = lax.dot_general(
-                delta_ref[here, :].astype(jnp.bfloat16),
-                key_ref[p, :, lanes],
-                (((1,), (1,)), ((), ())),
-                preferred_element_type=jnp.float32,
+            weight_ref[here, :] = jnp.dot(
+                delta_ref[here, :].astype(jnp.bfloat16), key_ref[j, p], preferred_element_type=jnp.float32
             )
         scores = score_ref[j] + weight_ref[...] * FACTOR
         own = (heads_ref[j] + delta_ref[...]) * fresh_k_ref[j]
@@ -374,11 +372,11 @@
             )
         mixed_ref[...] = (mixed_ref[...] + own_b * fresh_v_ref[j]) / totals
         for h in range(group_size):
-            out_ref[k, :, h * HEAD_SIZE : (h + 1) * HEAD_SIZE] = mixed_ref[
+            out_ref[j, :, h * HEAD_SIZE : (h + 1) * HEAD_SIZE] = mixed_ref[
                 pl.ds(h, requests, stride=group_size), :
             ].astype(jnp.bfloat16)
         copy = pltpu.make_async_copy(
-            out_ref.at[k], out_hbm.at[:, pl.ds(j * width, width)], sems.at[k]
+            out_ref.at[j], out_hbm.at[:, pl.ds(j * width, width)], sems.at[j]
         )
         copy.start()
         copies.append(copy)
@@ -386,31 +384,29 @@
         copy.wait()
 
 
-def attend(held, routing_b, returned, first, span, counts, out=None):
+def attend(held, routing_b, pieces):
     cached_count, rows, _ = held[0].shape
     requests = routing_b.shape[0]
     width = rows // requests * HEAD_SIZE
-    operands = [*held, routing_b, *returned]
-    aliases = {}
-    if out is not None:
-        aliases = {len(operands): 0}
-        operands.append(out)
+    parts, returned = [], []
+    for piece in pieces:
+        parts.append(list(range(len(returned), len(returned) + len(piece))))
+        returned.extend(piece)
     return pl.pallas_call(
-        functools.partial(attend_kernel, first, counts),
+        functools.partial(attend_kernel, parts),
         out_shape=jax.ShapeDtypeStruct((requests, cached_count * width), jnp.bfloat16),
-        in_specs=[VMEM] * (len(held) + 1 + len(returned)) + [ANYWHERE] * len(aliases),
+        in_specs=[VMEM] * (len(held) + 1 + len(returned)),
         out_specs=ANYWHERE,
-        input_output_aliases=aliases,
         scratch_shapes=[
             pltpu.VMEM((rows, HEAD_SIZE), jnp.float32),
             pltpu.VMEM((rows, held[1].shape[2]), jnp.float32),
             pltpu.VMEM((rows, HEAD_SIZE), jnp.float32),
-            pltpu.VMEM((span, requests, width), jnp.bfloat16),
-            pltpu.SemaphoreType.DMA((span,)),
+            pltpu.VMEM((cached_count, requests, width), jnp.bfloat16),
+            pltpu.SemaphoreType.DMA((cached_count,)),
         ],
         compiler_params=grant(8),
         name="attend",
-    )(*operands)
+    )(*held, routing_b, *returned)
 
 
 def after(arrays, *tokens):
@@ -464,7 +460,7 @@
     factors = [adapter_down, swap(adapter_down), adapter_up, swap(adapter_up)]
     cached_len, features = key_cache.shape[1:]
     pairs = (request_rows // 2, 2 * cached_len, features)
-    *held, factors[0], factors[2], key_cache, value_cache = prepare(
+    *held, factors[0], factors[2], value_cache = prepare(
         *after(
             [
                 base_query,
@@ -479,7 +475,7 @@
             routing_b,
         )
     )
-    held = [*held, key_cache, value_cache]
+    held = [*held, value_cache]
     *far, last = list(range(group_count // 2, group_count))
     near = list(range(group_count // 2))
     ready = after([place, spread], factors[1], factors[3])
@@ -493,15 +489,9 @@
     final = [move(last, rows) for rows in final]
     whole = [returned[g] for g in range(last)]
     others = [swap(rows) for rows in whole]
-    cached_count = features // HEAD_SIZE
-    span = cached_count // len(final)
-    out = None
-    for k, rows in enumerate(final):
-        first = k * span
-        pieces = [*whole, rows, *others, swap(rows)]
-        counts = [*[0] * last, first] * 2
-        out = attend(held, routing_b, pieces, first, span, counts, out)
-    return out
+    mine = [[rows] for rows in whole] + [final]
+    theirs = [[rows] for rows in others] + [[swap(rows) for rows in final]]
+    return attend(held, routing_b, mine + theirs)
 
 
 def solution(mesh):

time: 59.3 us -> 58 us (0.978)
  the two profiles are of different devices: /device:TPU:1 before, /device:TPU:19 now
where the time goes in v4:
time: 58 us; the launch traced here: 57.8 us
  waiting for transfers between devices  29.1 us (50%)
  starting transfers between devices  15.2 us (26%)
  Pallas kernels  13.4 us (23%)
    ppermute x9, waiting for transfers between devices, move(): parts.append(lax.ppermute(part, ('pool', 'tp'), pairs))  26.4 us
    ppermute x9, starting transfers between devices, move(): parts.append(lax.ppermute(part, ('pool', 'tp'), pairs))  14 us
    pallas_call x1, Pallas kernels, prepare(): pl.pallas_call(prepare_kernel, out_shape=[pltpu.VMEM((cached_count, rows,...  4.36 us
    pallas_call x1, Pallas kernels, attend(): pl.pallas_call(functools.partial(attend_kernel, parts), out_shape=jax.Sha...  3.82 us
    pallas_call x3, Pallas kernels, serve(): pl.pallas_call(functools.partial(serve_kernel, len(rows), parts), out_sha...  3.33 us
    ppermute x7, waiting for transfers between devices, swap(): return lax.ppermute(array, 'tp', [(0, 1), (1, 0)])  2.7 us
    pallas_call x1, Pallas kernels, pack(): pl.pallas_call(functools.partial(pack_kernel, pool_count, tp_count, capac...  1.57 us
    ppermute x7, starting transfers between devices, swap(): return lax.ppermute(array, 'tp', [(0, 1), (1, 0)])  1.2 us
  transfers between devices with their start and end apart: 16, of which 8 were waited for; matrix products, arithmetic and copies ran while one was open for 0% of the time, Pallas kernels for 16%

profile of v4, /device:TPU:19, one launch (start us, length us, event | category | flops | bytes accessed | tf_op | source)
XLA Modules:
  0.0 57.8 jit_solution(14422969667863660245)
XLA Ops:
  0.0 0.7 %collective-permute-start = (bf16[2,64,4096]{2,1,0:T(8,128)(2,1)}, bf16[2,64,4096]{2,1,0:T(8,128)(2,1)S(1)}, u32[]{:S(2)}, u32[]{:S(2)}) collective-permute-start(bf16[2,64,4096]{2,1,0:T(8,128)(2,1)} %bitcast.8), channel_id=1, source_target_pairs={{0,1},{1,0},{2,3},{3,2},{4,5},{5,4},{6,7},{7,6},{8,9},{9,8},{10,11... | collective-permute-start | bytes 3145736 | tf_op jit(solution)/shard_map/ppermute | solution.py:455
  0.7 0.0 collective-permute-start.1
  0.7 1.6 %pack.1 = (bf16[16,8320]{1,0:T(8,128)(2,1)S(1)}, bf16[16,8320]{1,0:T(8,128)(2,1)S(1)}, bf16[64,128]{1,0:T(8,128)(2,1)S(1)}, s32[2,64]{1,0:T(2,128)S(1)}, bf16[64,8192]{1,0:T(8,128)(2,1)S(1)}) custom-call(s32[1,64]{1,0:T(1,128)} %bitcast.10, s32[1,16]{1,0:T(1,128)} %bitcast.11, bf16[64,8192]{1,0:T(8,128)(2,1)} %hidden_hbm.1), custom_call_target="tpu_custom_call" | custom-call | tf_op jit(solution)/shard_map/pack/pallas_call | solution.py:118
  2.3 1.1 %collective-permute-start.4 = (bf16[16,8320]{1,0:T(8,128)(2,1)S(1)}, bf16[16,8320]{1,0:T(8,128)(2,1)S(1)}, u32[]{:S(2)}, u32[]{:S(2)}) collective-permute-start(bf16[16,8320]{1,0:T(8,128)(2,1)S(1)} %get-tuple-element.59), channel_id=1, source_target_pairs={{0,8},{1,11},{2,10},{3,9},{4,12},{5,15},{6,14},{7,13},{8,0},{9,3},... | collective-permute-start | bytes 798728 | tf_op jit(solution)/shard_map/ppermute | solution.py:451
  3.3 0.0 collective-permute-done.refs_2_.refs_3_
  3.3 1.3 %collective-permute-done.1.refs_4_.refs_5_ = bf16[2,64,4096]{2,1,0:T(8,128)(2,1)S(1)} collective-permute-done((bf16[2,64,4096]{2,1,0:T(8,128)(2,1)}, bf16[2,64,4096]{2,1,0:T(8,128)(2,1)S(1)}, u32[]{:S(2)}, u32[]{:S(2)}) %collective-permute-start.1) | collective-permute-done | bytes 1048608 | tf_op jit(solution)/shard_map/ppermute | solution.py:455
  4.7 0.3 pack_near.1
  5.0 3.2 %collective-permute-start.2 = (bf16[16,8320]{1,0:T(8,128)(2,1)S(1)}, bf16[16,8320]{1,0:T(8,128)(2,1)S(1)}, u32[]{:S(2)}, u32[]{:S(2)}) collective-permute-start(bf16[16,8320]{1,0:T(8,128)(2,1)S(1)} %get-tuple-element.57), channel_id=1, source_target_pairs={{0,0},{1,3},{2,2},{3,1},{4,4},{5,7},{6,6},{7,5},{8,8},{9,11},{10,1... | collective-permute-start | bytes 798728 | tf_op jit(solution)/shard_map/ppermute | solution.py:451
  8.1 1.3 %collective-permute-start.3 = (bf16[16,8320]{1,0:T(8,128)(2,1)S(1)}, bf16[16,8320]{1,0:T(8,128)(2,1)S(1)}, u32[]{:S(2)}, u32[]{:S(2)}) collective-permute-start(bf16[16,8320]{1,0:T(8,128)(2,1)S(1)} %get-tuple-element.58), channel_id=1, source_target_pairs={{0,4},{1,7},{2,6},{3,5},{4,0},{5,3},{6,2},{7,1},{8,12},{9,15},{10,... | collective-permute-start | bytes 798728 | tf_op jit(solution)/shard_map/ppermute | solution.py:451
  9.4 0.0 collective-permute-start.8
  9.4 4.4 %prepare.1 = (f32[4,512,128]{2,1,0:T(8,128)S(1)}, f32[4,512,128]{2,1,0:T(8,128)S(1)}, f32[4,512,128]{2,1,0:T(8,128)S(1)}, f32[4,512,128]{2,1,0:T(8,128)S(1)}, bf...) custom-call(bf16[64,4096]{1,0:T(8,128)(2,1)} %base_hbm, ...), custom_call_target="tpu_custom_call" | custom-call | bytes 10485760 | tf_op jit(solution)/shard_map/prepare/pallas_call | solution.py:295
  13.8 1.5 %collective-permute-done.4.refs_0_ = bf16[16,8320]{1,0:T(8,128)(2,1)S(1)} collective-permute-done((bf16[16,8320]{1,0:T(8,128)(2,1)S(1)}, bf16[16,8320]{1,0:T(8,128)(2,1)S(1)}, u32[]{:S(2)}, u32[]{:S(2)}) %collective-permute-start.4) | collective-permute-done | bytes 266272 | tf_op jit(solution)/shard_map/ppermute | solution.py:451
  15.3 1.1 %serve.3 = bf16[2,16,4096]{2,1,0:T(8,128)(2,1)S(1)} custom-call(bf16[16,8320]{1,0:T(8,128)(2,1)S(1)} %collective-permute-done.4.refs_0_, bf16[2,64,4096]{2,1,0:T(8,128)(2,1)S(1)} %get-tuple-element.60.refs_1_.refs_2_, bf16[2,64,4096]{2,1,0:T(8,128)(2,1)S(1)} %collective-permute-done.refs_2_.refs_3_, ...), custom_call_target="tpu_custom_call" | custom-call | tf_op jit(solution)/shard_map/serve/pallas_call | solution.py:199
  16.4 0.0 collective-permute-done.2.refs_0_
  16.4 9.0 %collective-permute-done.3.refs_1_ = bf16[16,8320]{1,0:T(8,128)(2,1)S(1)} collective-permute-done((bf16[16,8320]{1,0:T(8,128)(2,1)S(1)}, bf16[16,8320]{1,0:T(8,128)(2,1)S(1)}, u32[]{:S(2)}, u32[]{:S(2)}) %collective-permute-start.3) | collective-permute-done | bytes 266272 | tf_op jit(solution)/shard_map/ppermute | solution.py:451
  25.4 1.1 %serve.4 = (bf16[2,16,4096]{2,1,0:T(8,128)(2,1)S(1)}, bf16[2,16,4096]{2,1,0:T(8,128)(2,1)S(1)}) custom-call(bf16[16,8320]{1,0:T(8,128)(2,1)S(1)} %collective-permute-done.2.refs_0_, bf16[16,8320]{1,0:T(8,128)(2,1)S(1)} %collective-permute-done.3.refs_1_, bf16[2,64,4096]{2,1,0:T(8,128)(2,1)S(1)} %get-tuple-element.60.refs_1_.refs_2_, ...), custom_call_target="tpu_custom_call" | custom-call | tf_op jit(solution)/shard_map/serve/pallas_call | solution.py:199
  26.5 1.0 %collective-permute-start.7 = (bf16[2,16,4096]{2,1,0:T(8,128)(2,1)S(1)}, bf16[2,16,4096]{2,1,0:T(8,128)(2,1)S(1)}, u32[]{:S(2)}, u32[]{:S(2)}) collective-permute-start(bf16[2,16,4096]{2,1,0:T(8,128)(2,1)S(1)} %serve.3), channel_id=1, source_target_pairs={{0,8},{1,11},{2,10},{3,9},{4,12},{5,15},{6,14},{7,13},{8,0},{9,3},... | collective-permute-start | bytes 786440 | tf_op jit(solution)/shard_map/ppermute | solution.py:451
  27.5 2.0 %collective-permute-start.6 = (bf16[2,16,4096]{2,1,0:T(8,128)(2,1)S(1)}, bf16[2,16,4096]{2,1,0:T(8,128)(2,1)S(1)}, u32[]{:S(2)}, u32[]{:S(2)}) collective-permute-start(bf16[2,16,4096]{2,1,0:T(8,128)(2,1)S(1)} %get-tuple-element.65), channel_id=1, source_target_pairs={{0,4},{1,7},{2,6},{3,5},{4,0},{5,3},{6,2},{7,1},{8,12},{9,15},{10,... | collective-permute-start | bytes 786440 | tf_op jit(solution)/shard_map/ppermute | solution.py:451
  29.5 3.1 %collective-permute-start.5 = (bf16[2,16,4096]{2,1,0:T(8,128)(2,1)S(1)}, bf16[2,16,4096]{2,1,0:T(8,128)(2,1)S(1)}, u32[]{:S(2)}, u32[]{:S(2)}) collective-permute-start(bf16[2,16,4096]{2,1,0:T(8,128)(2,1)S(1)} %get-tuple-element.64), channel_id=1, source_target_pairs={{0,0},{1,3},{2,2},{3,1},{4,4},{5,7},{6,6},{7,5},{8,8},{9,11},{10,1... | collective-permute-start | bytes 786440 | tf_op jit(solution)/shard_map/ppermute | solution.py:451
  32.6 0.0 collective-permute-done.8.refs_0_
  32.6 1.1 %serve.5 = (bf16[2,16,2048]{2,1,0:T(8,128)(2,1)S(1)}, bf16[2,16,2048]{2,1,0:T(8,128)(2,1)S(1)}) custom-call(bf16[16,8320]{1,0:T(8,128)(2,1)S(1)} %collective-permute-done.8.refs_0_, bf16[2,64,4096]{2,1,0:T(8,128)(2,1)S(1)} %get-tuple-element.60.refs_1_.refs_2_, bf16[2,64,4096]{2,1,0:T(8,128)(2,1)S(1)} %collective-permute-done.refs_2_.refs_3_, ...), custom_call_target="tpu_custom_call" | custom-call | tf_op jit(solution)/shard_map/serve/pallas_call | solution.py:199
  33.7 1.1 %collective-permute-start.9 = (bf16[2,16,2048]{2,1,0:T(8,128)(2,1)S(1)}, bf16[2,16,2048]{2,1,0:T(8,128)(2,1)S(1)}, u32[]{:S(2)}, u32[]{:S(2)}) collective-permute-start(bf16[2,16,2048]{2,1,0:T(8,128)(2,1)S(1)} %get-tuple-element.69), channel_id=1, source_target_pairs={{0,12},{1,15},{2,14},{3,13},{4,8},{5,11},{6,10},{7,9},{8,4},{9,7},... | collective-permute-start | bytes 393224 | tf_op jit(solution)/shard_map/ppermute | solution.py:451
  34.8 1.3 %collective-permute-start.10 = (bf16[2,16,2048]{2,1,0:T(8,128)(2,1)S(1)}, bf16[2,16,2048]{2,1,0:T(8,128)(2,1)S(1)}, u32[]{:S(2)}, u32[]{:S(2)}) collective-permute-start(bf16[2,16,2048]{2,1,0:T(8,128)(2,1)S(1)} %get-tuple-element.70), channel_id=1, source_target_pairs={{0,12},{1,15},{2,14},{3,13},{4,8},{5,11},{6,10},{7,9},{8,4},{9,7},... | collective-permute-start | bytes 393224 | tf_op jit(solution)/shard_map/ppermute | solution.py:451
  36.1 4.6 %collective-permute-done.7.refs_2_ = bf16[2,16,4096]{2,1,0:T(8,128)(2,1)S(1)} collective-permute-done((bf16[2,16,4096]{2,1,0:T(8,128)(2,1)S(1)}, bf16[2,16,4096]{2,1,0:T(8,128)(2,1)S(1)}, u32[]{:S(2)}, u32[]{:S(2)}) %collective-permute-start.7) | collective-permute-done | bytes 262176 | tf_op jit(solution)/shard_map/ppermute | solution.py:451
  40.7 0.0 collective-permute-start.13
  40.7 0.8 %collective-permute-done.6.refs_1_ = bf16[2,16,4096]{2,1,0:T(8,128)(2,1)S(1)} collective-permute-done((bf16[2,16,4096]{2,1,0:T(8,128)(2,1)S(1)}, bf16[2,16,4096]{2,1,0:T(8,128)(2,1)S(1)}, u32[]{:S(2)}, u32[]{:S(2)}) %collective-permute-start.6) | collective-permute-done | bytes 262176 | tf_op jit(solution)/shard_map/ppermute | solution.py:451
  41.6 0.0 collective-permute-start.12
  41.6 0.0 collective-permute-done.5.refs_0_
  41.6 0.5 collective-permute-start.11
  42.1 7.8 %collective-permute-done.9.refs_3_ = bf16[2,16,2048]{2,1,0:T(8,128)(2,1)S(1)} collective-permute-done((bf16[2,16,2048]{2,1,0:T(8,128)(2,1)S(1)}, bf16[2,16,2048]{2,1,0:T(8,128)(2,1)S(1)}, u32[]{:S(2)}, u32[]{:S(2)}) %collective-permute-start.9) | collective-permute-done | bytes 131104 | tf_op jit(solution)/shard_map/ppermute | solution.py:451
  49.9 0.0 collective-permute-start.14
  49.9 2.7 %collective-permute-done.10.refs_4_ = bf16[2,16,2048]{2,1,0:T(8,128)(2,1)S(1)} collective-permute-done((bf16[2,16,2048]{2,1,0:T(8,128)(2,1)S(1)}, bf16[2,16,2048]{2,1,0:T(8,128)(2,1)S(1)}, u32[]{:S(2)}, u32[]{:S(2)}) %collective-permute-start.10) | collective-permute-done | bytes 131104 | tf_op jit(solution)/shard_map/ppermute | solution.py:451
  52.6 0.0 collective-permute-start.15
  52.6 0.0 collective-permute-done.14.refs_8_
  52.6 1.3 %collective-permute-done.15.refs_9_ = bf16[2,16,2048]{2,1,0:T(8,128)(2,1)S(1)} collective-permute-done((bf16[2,16,2048]{2,1,0:T(8,128)(2,1)S(1)}, bf16[2,16,2048]{2,1,0:T(8,128)(2,1)S(1)}, u32[]{:S(2)}, u32[]{:S(2)}) %collective-permute-start.15) | collective-permute-done | bytes 131104 | tf_op jit(solution)/shard_map/ppermute | solution.py:455
  54.0 0.0 collective-permute-done.13.refs_7_
  54.0 0.0 collective-permute-done.12.refs_6_
  54.0 0.0 collective-permute-done.11.refs_5_
  54.0 3.8 %attend.1 = bf16[64,4096]{1,0:T(8,128)(2,1)} custom-call(f32[4,512,128]{2,1,0:T(8,128)S(1)} %get-tuple-element.47.heads_ref, f32[4,512,128]{2,1,0:T(8,128)S(1)} %get-tuple-element.48.score_ref, f32[4,512,128]{2,1,0:T(8,128)S(1)} %get-tuple-element.49.fresh_k_ref, f32[4,512,128]{2,1,0:T(8,128)S(1)} %get-tuple-element.50.fresh_v_ref, ...), custom_call_target="tpu_custom_call" | custom-call | tf_op jit(solution)/shard_map/attend/pallas_call | solution.py:395
Async XLA Ops:
  0.0 3.3 %collective-permute-start = (bf16[2,64,4096]{2,1,0:T(8,128)(2,1)}, bf16[2,64,4096]{2,1,0:T(8,128)(2,1)S(1)}, u32[]{:S(2)}, u32[]{:S(2)}) collective-permute-start(bf16[2,64,4096]{2,1,0:T(8,128)(2,1)} %bitcast.8), channel_id=1, source_target_pairs={{0,1},{1,0},{2,3},{3,2},{4,5},{5,4},{6,7},{7,6},{8,9},{9,8},{10,11... | collective-permute-start | bytes 3145736 | tf_op jit(solution)/shard_map/ppermute | solution.py:455
  0.7 4.0 %collective-permute-start.1 = (bf16[2,64,4096]{2,1,0:T(8,128)(2,1)}, bf16[2,64,4096]{2,1,0:T(8,128)(2,1)S(1)}, u32[]{:S(2)}, u32[]{:S(2)}) collective-permute-start(bf16[2,64,4096]{2,1,0:T(8,128)(2,1)} %up_hbm), channel_id=1, source_target_pairs={{0,1},{1,0},{2,3},{3,2},{4,5},{5,4},{6,7},{7,6},{8,9},{9,8},{10,11... | collective-permute-start | bytes 3145736 | tf_op jit(solution)/shard_map/ppermute | solution.py:455
  2.3 13.0 %collective-permute-start.4 = (bf16[16,8320]{1,0:T(8,128)(2,1)S(1)}, bf16[16,8320]{1,0:T(8,128)(2,1)S(1)}, u32[]{:S(2)}, u32[]{:S(2)}) collective-permute-start(bf16[16,8320]{1,0:T(8,128)(2,1)S(1)} %get-tuple-element.59), channel_id=1, source_target_pairs={{0,8},{1,11},{2,10},{3,9},{4,12},{5,15},{6,14},{7,13},{8,0},{9,3},... | collective-permute-start | bytes 798728 | tf_op jit(solution)/shard_map/ppermute | solution.py:451
  5.0 11.4 %collective-permute-start.2 = (bf16[16,8320]{1,0:T(8,128)(2,1)S(1)}, bf16[16,8320]{1,0:T(8,128)(2,1)S(1)}, u32[]{:S(2)}, u32[]{:S(2)}) collective-permute-start(bf16[16,8320]{1,0:T(8,128)(2,1)S(1)} %get-tuple-element.57), channel_id=1, source_target_pairs={{0,0},{1,3},{2,2},{3,1},{4,4},{5,7},{6,6},{7,5},{8,8},{9,11},{10,1... | collective-permute-start | bytes 798728 | tf_op jit(solution)/shard_map/ppermute | solution.py:451
  8.1 17.2 %collective-permute-start.3 = (bf16[16,8320]{1,0:T(8,128)(2,1)S(1)}, bf16[16,8320]{1,0:T(8,128)(2,1)S(1)}, u32[]{:S(2)}, u32[]{:S(2)}) collective-permute-start(bf16[16,8320]{1,0:T(8,128)(2,1)S(1)} %get-tuple-element.58), channel_id=1, source_target_pairs={{0,4},{1,7},{2,6},{3,5},{4,0},{5,3},{6,2},{7,1},{8,12},{9,15},{10,... | collective-permute-start | bytes 798728 | tf_op jit(solution)/shard_map/ppermute | solution.py:451
  9.4 23.2 %collective-permute-start.8 = (bf16[16,8320]{1,0:T(8,128)(2,1)S(1)}, bf16[16,8320]{1,0:T(8,128)(2,1)S(1)}, u32[]{:S(2)}, u32[]{:S(2)}) collective-permute-start(bf16[16,8320]{1,0:T(8,128)(2,1)S(1)} %get-tuple-element.67), channel_id=1, source_target_pairs={{0,12},{1,15},{2,14},{3,13},{4,8},{5,11},{6,10},{7,9},{8,4},{9,7},... | collective-permute-start | bytes 798728 | tf_op jit(solution)/shard_map/ppermute | solution.py:451
  26.5 14.2 %collective-permute-start.7 = (bf16[2,16,4096]{2,1,0:T(8,128)(2,1)S(1)}, bf16[2,16,4096]{2,1,0:T(8,128)(2,1)S(1)}, u32[]{:S(2)}, u32[]{:S(2)}) collective-permute-start(bf16[2,16,4096]{2,1,0:T(8,128)(2,1)S(1)} %serve.3), channel_id=1, source_target_pairs={{0,8},{1,11},{2,10},{3,9},{4,12},{5,15},{6,14},{7,13},{8,0},{9,3},... | collective-permute-start | bytes 786440 | tf_op jit(solution)/shard_map/ppermute | solution.py:451
  27.5 14.1 %collective-permute-start.6 = (bf16[2,16,4096]{2,1,0:T(8,128)(2,1)S(1)}, bf16[2,16,4096]{2,1,0:T(8,128)(2,1)S(1)}, u32[]{:S(2)}, u32[]{:S(2)}) collective-permute-start(bf16[2,16,4096]{2,1,0:T(8,128)(2,1)S(1)} %get-tuple-element.65), channel_id=1, source_target_pairs={{0,4},{1,7},{2,6},{3,5},{4,0},{5,3},{6,2},{7,1},{8,12},{9,15},{10,... | collective-permute-start | bytes 786440 | tf_op jit(solution)/shard_map/ppermute | solution.py:451
  29.5 12.1 %collective-permute-start.5 = (bf16[2,16,4096]{2,1,0:T(8,128)(2,1)S(1)}, bf16[2,16,4096]{2,1,0:T(8,128)(2,1)S(1)}, u32[]{:S(2)}, u32[]{:S(2)}) collective-permute-start(bf16[2,16,4096]{2,1,0:T(8,128)(2,1)S(1)} %get-tuple-element.64), channel_id=1, source_target_pairs={{0,0},{1,3},{2,2},{3,1},{4,4},{5,7},{6,6},{7,5},{8,8},{9,11},{10,1... | collective-permute-start | bytes 786440 | tf_op jit(solution)/shard_map/ppermute | solution.py:451
  33.7 16.2 %collective-permute-start.9 = (bf16[2,16,2048]{2,1,0:T(8,128)(2,1)S(1)}, bf16[2,16,2048]{2,1,0:T(8,128)(2,1)S(1)}, u32[]{:S(2)}, u32[]{:S(2)}) collective-permute-start(bf16[2,16,2048]{2,1,0:T(8,128)(2,1)S(1)} %get-tuple-element.69), channel_id=1, source_target_pairs={{0,12},{1,15},{2,14},{3,13},{4,8},{5,11},{6,10},{7,9},{8,4},{9,7},... | collective-permute-start | bytes 393224 | tf_op jit(solution)/shard_map/ppermute | solution.py:451
  34.8 17.8 %collective-permute-start.10 = (bf16[2,16,2048]{2,1,0:T(8,128)(2,1)S(1)}, bf16[2,16,2048]{2,1,0:T(8,128)(2,1)S(1)}, u32[]{:S(2)}, u32[]{:S(2)}) collective-permute-start(bf16[2,16,2048]{2,1,0:T(8,128)(2,1)S(1)} %get-tuple-element.70), channel_id=1, source_target_pairs={{0,12},{1,15},{2,14},{3,13},{4,8},{5,11},{6,10},{7,9},{8,4},{9,7},... | collective-permute-start | bytes 393224 | tf_op jit(solution)/shard_map/ppermute | solution.py:451
  40.7 13.2 %collective-permute-start.13 = (bf16[2,16,4096]{2,1,0:T(8,128)(2,1)S(1)}, bf16[2,16,4096]{2,1,0:T(8,128)(2,1)S(1)}, u32[]{:S(2)}, u32[]{:S(2)}) collective-permute-start(bf16[2,16,4096]{2,1,0:T(8,128)(2,1)S(1)} %collective-permute-done.7.refs_2_), channel_id=1, source_target_pairs={{0,1},{1,0},{2,3},{3,2},{4,5},{5,4},{6,7},{7,6},{8,9},{9,8},{10,11... | collective-permute-start | bytes 786440 | tf_op jit(solution)/shard_map/ppermute | solution.py:455
  41.6 12.4 %collective-permute-start.12 = (bf16[2,16,4096]{2,1,0:T(8,128)(2,1)S(1)}, bf16[2,16,4096]{2,1,0:T(8,128)(2,1)S(1)}, u32[]{:S(2)}, u32[]{:S(2)}) collective-permute-start(bf16[2,16,4096]{2,1,0:T(8,128)(2,1)S(1)} %collective-permute-done.6.refs_1_), channel_id=1, source_target_pairs={{0,1},{1,0},{2,3},{3,2},{4,5},{5,4},{6,7},{7,6},{8,9},{9,8},{10,11... | collective-permute-start | bytes 786440 | tf_op jit(solution)/shard_map/ppermute | solution.py:455
  41.6 12.4 %collective-permute-start.11 = (bf16[2,16,4096]{2,1,0:T(8,128)(2,1)S(1)}, bf16[2,16,4096]{2,1,0:T(8,128)(2,1)S(1)}, u32[]{:S(2)}, u32[]{:S(2)}) collective-permute-start(bf16[2,16,4096]{2,1,0:T(8,128)(2,1)S(1)} %collective-permute-done.5.refs_0_), channel_id=1, source_target_pairs={{0,1},{1,0},{2,3},{3,2},{4,5},{5,4},{6,7},{7,6},{8,9},{9,8},{10,11... | collective-permute-start | bytes 786440 | tf_op jit(solution)/shard_map/ppermute | solution.py:455
  49.9 2.7 %collective-permute-start.14 = (bf16[2,16,2048]{2,1,0:T(8,128)(2,1)S(1)}, bf16[2,16,2048]{2,1,0:T(8,128)(2,1)S(1)}, u32[]{:S(2)}, u32[]{:S(2)}) collective-permute-start(bf16[2,16,2048]{2,1,0:T(8,128)(2,1)S(1)} %collective-permute-done.9.refs_3_), channel_id=1, source_target_pairs={{0,1},{1,0},{2,3},{3,2},{4,5},{5,4},{6,7},{7,6},{8,9},{9,8},{10,11... | collective-permute-start | bytes 393224 | tf_op jit(solution)/shard_map/ppermute | solution.py:455
  52.6 1.3 %collective-permute-start.15 = (bf16[2,16,2048]{2,1,0:T(8,128)(2,1)S(1)}, bf16[2,16,2048]{2,1,0:T(8,128)(2,1)S(1)}, u32[]{:S(2)}, u32[]{:S(2)}) collective-permute-start(bf16[2,16,2048]{2,1,0:T(8,128)(2,1)S(1)} %collective-permute-done.10.refs_4_), channel_id=1, source_target_pairs={{0,1},{1,0},{2,3},{3,2},{4,5},{5,4},{6,7},{7,6},{8,9},{9,8},{10,11... | collective-permute-start | bytes 393224 | tf_op jit(solution)/shard_map/ppermute | solution.py:455

commit v5 on v4

--- a/solution.py
+++ b/solution.py
@@ -336,8 +336,8 @@
     width = group_size * HEAD_SIZE
     copies = []
     cached_count = out_ref.shape[0]
-    for j in range(cached_count):
-        lanes = slice(j * HEAD_SIZE, (j + 1) * HEAD_SIZE)
+
+    def unpack(j):
         arrived = []
         for piece in parts:
             part, at = divmod(j * len(piece), cached_count)
@@ -346,40 +346,57 @@
         arrived = jnp.concatenate(arrived, axis=0)
         delta = jnp.dot(routing_ref[...], arrived, preferred_element_type=jnp.float32)
         for h in range(group_size):
-            delta_ref[pl.ds(h, requests, stride=group_size), :] = delta[
+            delta_ref[j, pl.ds(h, requests, stride=group_size), :] = delta[
                 :, h * HEAD_SIZE : (h + 1) * HEAD_SIZE
             ]
+
+    def score(j):
         for p in range(pair_count):
             here = slice(p * block, (p + 1) * block)
-            weight_ref[here, :] = jnp.dot(
-                delta_ref[here, :].astype(jnp.bfloat16), key_ref[j, p], preferred_element_type=jnp.float32
+            weight_ref[j, here, :] = jnp.dot(
+                delta_ref[j, here, :].astype(jnp.bfloat16), key_ref[j, p], preferred_element_type=jnp.float32
             )
-        scores = score_ref[j] + weight_ref[...] * FACTOR
-        own = (heads_ref[j] + delta_ref[...]) * fresh_k_ref[j]
+
+    def weigh(j):
+        scores = score_ref[j] + weight_ref[j] * FACTOR
+        own = (heads_ref[j] + delta_ref[j]) * fresh_k_ref[j]
         own = jnp.sum(own, axis=1, keepdims=True) * FACTOR
         highest = jnp.maximum(jnp.max(scores, axis=1, keepdims=True), own)
         weights = jnp.exp(scores - highest)
         own_weight = jnp.exp(own - highest)
         totals = jnp.sum(weights, axis=1, keepdims=True) + own_weight
-        weight_ref[...] = weights
+        weight_ref[j] = weights
         own_b = own_weight.astype(jnp.bfloat16).astype(jnp.float32)
+        delta_ref[j] = own_b * fresh_v_ref[j]
+        return totals
+
+    def mix(j, totals):
+        lanes = slice(j * HEAD_SIZE, (j + 1) * HEAD_SIZE)
         for p in range(pair_count):
             here = slice(p * block, (p + 1) * block)
-            mixed_ref[here, :] = jnp.dot(
-                weight_ref[here, :].astype(jnp.bfloat16),
+            mixed_ref[j, here, :] = jnp.dot(
+                weight_ref[j, here, :].astype(jnp.bfloat16),
                 value_ref[p, :, lanes],
                 preferred_element_type=jnp.float32,
             )
-        mixed_ref[...] = (mixed_ref[...] + own_b * fresh_v_ref[j]) / totals
+        mixed_ref[j] = (mixed_ref[j] + delta_ref[j]) / totals
         for h in range(group_size):
             out_ref[j, :, h * HEAD_SIZE : (h + 1) * HEAD_SIZE] = mixed_ref[
-                pl.ds(h, requests, stride=group_size), :
+                j, pl.ds(h, requests, stride=group_size), :
             ].astype(jnp.bfloat16)
         copy = pltpu.make_async_copy(
             out_ref.at[j], out_hbm.at[:, pl.ds(j * width, width)], sems.at[j]
         )
         copy.start()
         copies.append(copy)
+
+    for j in range(cached_count):
+        unpack(j)
+    for j in range(cached_count):
+        score(j)
+    totals = [weigh(j) for j in range(cached_count)]
+    for j in range(cached_count):
+        mix(j, totals[j])
     for copy in copies:
         copy.wait()
 
@@ -398,9 +415,9 @@
         in_specs=[VMEM] * (len(held) + 1 + len(returned)),
         out_specs=ANYWHERE,
         scratch_shapes=[
-            pltpu.VMEM((rows, HEAD_SIZE), jnp.float32),
-            pltpu.VMEM((rows, held[1].shape[2]), jnp.float32),
-            pltpu.VMEM((rows, HEAD_SIZE), jnp.float32),
+            pltpu.VMEM((cached_count, rows, HEAD_SIZE), jnp.float32),
+            pltpu.VMEM((cached_count, rows, held[1].shape[2]), jnp.float32),
+            pltpu.VMEM((cached_count, rows, HEAD_SIZE), jnp.float32),
             pltpu.VMEM((cached_count, requests, width), jnp.bfloat16),
             pltpu.SemaphoreType.DMA((cached_count,)),
         ],

time: 58 us -> 57.5 us (level)
  transfers between devices with their start and end apart: 16 -> 16, of which waited for: 8 -> 8; matrix products, arithmetic and copies ran while one was open for 0% -> 0% of each run, Pallas kernels for 16% -> 17%
where the time goes in v5:
time: 57.5 us; the launch traced here: 57.3 us
  waiting for transfers between devices  29.1 us (51%)
  starting transfers between devices  15.2 us (26%)
  Pallas kernels  12.9 us (22%)
    ppermute x9, waiting for transfers between devices, move(): parts.append(lax.ppermute(part, ('pool', 'tp'), pairs))  26.4 us
    ppermute x9, starting transfers between devices, move(): parts.append(lax.ppermute(part, ('pool', 'tp'), pairs))  14 us
    pallas_call x1, Pallas kernels, prepare(): pl.pallas_call(prepare_kernel, out_shape=[pltpu.VMEM((cached_count, rows,...  4.36 us
    pallas_call x1, Pallas kernels, attend(): pl.pallas_call(functools.partial(attend_kernel, parts), out_shape=jax.Sha...  3.33 us
    pallas_call x3, Pallas kernels, serve(): pl.pallas_call(functools.partial(serve_kernel, len(rows), parts), out_sha...  3.33 us
    ppermute x7, waiting for transfers between devices, swap(): return lax.ppermute(array, 'tp', [(0, 1), (1, 0)])  2.7 us
    pallas_call x1, Pallas kernels, pack(): pl.pallas_call(functools.partial(pack_kernel, pool_count, tp_count, capac...  1.57 us
    ppermute x7, starting transfers between devices, swap(): return lax.ppermute(array, 'tp', [(0, 1), (1, 0)])  1.2 us
  transfers between devices with their start and end apart: 16, of which 8 were waited for; matrix products, arithmetic and copies ran while one was open for 0% of the time, Pallas kernels for 17%

profile of v5, /device:TPU:19, one launch (start us, length us, event | category | flops | bytes accessed | tf_op | source)
XLA Modules:
  0.0 57.3 jit_solution(16039258731437072261)
XLA Ops:
  0.0 0.7 %collective-permute-start = (bf16[2,64,4096]{2,1,0:T(8,128)(2,1)}, bf16[2,64,4096]{2,1,0:T(8,128)(2,1)S(1)}, u32[]{:S(2)}, u32[]{:S(2)}) collective-permute-start(bf16[2,64,4096]{2,1,0:T(8,128)(2,1)} %bitcast.8), channel_id=1, source_target_pairs={{0,1},{1,0},{2,3},{3,2},{4,5},{5,4},{6,7},{7,6},{8,9},{9,8},{10,11... | collective-permute-start | bytes 3145736 | tf_op jit(solution)/shard_map/ppermute | solution.py:472
  0.7 0.0 collective-permute-start.1
  0.7 1.6 %pack.1 = (bf16[16,8320]{1,0:T(8,128)(2,1)S(1)}, bf16[16,8320]{1,0:T(8,128)(2,1)S(1)}, bf16[64,128]{1,0:T(8,128)(2,1)S(1)}, s32[2,64]{1,0:T(2,128)S(1)}, bf16[64,8192]{1,0:T(8,128)(2,1)S(1)}) custom-call(s32[1,64]{1,0:T(1,128)} %bitcast.10, s32[1,16]{1,0:T(1,128)} %bitcast.11, bf16[64,8192]{1,0:T(8,128)(2,1)} %hidden_hbm.1), custom_call_target="tpu_custom_call" | custom-call | tf_op jit(solution)/shard_map/pack/pallas_call | solution.py:118
  2.3 1.1 %collective-permute-start.4 = (bf16[16,8320]{1,0:T(8,128)(2,1)S(1)}, bf16[16,8320]{1,0:T(8,128)(2,1)S(1)}, u32[]{:S(2)}, u32[]{:S(2)}) collective-permute-start(bf16[16,8320]{1,0:T(8,128)(2,1)S(1)} %get-tuple-element.59), channel_id=1, source_target_pairs={{0,8},{1,11},{2,10},{3,9},{4,12},{5,15},{6,14},{7,13},{8,0},{9,3},... | collective-permute-start | bytes 798728 | tf_op jit(solution)/shard_map/ppermute | solution.py:468
  3.3 0.0 collective-permute-done.refs_2_.refs_3_
  3.3 1.3 %collective-permute-done.1.refs_4_.refs_5_ = bf16[2,64,4096]{2,1,0:T(8,128)(2,1)S(1)} collective-permute-done((bf16[2,64,4096]{2,1,0:T(8,128)(2,1)}, bf16[2,64,4096]{2,1,0:T(8,128)(2,1)S(1)}, u32[]{:S(2)}, u32[]{:S(2)}) %collective-permute-start.1) | collective-permute-done | bytes 1048608 | tf_op jit(solution)/shard_map/ppermute | solution.py:472
  4.7 0.3 pack_near.1
  5.0 3.2 %collective-permute-start.2 = (bf16[16,8320]{1,0:T(8,128)(2,1)S(1)}, bf16[16,8320]{1,0:T(8,128)(2,1)S(1)}, u32[]{:S(2)}, u32[]{:S(2)}) collective-permute-start(bf16[16,8320]{1,0:T(8,128)(2,1)S(1)} %get-tuple-element.57), channel_id=1, source_target_pairs={{0,0},{1,3},{2,2},{3,1},{4,4},{5,7},{6,6},{7,5},{8,8},{9,11},{10,1... | collective-permute-start | bytes 798728 | tf_op jit(solution)/shard_map/ppermute | solution.py:468
  8.1 1.3 %collective-permute-start.3 = (bf16[16,8320]{1,0:T(8,128)(2,1)S(1)}, bf16[16,8320]{1,0:T(8,128)(2,1)S(1)}, u32[]{:S(2)}, u32[]{:S(2)}) collective-permute-start(bf16[16,8320]{1,0:T(8,128)(2,1)S(1)} %get-tuple-element.58), channel_id=1, source_target_pairs={{0,4},{1,7},{2,6},{3,5},{4,0},{5,3},{6,2},{7,1},{8,12},{9,15},{10,... | collective-permute-start | bytes 798728 | tf_op jit(solution)/shard_map/ppermute | solution.py:468
  9.4 0.0 collective-permute-start.8
  9.4 4.4 %prepare.1 = (f32[4,512,128]{2,1,0:T(8,128)S(1)}, f32[4,512,128]{2,1,0:T(8,128)S(1)}, f32[4,512,128]{2,1,0:T(8,128)S(1)}, f32[4,512,128]{2,1,0:T(8,128)S(1)}, bf...) custom-call(bf16[64,4096]{1,0:T(8,128)(2,1)} %base_hbm, ...), custom_call_target="tpu_custom_call" | custom-call | bytes 10485760 | tf_op jit(solution)/shard_map/prepare/pallas_call | solution.py:295
  13.8 1.5 %collective-permute-done.4.refs_0_ = bf16[16,8320]{1,0:T(8,128)(2,1)S(1)} collective-permute-done((bf16[16,8320]{1,0:T(8,128)(2,1)S(1)}, bf16[16,8320]{1,0:T(8,128)(2,1)S(1)}, u32[]{:S(2)}, u32[]{:S(2)}) %collective-permute-start.4) | collective-permute-done | bytes 266272 | tf_op jit(solution)/shard_map/ppermute | solution.py:468
  15.3 1.1 %serve.3 = bf16[2,16,4096]{2,1,0:T(8,128)(2,1)S(1)} custom-call(bf16[16,8320]{1,0:T(8,128)(2,1)S(1)} %collective-permute-done.4.refs_0_, bf16[2,64,4096]{2,1,0:T(8,128)(2,1)S(1)} %get-tuple-element.60.refs_1_.refs_2_, bf16[2,64,4096]{2,1,0:T(8,128)(2,1)S(1)} %collective-permute-done.refs_2_.refs_3_, ...), custom_call_target="tpu_custom_call" | custom-call | tf_op jit(solution)/shard_map/serve/pallas_call | solution.py:199
  16.4 0.0 collective-permute-done.2.refs_0_
  16.4 9.0 %collective-permute-done.3.refs_1_ = bf16[16,8320]{1,0:T(8,128)(2,1)S(1)} collective-permute-done((bf16[16,8320]{1,0:T(8,128)(2,1)S(1)}, bf16[16,8320]{1,0:T(8,128)(2,1)S(1)}, u32[]{:S(2)}, u32[]{:S(2)}) %collective-permute-start.3) | collective-permute-done | bytes 266272 | tf_op jit(solution)/shard_map/ppermute | solution.py:468
  25.4 1.1 %serve.4 = (bf16[2,16,4096]{2,1,0:T(8,128)(2,1)S(1)}, bf16[2,16,4096]{2,1,0:T(8,128)(2,1)S(1)}) custom-call(bf16[16,8320]{1,0:T(8,128)(2,1)S(1)} %collective-permute-done.2.refs_0_, bf16[16,8320]{1,0:T(8,128)(2,1)S(1)} %collective-permute-done.3.refs_1_, bf16[2,64,4096]{2,1,0:T(8,128)(2,1)S(1)} %get-tuple-element.60.refs_1_.refs_2_, ...), custom_call_target="tpu_custom_call" | custom-call | tf_op jit(solution)/shard_map/serve/pallas_call | solution.py:199
  26.5 1.0 %collective-permute-start.7 = (bf16[2,16,4096]{2,1,0:T(8,128)(2,1)S(1)}, bf16[2,16,4096]{2,1,0:T(8,128)(2,1)S(1)}, u32[]{:S(2)}, u32[]{:S(2)}) collective-permute-start(bf16[2,16,4096]{2,1,0:T(8,128)(2,1)S(1)} %serve.3), channel_id=1, source_target_pairs={{0,8},{1,11},{2,10},{3,9},{4,12},{5,15},{6,14},{7,13},{8,0},{9,3},... | collective-permute-start | bytes 786440 | tf_op jit(solution)/shard_map/ppermute | solution.py:468
  27.5 2.0 %collective-permute-start.6 = (bf16[2,16,4096]{2,1,0:T(8,128)(2,1)S(1)}, bf16[2,16,4096]{2,1,0:T(8,128)(2,1)S(1)}, u32[]{:S(2)}, u32[]{:S(2)}) collective-permute-start(bf16[2,16,4096]{2,1,0:T(8,128)(2,1)S(1)} %get-tuple-element.65), channel_id=1, source_target_pairs={{0,4},{1,7},{2,6},{3,5},{4,0},{5,3},{6,2},{7,1},{8,12},{9,15},{10,... | collective-permute-start | bytes 786440 | tf_op jit(solution)/shard_map/ppermute | solution.py:468
  29.5 3.1 %collective-permute-start.5 = (bf16[2,16,4096]{2,1,0:T(8,128)(2,1)S(1)}, bf16[2,16,4096]{2,1,0:T(8,128)(2,1)S(1)}, u32[]{:S(2)}, u32[]{:S(2)}) collective-permute-start(bf16[2,16,4096]{2,1,0:T(8,128)(2,1)S(1)} %get-tuple-element.64), channel_id=1, source_target_pairs={{0,0},{1,3},{2,2},{3,1},{4,4},{5,7},{6,6},{7,5},{8,8},{9,11},{10,1... | collective-permute-start | bytes 786440 | tf_op jit(solution)/shard_map/ppermute | solution.py:468
  32.6 0.0 collective-permute-done.8.refs_0_
  32.6 1.1 %serve.5 = (bf16[2,16,2048]{2,1,0:T(8,128)(2,1)S(1)}, bf16[2,16,2048]{2,1,0:T(8,128)(2,1)S(1)}) custom-call(bf16[16,8320]{1,0:T(8,128)(2,1)S(1)} %collective-permute-done.8.refs_0_, bf16[2,64,4096]{2,1,0:T(8,128)(2,1)S(1)} %get-tuple-element.60.refs_1_.refs_2_, bf16[2,64,4096]{2,1,0:T(8,128)(2,1)S(1)} %collective-permute-done.refs_2_.refs_3_, ...), custom_call_target="tpu_custom_call" | custom-call | tf_op jit(solution)/shard_map/serve/pallas_call | solution.py:199
  33.7 1.1 %collective-permute-start.9 = (bf16[2,16,2048]{2,1,0:T(8,128)(2,1)S(1)}, bf16[2,16,2048]{2,1,0:T(8,128)(2,1)S(1)}, u32[]{:S(2)}, u32[]{:S(2)}) collective-permute-start(bf16[2,16,2048]{2,1,0:T(8,128)(2,1)S(1)} %get-tuple-element.69), channel_id=1, source_target_pairs={{0,12},{1,15},{2,14},{3,13},{4,8},{5,11},{6,10},{7,9},{8,4},{9,7},... | collective-permute-start | bytes 393224 | tf_op jit(solution)/shard_map/ppermute | solution.py:468
  34.8 1.3 %collective-permute-start.10 = (bf16[2,16,2048]{2,1,0:T(8,128)(2,1)S(1)}, bf16[2,16,2048]{2,1,0:T(8,128)(2,1)S(1)}, u32[]{:S(2)}, u32[]{:S(2)}) collective-permute-start(bf16[2,16,2048]{2,1,0:T(8,128)(2,1)S(1)} %get-tuple-element.70), channel_id=1, source_target_pairs={{0,12},{1,15},{2,14},{3,13},{4,8},{5,11},{6,10},{7,9},{8,4},{9,7},... | collective-permute-start | bytes 393224 | tf_op jit(solution)/shard_map/ppermute | solution.py:468
  36.1 4.6 %collective-permute-done.7.refs_2_ = bf16[2,16,4096]{2,1,0:T(8,128)(2,1)S(1)} collective-permute-done((bf16[2,16,4096]{2,1,0:T(8,128)(2,1)S(1)}, bf16[2,16,4096]{2,1,0:T(8,128)(2,1)S(1)}, u32[]{:S(2)}, u32[]{:S(2)}) %collective-permute-start.7) | collective-permute-done | bytes 262176 | tf_op jit(solution)/shard_map/ppermute | solution.py:468
  40.7 0.0 collective-permute-start.13
  40.7 0.8 %collective-permute-done.6.refs_1_ = bf16[2,16,4096]{2,1,0:T(8,128)(2,1)S(1)} collective-permute-done((bf16[2,16,4096]{2,1,0:T(8,128)(2,1)S(1)}, bf16[2,16,4096]{2,1,0:T(8,128)(2,1)S(1)}, u32[]{:S(2)}, u32[]{:S(2)}) %collective-permute-start.6) | collective-permute-done | bytes 262176 | tf_op jit(solution)/shard_map/ppermute | solution.py:468
  41.6 0.0 collective-permute-start.12
  41.6 0.0 collective-permute-done.5.refs_0_
  41.6 0.5 collective-permute-start.11
  42.1 7.8 %collective-permute-done.9.refs_3_ = bf16[2,16,2048]{2,1,0:T(8,128)(2,1)S(1)} collective-permute-done((bf16[2,16,2048]{2,1,0:T(8,128)(2,1)S(1)}, bf16[2,16,2048]{2,1,0:T(8,128)(2,1)S(1)}, u32[]{:S(2)}, u32[]{:S(2)}) %collective-permute-start.9) | collective-permute-done | bytes 131104 | tf_op jit(solution)/shard_map/ppermute | solution.py:468
  49.9 0.0 collective-permute-start.14
  49.9 2.7 %collective-permute-done.10.refs_4_ = bf16[2,16,2048]{2,1,0:T(8,128)(2,1)S(1)} collective-permute-done((bf16[2,16,2048]{2,1,0:T(8,128)(2,1)S(1)}, bf16[2,16,2048]{2,1,0:T(8,128)(2,1)S(1)}, u32[]{:S(2)}, u32[]{:S(2)}) %collective-permute-start.10) | collective-permute-done | bytes 131104 | tf_op jit(solution)/shard_map/ppermute | solution.py:468
  52.6 0.0 collective-permute-start.15
  52.6 0.0 collective-permute-done.14.refs_8_
  52.6 1.3 %collective-permute-done.15.refs_9_ = bf16[2,16,2048]{2,1,0:T(8,128)(2,1)S(1)} collective-permute-done((bf16[2,16,2048]{2,1,0:T(8,128)(2,1)S(1)}, bf16[2,16,2048]{2,1,0:T(8,128)(2,1)S(1)}, u32[]{:S(2)}, u32[]{:S(2)}) %collective-permute-start.15) | collective-permute-done | bytes 131104 | tf_op jit(solution)/shard_map/ppermute | solution.py:472
  54.0 0.0 collective-permute-done.13.refs_7_
  54.0 0.0 collective-permute-done.12.refs_6_
  54.0 0.0 collective-permute-done.11.refs_5_
  54.0 3.3 %attend.1 = bf16[64,4096]{1,0:T(8,128)(2,1)} custom-call(f32[4,512,128]{2,1,0:T(8,128)S(1)} %get-tuple-element.47.heads_ref, f32[4,512,128]{2,1,0:T(8,128)S(1)} %get-tuple-element.48.score_ref, f32[4,512,128]{2,1,0:T(8,128)S(1)} %get-tuple-element.49.fresh_k_ref, f32[4,512,128]{2,1,0:T(8,128)S(1)} %get-tuple-element.50.fresh_v_ref, ...), custom_call_target="tpu_custom_call" | custom-call | tf_op jit(solution)/shard_map/attend/pallas_call | solution.py:412
Async XLA Ops:
  0.0 3.3 %collective-permute-start = (bf16[2,64,4096]{2,1,0:T(8,128)(2,1)}, bf16[2,64,4096]{2,1,0:T(8,128)(2,1)S(1)}, u32[]{:S(2)}, u32[]{:S(2)}) collective-permute-start(bf16[2,64,4096]{2,1,0:T(8,128)(2,1)} %bitcast.8), channel_id=1, source_target_pairs={{0,1},{1,0},{2,3},{3,2},{4,5},{5,4},{6,7},{7,6},{8,9},{9,8},{10,11... | collective-permute-start | bytes 3145736 | tf_op jit(solution)/shard_map/ppermute | solution.py:472
  0.7 4.0 %collective-permute-start.1 = (bf16[2,64,4096]{2,1,0:T(8,128)(2,1)}, bf16[2,64,4096]{2,1,0:T(8,128)(2,1)S(1)}, u32[]{:S(2)}, u32[]{:S(2)}) collective-permute-start(bf16[2,64,4096]{2,1,0:T(8,128)(2,1)} %up_hbm), channel_id=1, source_target_pairs={{0,1},{1,0},{2,3},{3,2},{4,5},{5,4},{6,7},{7,6},{8,9},{9,8},{10,11... | collective-permute-start | bytes 3145736 | tf_op jit(solution)/shard_map/ppermute | solution.py:472
  2.3 13.0 %collective-permute-start.4 = (bf16[16,8320]{1,0:T(8,128)(2,1)S(1)}, bf16[16,8320]{1,0:T(8,128)(2,1)S(1)}, u32[]{:S(2)}, u32[]{:S(2)}) collective-permute-start(bf16[16,8320]{1,0:T(8,128)(2,1)S(1)} %get-tuple-element.59), channel_id=1, source_target_pairs={{0,8},{1,11},{2,10},{3,9},{4,12},{5,15},{6,14},{7,13},{8,0},{9,3},... | collective-permute-start | bytes 798728 | tf_op jit(solution)/shard_map/ppermute | solution.py:468
  5.0 11.4 %collective-permute-start.2 = (bf16[16,8320]{1,0:T(8,128)(2,1)S(1)}, bf16[16,8320]{1,0:T(8,128)(2,1)S(1)}, u32[]{:S(2)}, u32[]{:S(2)}) collective-permute-start(bf16[16,8320]{1,0:T(8,128)(2,1)S(1)} %get-tuple-element.57), channel_id=1, source_target_pairs={{0,0},{1,3},{2,2},{3,1},{4,4},{5,7},{6,6},{7,5},{8,8},{9,11},{10,1... | collective-permute-start | bytes 798728 | tf_op jit(solution)/shard_map/ppermute | solution.py:468
  8.1 17.2 %collective-permute-start.3 = (bf16[16,8320]{1,0:T(8,128)(2,1)S(1)}, bf16[16,8320]{1,0:T(8,128)(2,1)S(1)}, u32[]{:S(2)}, u32[]{:S(2)}) collective-permute-start(bf16[16,8320]{1,0:T(8,128)(2,1)S(1)} %get-tuple-element.58), channel_id=1, source_target_pairs={{0,4},{1,7},{2,6},{3,5},{4,0},{5,3},{6,2},{7,1},{8,12},{9,15},{10,... | collective-permute-start | bytes 798728 | tf_op jit(solution)/shard_map/ppermute | solution.py:468
  9.4 23.2 %collective-permute-start.8 = (bf16[16,8320]{1,0:T(8,128)(2,1)S(1)}, bf16[16,8320]{1,0:T(8,128)(2,1)S(1)}, u32[]{:S(2)}, u32[]{:S(2)}) collective-permute-start(bf16[16,8320]{1,0:T(8,128)(2,1)S(1)} %get-tuple-element.67), channel_id=1, source_target_pairs={{0,12},{1,15},{2,14},{3,13},{4,8},{5,11},{6,10},{7,9},{8,4},{9,7},... | collective-permute-start | bytes 798728 | tf_op jit(solution)/shard_map/ppermute | solution.py:468
  26.5 14.2 %collective-permute-start.7 = (bf16[2,16,4096]{2,1,0:T(8,128)(2,1)S(1)}, bf16[2,16,4096]{2,1,0:T(8,128)(2,1)S(1)}, u32[]{:S(2)}, u32[]{:S(2)}) collective-permute-start(bf16[2,16,4096]{2,1,0:T(8,128)(2,1)S(1)} %serve.3), channel_id=1, source_target_pairs={{0,8},{1,11},{2,10},{3,9},{4,12},{5,15},{6,14},{7,13},{8,0},{9,3},... | collective-permute-start | bytes 786440 | tf_op jit(solution)/shard_map/ppermute | solution.py:468
  27.5 14.1 %collective-permute-start.6 = (bf16[2,16,4096]{2,1,0:T(8,128)(2,1)S(1)}, bf16[2,16,4096]{2,1,0:T(8,128)(2,1)S(1)}, u32[]{:S(2)}, u32[]{:S(2)}) collective-permute-start(bf16[2,16,4096]{2,1,0:T(8,128)(2,1)S(1)} %get-tuple-element.65), channel_id=1, source_target_pairs={{0,4},{1,7},{2,6},{3,5},{4,0},{5,3},{6,2},{7,1},{8,12},{9,15},{10,... | collective-permute-start | bytes 786440 | tf_op jit(solution)/shard_map/ppermute | solution.py:468
  29.5 12.1 %collective-permute-start.5 = (bf16[2,16,4096]{2,1,0:T(8,128)(2,1)S(1)}, bf16[2,16,4096]{2,1,0:T(8,128)(2,1)S(1)}, u32[]{:S(2)}, u32[]{:S(2)}) collective-permute-start(bf16[2,16,4096]{2,1,0:T(8,128)(2,1)S(1)} %get-tuple-element.64), channel_id=1, source_target_pairs={{0,0},{1,3},{2,2},{3,1},{4,4},{5,7},{6,6},{7,5},{8,8},{9,11},{10,1... | collective-permute-start | bytes 786440 | tf_op jit(solution)/shard_map/ppermute | solution.py:468
  33.7 16.2 %collective-permute-start.9 = (bf16[2,16,2048]{2,1,0:T(8,128)(2,1)S(1)}, bf16[2,16,2048]{2,1,0:T(8,128)(2,1)S(1)}, u32[]{:S(2)}, u32[]{:S(2)}) collective-permute-start(bf16[2,16,2048]{2,1,0:T(8,128)(2,1)S(1)} %get-tuple-element.69), channel_id=1, source_target_pairs={{0,12},{1,15},{2,14},{3,13},{4,8},{5,11},{6,10},{7,9},{8,4},{9,7},... | collective-permute-start | bytes 393224 | tf_op jit(solution)/shard_map/ppermute | solution.py:468
  34.8 17.8 %collective-permute-start.10 = (bf16[2,16,2048]{2,1,0:T(8,128)(2,1)S(1)}, bf16[2,16,2048]{2,1,0:T(8,128)(2,1)S(1)}, u32[]{:S(2)}, u32[]{:S(2)}) collective-permute-start(bf16[2,16,2048]{2,1,0:T(8,128)(2,1)S(1)} %get-tuple-element.70), channel_id=1, source_target_pairs={{0,12},{1,15},{2,14},{3,13},{4,8},{5,11},{6,10},{7,9},{8,4},{9,7},... | collective-permute-start | bytes 393224 | tf_op jit(solution)/shard_map/ppermute | solution.py:468
  40.7 13.2 %collective-permute-start.13 = (bf16[2,16,4096]{2,1,0:T(8,128)(2,1)S(1)}, bf16[2,16,4096]{2,1,0:T(8,128)(2,1)S(1)}, u32[]{:S(2)}, u32[]{:S(2)}) collective-permute-start(bf16[2,16,4096]{2,1,0:T(8,128)(2,1)S(1)} %collective-permute-done.7.refs_2_), channel_id=1, source_target_pairs={{0,1},{1,0},{2,3},{3,2},{4,5},{5,4},{6,7},{7,6},{8,9},{9,8},{10,11... | collective-permute-start | bytes 786440 | tf_op jit(solution)/shard_map/ppermute | solution.py:472
  41.6 12.4 %collective-permute-start.12 = (bf16[2,16,4096]{2,1,0:T(8,128)(2,1)S(1)}, bf16[2,16,4096]{2,1,0:T(8,128)(2,1)S(1)}, u32[]{:S(2)}, u32[]{:S(2)}) collective-permute-start(bf16[2,16,4096]{2,1,0:T(8,128)(2,1)S(1)} %collective-permute-done.6.refs_1_), channel_id=1, source_target_pairs={{0,1},{1,0},{2,3},{3,2},{4,5},{5,4},{6,7},{7,6},{8,9},{9,8},{10,11... | collective-permute-start | bytes 786440 | tf_op jit(solution)/shard_map/ppermute | solution.py:472
  41.6 12.4 %collective-permute-start.11 = (bf16[2,16,4096]{2,1,0:T(8,128)(2,1)S(1)}, bf16[2,16,4096]{2,1,0:T(8,128)(2,1)S(1)}, u32[]{:S(2)}, u32[]{:S(2)}) collective-permute-start(bf16[2,16,4096]{2,1,0:T(8,128)(2,1)S(1)} %collective-permute-done.5.refs_0_), channel_id=1, source_target_pairs={{0,1},{1,0},{2,3},{3,2},{4,5},{5,4},{6,7},{7,6},{8,9},{9,8},{10,11... | collective-permute-start | bytes 786440 | tf_op jit(solution)/shard_map/ppermute | solution.py:472
  49.9 2.7 %collective-permute-start.14 = (bf16[2,16,2048]{2,1,0:T(8,128)(2,1)S(1)}, bf16[2,16,2048]{2,1,0:T(8,128)(2,1)S(1)}, u32[]{:S(2)}, u32[]{:S(2)}) collective-permute-start(bf16[2,16,2048]{2,1,0:T(8,128)(2,1)S(1)} %collective-permute-done.9.refs_3_), channel_id=1, source_target_pairs={{0,1},{1,0},{2,3},{3,2},{4,5},{5,4},{6,7},{7,6},{8,9},{9,8},{10,11... | collective-permute-start | bytes 393224 | tf_op jit(solution)/shard_map/ppermute | solution.py:472
  52.6 1.3 %collective-permute-start.15 = (bf16[2,16,2048]{2,1,0:T(8,128)(2,1)S(1)}, bf16[2,16,2048]{2,1,0:T(8,128)(2,1)S(1)}, u32[]{:S(2)}, u32[]{:S(2)}) collective-permute-start(bf16[2,16,2048]{2,1,0:T(8,128)(2,1)S(1)} %collective-permute-done.10.refs_4_), channel_id=1, source_target_pairs={{0,1},{1,0},{2,3},{3,2},{4,5},{5,4},{6,7},{7,6},{8,9},{9,8},{10,11... | collective-permute-start | bytes 393224 | tf_op jit(solution)/shard_map/ppermute | solution.py:472

commit v6 on v5

--- a/solution.py
+++ b/solution.py
@@ -175,6 +175,9 @@
                 preferred_element_type=jnp.float32,
             )
             middle = middle + jnp.where(tags == float(slot), partial, 0.0)
+    for out in outs:
+        if out.shape[2] > width // parts:
+            out[:, :, width // parts :] = jnp.zeros((2, out.shape[1], out.shape[2] - width // parts), jnp.bfloat16)
     middle = middle.astype(jnp.bfloat16).astype(jnp.float32)
     chosen = jnp.concatenate(
         [jnp.where(tags == float(slot), middle, 0.0) for slot in range(owned_count)], axis=1
@@ -194,12 +197,14 @@
                 at += out.shape[1]
 
 
-def serve(rows, factors, parts=1):
+def serve(rows, factors, parts=1, extra=0):
     width = factors[0].shape[2]
     return pl.pallas_call(
         functools.partial(serve_kernel, len(rows), parts),
         out_shape=[
-            pltpu.VMEM((2, row.shape[0], width // parts), jnp.bfloat16) for row in rows for _ in range(parts)
+            pltpu.VMEM((2, row.shape[0], width // parts + extra * (part == parts - 1)), jnp.bfloat16)
+            for row in rows
+            for part in range(parts)
         ],
         in_specs=[VMEM] * (len(rows) + 4),
         out_specs=[VMEM] * (len(rows) * parts),
@@ -315,7 +320,8 @@
 
 
 def attend_kernel(
-    parts,
+    first,
+    begins,
     heads_ref,
     score_ref,
     fresh_k_ref,
@@ -325,24 +331,35 @@
     routing_ref,
     *refs,
 ):
-    returned = refs[:-6]
-    out_hbm, delta_ref, weight_ref, mixed_ref, out_ref, sems = refs[-6:]
+    returned = refs[: len(begins)]
+    if first == 0:
+        out_ref, delta_ref, weight_ref, mixed_ref = refs[len(begins) :]
+    else:
+        before_ref, out_hbm, delta_ref, weight_ref, mixed_ref, out_ref, sems = refs[len(begins) :]
     _, pair_count, _, _ = key_ref.shape
     _, rows, _ = heads_ref.shape
-    requests = out_hbm.shape[0]
+    requests = routing_ref.shape[0]
     group_size = rows // requests
     block = rows // pair_count
     half = lax.axis_index("tp")
     width = group_size * HEAD_SIZE
     copies = []
-    cached_count = out_ref.shape[0]
+    span = range(out_ref.shape[0])
+
+    def send(source, j):
+        copy = pltpu.make_async_copy(source, out_hbm.at[:, pl.ds(j * width, width)], sems.at[j])
+        copy.start()
+        copies.append(copy)
+
+    if first:
+        for j in range(first):
+            send(before_ref.at[j], j)
 
     def unpack(j):
         arrived = []
-        for piece in parts:
-            part, at = divmod(j * len(piece), cached_count)
-            at = at // len(piece) * width
-            arrived.append(returned[piece[part]][half, :, at : at + width])
+        for piece, begin in zip(returned, begins):
+            wide = slice((first + j - begin) * width, (first + j - begin + 1) * width)
+            arrived.append(piece[half, :, wide] if len(piece.shape) == 3 else piece[:, wide])
         arrived = jnp.concatenate(arrived, axis=0)
         delta = jnp.dot(routing_ref[...], arrived, preferred_element_type=jnp.float32)
         for h in range(group_size):
@@ -354,12 +371,12 @@
         for p in range(pair_count):
             here = slice(p * block, (p + 1) * block)
             weight_ref[j, here, :] = jnp.dot(
-                delta_ref[j, here, :].astype(jnp.bfloat16), key_ref[j, p], preferred_element_type=jnp.float32
+                delta_ref[j, here, :].astype(jnp.bfloat16), key_ref[first + j, p], preferred_element_type=jnp.float32
             )
 
     def weigh(j):
-        scores = score_ref[j] + weight_ref[j] * FACTOR
-        own = (heads_ref[j] + delta_ref[j]) * fresh_k_ref[j]
+        scores = score_ref[first + j] + weight_ref[j] * FACTOR
+        own = (heads_ref[first + j] + delta_ref[j]) * fresh_k_ref[first + j]
         own = jnp.sum(own, axis=1, keepdims=True) * FACTOR
         highest = jnp.maximum(jnp.max(scores, axis=1, keepdims=True), own)
         weights = jnp.exp(scores - highest)
@@ -367,11 +384,11 @@
         totals = jnp.sum(weights, axis=1, keepdims=True) + own_weight
         weight_ref[j] = weights
         own_b = own_weight.astype(jnp.bfloat16).astype(jnp.float32)
-        delta_ref[j] = own_b * fresh_v_ref[j]
+        delta_ref[j] = own_b * fresh_v_ref[first + j]
         return totals
 
     def mix(j, totals):
-        lanes = slice(j * HEAD_SIZE, (j + 1) * HEAD_SIZE)
+        lanes = slice((first + j) * HEAD_SIZE, (first + j + 1) * HEAD_SIZE)
         for p in range(pair_count):
             here = slice(p * block, (p + 1) * block)
             mixed_ref[j, here, :] = jnp.dot(
@@ -384,46 +401,63 @@
             out_ref[j, :, h * HEAD_SIZE : (h + 1) * HEAD_SIZE] = mixed_ref[
                 j, pl.ds(h, requests, stride=group_size), :
             ].astype(jnp.bfloat16)
-        copy = pltpu.make_async_copy(
-            out_ref.at[j], out_hbm.at[:, pl.ds(j * width, width)], sems.at[j]
-        )
-        copy.start()
-        copies.append(copy)
-
-    for j in range(cached_count):
+        if first:
+            send(out_ref.at[j], first + j)
+
+    for j in span:
         unpack(j)
-    for j in range(cached_count):
+    for j in span:
         score(j)
-    totals = [weigh(j) for j in range(cached_count)]
-    for j in range(cached_count):
+    totals = [weigh(j) for j in span]
+    for j in span:
         mix(j, totals[j])
     for copy in copies:
         copy.wait()
 
 
-def attend(held, routing_b, pieces):
+def attend(held, routing_b, pieces, first, span, out):
     cached_count, rows, _ = held[0].shape
     requests = routing_b.shape[0]
     width = rows // requests * HEAD_SIZE
-    parts, returned = [], []
-    for piece in pieces:
-        parts.append(list(range(len(returned), len(returned) + len(piece))))
-        returned.extend(piece)
+    operands = [*held, routing_b, *[piece for piece, _ in pieces]]
+    some = (span, requests, width)
+    scratch = [
+        pltpu.VMEM((span, rows, HEAD_SIZE), jnp.float32),
+        pltpu.VMEM((span, rows, held[1].shape[2]), jnp.float32),
+        pltpu.VMEM((span, rows, HEAD_SIZE), jnp.float32),
+    ]
+    if first == 0:
+        result, place = pltpu.VMEM(some, jnp.bfloat16), VMEM
+    else:
+        operands.append(out)
+        result, place = jax.ShapeDtypeStruct((requests, cached_count * width), jnp.bfloat16), ANYWHERE
+        scratch += [pltpu.VMEM(some, jnp.bfloat16), pltpu.SemaphoreType.DMA((cached_count,))]
     return pl.pallas_call(
-        functools.partial(attend_kernel, parts),
-        out_shape=jax.ShapeDtypeStruct((requests, cached_count * width), jnp.bfloat16),
-        in_specs=[VMEM] * (len(held) + 1 + len(returned)),
-        out_specs=ANYWHERE,
-        scratch_shapes=[
-            pltpu.VMEM((cached_count, rows, HEAD_SIZE), jnp.float32),
-            pltpu.VMEM((cached_count, rows, held[1].shape[2]), jnp.float32),
-            pltpu.VMEM((cached_count, rows, HEAD_SIZE), jnp.float32),
-            pltpu.VMEM((cached_count, requests, width), jnp.bfloat16),
-            pltpu.SemaphoreType.DMA((cached_count,)),
-        ],
+        functools.partial(attend_kernel, first, [begin for _, begin in pieces]),
+        out_shape=result,
+        in_specs=[VMEM] * len(operands),
+        out_specs=place,
+        scratch_shapes=scratch,
         compiler_params=grant(8),
+        cost_estimate=pl.CostEstimate(flops=0, bytes_accessed=0, transcendentals=0),
         name="attend",
-    )(*held, routing_b, *returned)
+    )(*operands)
+
+
+def theirs_kernel(rows_ref, out_ref):
+    out_ref[...] = rows_ref[1 - lax.axis_index("tp")]
+
+
+def theirs_of(rows):
+    return pl.pallas_call(
+        theirs_kernel,
+        out_shape=pltpu.VMEM(rows.shape[1:], rows.dtype),
+        in_specs=[VMEM],
+        out_specs=VMEM,
+        compiler_params=grant(8),
+        cost_estimate=pl.CostEstimate(flops=0, bytes_accessed=0, transcendentals=0),
+        name="theirs",
+    )(rows)
 
 
 def after(arrays, *tokens):
@@ -502,13 +536,22 @@
     served = serve(after([arrived[g] for g in near], early[0]), factors)
     returned = {g: move(g, rows) for g, rows in zip(near, served)}
     returned |= {g: move(g, rows) for g, rows in zip(far, after(early, served[0]))}
-    final = serve(after([arrived[last]], served[0]), factors, parts=2)
+    final = serve(after([arrived[last]], served[0]), factors, parts=2, extra=0)
     final = [move(last, rows) for rows in final]
+
+    def hand(rows):
+        return swap(theirs_of(rows))
+
     whole = [returned[g] for g in range(last)]
-    others = [swap(rows) for rows in whole]
-    mine = [[rows] for rows in whole] + [final]
-    theirs = [[rows] for rows in others] + [[swap(rows) for rows in final]]
-    return attend(held, routing_b, mine + theirs)
+    others = [hand(rows) for rows in whole]
+    span = features // HEAD_SIZE // len(final)
+    out = None
+    for k, rows in enumerate(final):
+        turn = rows
+        pieces = [(piece, 0) for piece in whole] + [(rows, k * span)]
+        pieces += [(piece, 0) for piece in others] + [(hand(turn), k * span)]
+        out = attend(held, routing_b, pieces, k * span, span, out)
+    return out
 
 
 def solution(mesh):

time: 57.5 us -> 56.4 us (0.981)
  waiting for transfers between devices: 29.1 us -> 27.5 us
    ppermute x7, waiting for transfers between devices: 2.7 us -> 1.36 us  [swap(): return lax.ppermute(array, 'tp', [(0, 1), (1, 0)])]
    pallas_call x1 -> x7, Pallas kernels: 3.33 us -> 3.64 us  [the longest x2 3.59 us: attend(): pl.pallas_call(functools.partial(attend_kernel, first, [begin for _, begi...]
  transfers between devices with their start and end apart: 16 -> 16, of which waited for: 8 -> 7; matrix products, arithmetic and copies ran while one was open for 0% -> 0% of each run, Pallas kernels for 17% -> 20%
where the time goes in v6:
time: 56.4 us; the launch traced here: 56.3 us
  waiting for transfers between devices  27.5 us (49%)
  starting transfers between devices  15.4 us (27%)
  Pallas kernels  13.2 us (23%)
    ppermute x9, waiting for transfers between devices, move(): parts.append(lax.ppermute(part, ('pool', 'tp'), pairs))  26.2 us
    ppermute x9, starting transfers between devices, move(): parts.append(lax.ppermute(part, ('pool', 'tp'), pairs))  14 us
    pallas_call x1, Pallas kernels, prepare(): pl.pallas_call(prepare_kernel, out_shape=[pltpu.VMEM((cached_count, rows,...  4.36 us
    pallas_call x2, Pallas kernels, attend(): pl.pallas_call(functools.partial(attend_kernel, first, [begin for _, begi...  3.59 us
    pallas_call x3, Pallas kernels, serve(): pl.pallas_call(functools.partial(serve_kernel, len(rows), parts), out_sha...  3.33 us
    pallas_call x1, Pallas kernels, pack(): pl.pallas_call(functools.partial(pack_kernel, pool_count, tp_count, capac...  1.57 us
    ppermute x7, starting transfers between devices, swap(): return lax.ppermute(array, 'tp', [(0, 1), (1, 0)])  1.37 us
    ppermute x7, waiting for transfers between devices, swap(): return lax.ppermute(array, 'tp', [(0, 1), (1, 0)])  1.36 us
  transfers between devices with their start and end apart: 16, of which 7 were waited for; matrix products, arithmetic and copies ran while one was open for 0% of the time, Pallas kernels for 20%

profile of v6, /device:TPU:19, one launch (start us, length us, event | category | flops | bytes accessed | tf_op | source)
XLA Modules:
  0.0 56.3 jit_solution(841973974846164078)
XLA Ops:
  0.0 0.7 %collective-permute-start = (bf16[2,64,4096]{2,1,0:T(8,128)(2,1)}, bf16[2,64,4096]{2,1,0:T(8,128)(2,1)S(1)}, u32[]{:S(2)}, u32[]{:S(2)}) collective-permute-start(bf16[2,64,4096]{2,1,0:T(8,128)(2,1)} %bitcast.8), channel_id=1, source_target_pairs={{0,1},{1,0},{2,3},{3,2},{4,5},{5,4},{6,7},{7,6},{8,9},{9,8},{10,11... | collective-permute-start | bytes 3145736 | tf_op jit(solution)/shard_map/ppermute | solution.py:506
  0.7 0.0 collective-permute-start.1
  0.7 1.6 %pack.1 = (bf16[16,8320]{1,0:T(8,128)(2,1)S(1)}, bf16[16,8320]{1,0:T(8,128)(2,1)S(1)}, bf16[64,128]{1,0:T(8,128)(2,1)S(1)}, s32[2,64]{1,0:T(2,128)S(1)}, bf16[64,8192]{1,0:T(8,128)(2,1)S(1)}) custom-call(s32[1,64]{1,0:T(1,128)} %bitcast.10, s32[1,16]{1,0:T(1,128)} %bitcast.11, bf16[64,8192]{1,0:T(8,128)(2,1)} %hidden_hbm.1), custom_call_target="tpu_custom_call" | custom-call | tf_op jit(solution)/shard_map/pack/pallas_call | solution.py:118
  2.3 1.1 %collective-permute-start.4 = (bf16[16,8320]{1,0:T(8,128)(2,1)S(1)}, bf16[16,8320]{1,0:T(8,128)(2,1)S(1)}, u32[]{:S(2)}, u32[]{:S(2)}) collective-permute-start(bf16[16,8320]{1,0:T(8,128)(2,1)S(1)} %get-tuple-element.59), channel_id=1, source_target_pairs={{0,8},{1,11},{2,10},{3,9},{4,12},{5,15},{6,14},{7,13},{8,0},{9,3},... | collective-permute-start | bytes 798728 | tf_op jit(solution)/shard_map/ppermute | solution.py:502
  3.3 0.0 collective-permute-done.refs_2_.refs_3_
  3.3 1.3 %collective-permute-done.1.refs_4_.refs_5_ = bf16[2,64,4096]{2,1,0:T(8,128)(2,1)S(1)} collective-permute-done((bf16[2,64,4096]{2,1,0:T(8,128)(2,1)}, bf16[2,64,4096]{2,1,0:T(8,128)(2,1)S(1)}, u32[]{:S(2)}, u32[]{:S(2)}) %collective-permute-start.1) | collective-permute-done | bytes 1048608 | tf_op jit(solution)/shard_map/ppermute | solution.py:506
  4.7 0.3 pack_near.1
  5.0 3.2 %collective-permute-start.2 = (bf16[16,8320]{1,0:T(8,128)(2,1)S(1)}, bf16[16,8320]{1,0:T(8,128)(2,1)S(1)}, u32[]{:S(2)}, u32[]{:S(2)}) collective-permute-start(bf16[16,8320]{1,0:T(8,128)(2,1)S(1)} %get-tuple-element.57), channel_id=1, source_target_pairs={{0,0},{1,3},{2,2},{3,1},{4,4},{5,7},{6,6},{7,5},{8,8},{9,11},{10,1... | collective-permute-start | bytes 798728 | tf_op jit(solution)/shard_map/ppermute | solution.py:502
  8.1 1.3 %collective-permute-start.3 = (bf16[16,8320]{1,0:T(8,128)(2,1)S(1)}, bf16[16,8320]{1,0:T(8,128)(2,1)S(1)}, u32[]{:S(2)}, u32[]{:S(2)}) collective-permute-start(bf16[16,8320]{1,0:T(8,128)(2,1)S(1)} %get-tuple-element.58), channel_id=1, source_target_pairs={{0,4},{1,7},{2,6},{3,5},{4,0},{5,3},{6,2},{7,1},{8,12},{9,15},{10,... | collective-permute-start | bytes 798728 | tf_op jit(solution)/shard_map/ppermute | solution.py:502
  9.4 0.0 collective-permute-start.8
  9.4 4.4 %prepare.1 = (f32[4,512,128]{2,1,0:T(8,128)S(1)}, f32[4,512,128]{2,1,0:T(8,128)S(1)}, f32[4,512,128]{2,1,0:T(8,128)S(1)}, f32[4,512,128]{2,1,0:T(8,128)S(1)}, bf...) custom-call(bf16[64,4096]{1,0:T(8,128)(2,1)} %base_hbm, ...), custom_call_target="tpu_custom_call" | custom-call | bytes 10485760 | tf_op jit(solution)/shard_map/prepare/pallas_call | solution.py:300
  13.8 1.5 %collective-permute-done.4.refs_0_ = bf16[16,8320]{1,0:T(8,128)(2,1)S(1)} collective-permute-done((bf16[16,8320]{1,0:T(8,128)(2,1)S(1)}, bf16[16,8320]{1,0:T(8,128)(2,1)S(1)}, u32[]{:S(2)}, u32[]{:S(2)}) %collective-permute-start.4) | collective-permute-done | bytes 266272 | tf_op jit(solution)/shard_map/ppermute | solution.py:502
  15.3 1.1 %serve.3 = bf16[2,16,4096]{2,1,0:T(8,128)(2,1)S(1)} custom-call(bf16[16,8320]{1,0:T(8,128)(2,1)S(1)} %collective-permute-done.4.refs_0_, bf16[2,64,4096]{2,1,0:T(8,128)(2,1)S(1)} %get-tuple-element.60.refs_1_.refs_2_, bf16[2,64,4096]{2,1,0:T(8,128)(2,1)S(1)} %collective-permute-done.refs_2_.refs_3_, ...), custom_call_target="tpu_custom_call" | custom-call | tf_op jit(solution)/shard_map/serve/pallas_call | solution.py:202
  16.4 0.0 collective-permute-done.2.refs_0_
  16.4 9.0 %collective-permute-done.3.refs_1_ = bf16[16,8320]{1,0:T(8,128)(2,1)S(1)} collective-permute-done((bf16[16,8320]{1,0:T(8,128)(2,1)S(1)}, bf16[16,8320]{1,0:T(8,128)(2,1)S(1)}, u32[]{:S(2)}, u32[]{:S(2)}) %collective-permute-start.3) | collective-permute-done | bytes 266272 | tf_op jit(solution)/shard_map/ppermute | solution.py:502
  25.4 1.1 %serve.4 = (bf16[2,16,4096]{2,1,0:T(8,128)(2,1)S(1)}, bf16[2,16,4096]{2,1,0:T(8,128)(2,1)S(1)}) custom-call(bf16[16,8320]{1,0:T(8,128)(2,1)S(1)} %collective-permute-done.2.refs_0_, bf16[16,8320]{1,0:T(8,128)(2,1)S(1)} %collective-permute-done.3.refs_1_, bf16[2,64,4096]{2,1,0:T(8,128)(2,1)S(1)} %get-tuple-element.60.refs_1_.refs_2_, ...), custom_call_target="tpu_custom_call" | custom-call | tf_op jit(solution)/shard_map/serve/pallas_call | solution.py:202
  26.5 1.0 %collective-permute-start.7 = (bf16[2,16,4096]{2,1,0:T(8,128)(2,1)S(1)}, bf16[2,16,4096]{2,1,0:T(8,128)(2,1)S(1)}, u32[]{:S(2)}, u32[]{:S(2)}) collective-permute-start(bf16[2,16,4096]{2,1,0:T(8,128)(2,1)S(1)} %serve.3), channel_id=1, source_target_pairs={{0,8},{1,11},{2,10},{3,9},{4,12},{5,15},{6,14},{7,13},{8,0},{9,3},... | collective-permute-start | bytes 786440 | tf_op jit(solution)/shard_map/ppermute | solution.py:502
  27.5 2.0 %collective-permute-start.6 = (bf16[2,16,4096]{2,1,0:T(8,128)(2,1)S(1)}, bf16[2,16,4096]{2,1,0:T(8,128)(2,1)S(1)}, u32[]{:S(2)}, u32[]{:S(2)}) collective-permute-start(bf16[2,16,4096]{2,1,0:T(8,128)(2,1)S(1)} %get-tuple-element.65), channel_id=1, source_target_pairs={{0,4},{1,7},{2,6},{3,5},{4,0},{5,3},{6,2},{7,1},{8,12},{9,15},{10,... | collective-permute-start | bytes 786440 | tf_op jit(solution)/shard_map/ppermute | solution.py:502
  29.5 3.1 %collective-permute-start.5 = (bf16[2,16,4096]{2,1,0:T(8,128)(2,1)S(1)}, bf16[2,16,4096]{2,1,0:T(8,128)(2,1)S(1)}, u32[]{:S(2)}, u32[]{:S(2)}) collective-permute-start(bf16[2,16,4096]{2,1,0:T(8,128)(2,1)S(1)} %get-tuple-element.64), channel_id=1, source_target_pairs={{0,0},{1,3},{2,2},{3,1},{4,4},{5,7},{6,6},{7,5},{8,8},{9,11},{10,1... | collective-permute-start | bytes 786440 | tf_op jit(solution)/shard_map/ppermute | solution.py:502
  32.6 0.0 collective-permute-done.8.refs_0_
  32.6 1.1 %serve.5 = (bf16[2,16,2048]{2,1,0:T(8,128)(2,1)S(1)}, bf16[2,16,2048]{2,1,0:T(8,128)(2,1)S(1)}) custom-call(bf16[16,8320]{1,0:T(8,128)(2,1)S(1)} %collective-permute-done.8.refs_0_, bf16[2,64,4096]{2,1,0:T(8,128)(2,1)S(1)} %get-tuple-element.60.refs_1_.refs_2_, bf16[2,64,4096]{2,1,0:T(8,128)(2,1)S(1)} %collective-permute-done.refs_2_.refs_3_, ...), custom_call_target="tpu_custom_call" | custom-call | tf_op jit(solution)/shard_map/serve/pallas_call | solution.py:202
  33.7 1.1 %collective-permute-start.14 = (bf16[2,16,2048]{2,1,0:T(8,128)(2,1)S(1)}, bf16[2,16,2048]{2,1,0:T(8,128)(2,1)S(1)}, u32[]{:S(2)}, u32[]{:S(2)}) collective-permute-start(bf16[2,16,2048]{2,1,0:T(8,128)(2,1)S(1)} %get-tuple-element.70), channel_id=1, source_target_pairs={{0,12},{1,15},{2,14},{3,13},{4,8},{5,11},{6,10},{7,9},{8,4},{9,7},... | collective-permute-start | bytes 393224 | tf_op jit(solution)/shard_map/ppermute | solution.py:502
  34.8 1.3 %collective-permute-start.9 = (bf16[2,16,2048]{2,1,0:T(8,128)(2,1)S(1)}, bf16[2,16,2048]{2,1,0:T(8,128)(2,1)S(1)}, u32[]{:S(2)}, u32[]{:S(2)}) collective-permute-start(bf16[2,16,2048]{2,1,0:T(8,128)(2,1)S(1)} %get-tuple-element.69), channel_id=1, source_target_pairs={{0,12},{1,15},{2,14},{3,13},{4,8},{5,11},{6,10},{7,9},{8,4},{9,7},... | collective-permute-start | bytes 393224 | tf_op jit(solution)/shard_map/ppermute | solution.py:502
  36.1 4.6 %collective-permute-done.7.rows_ref.refs_2_ = bf16[2,16,4096]{2,1,0:T(8,128)(2,1)S(1)} collective-permute-done((bf16[2,16,4096]{2,1,0:T(8,128)(2,1)S(1)}, bf16[2,16,4096]{2,1,0:T(8,128)(2,1)S(1)}, u32[]{:S(2)}, u32[]{:S(2)}) %collective-permute-start.7) | collective-permute-done | bytes 262176 | tf_op jit(solution)/shard_map/ppermute | solution.py:502
  40.7 0.1 collective-permute-start.12
  40.8 0.8 %collective-permute-done.6.rows_ref.refs_1_ = bf16[2,16,4096]{2,1,0:T(8,128)(2,1)S(1)} collective-permute-done((bf16[2,16,4096]{2,1,0:T(8,128)(2,1)S(1)}, bf16[2,16,4096]{2,1,0:T(8,128)(2,1)S(1)}, u32[]{:S(2)}, u32[]{:S(2)}) %collective-permute-start.6) | collective-permute-done | bytes 262176 | tf_op jit(solution)/shard_map/ppermute | solution.py:502
  41.6 0.1 collective-permute-start.11
  41.7 0.0 collective-permute-done.5.rows_ref.refs_0_
  41.7 0.5 collective-permute-start.10
  42.2 7.6 %collective-permute-done.14.rows_ref.refs_3_ = bf16[2,16,2048]{2,1,0:T(8,128)(2,1)S(1)} collective-permute-done((bf16[2,16,2048]{2,1,0:T(8,128)(2,1)S(1)}, bf16[2,16,2048]{2,1,0:T(8,128)(2,1)S(1)}, u32[]{:S(2)}, u32[]{:S(2)}) %collective-permute-start.14) | collective-permute-done | bytes 131104 | tf_op jit(solution)/shard_map/ppermute | solution.py:502
  49.9 0.0 collective-permute-start.15
  49.9 2.7 %collective-permute-done.9.rows_ref.refs_3_ = bf16[2,16,2048]{2,1,0:T(8,128)(2,1)S(1)} collective-permute-done((bf16[2,16,2048]{2,1,0:T(8,128)(2,1)S(1)}, bf16[2,16,2048]{2,1,0:T(8,128)(2,1)S(1)}, u32[]{:S(2)}, u32[]{:S(2)}) %collective-permute-start.9) | collective-permute-done | bytes 131104 | tf_op jit(solution)/shard_map/ppermute | solution.py:502
  52.6 0.0 collective-permute-start.13
  52.6 0.0 collective-permute-done.15.refs_7_
  52.6 0.0 collective-permute-done.12.refs_6_
  52.6 0.0 collective-permute-done.11.refs_5_
  52.7 0.0 collective-permute-done.10.refs_4_
  52.7 1.4 %attend.2.refs_8_ = bf16[2,64,1024]{2,1,0:T(8,128)(2,1)S(1)} custom-call(f32[4,512,128]{2,1,0:T(8,128)S(1)} %get-tuple-element.47.heads_ref, f32[4,512,128]{2,1,0:T(8,128)S(1)} %get-tuple-element.48.score_ref, f32[4,512,128]{2,1,0:T(8,128)S(1)} %get-tuple-element.49.fresh_k_ref, f32[4,512,128]{2,1,0:T(8,128)S(1)} %get-tuple-element.50.fresh_v_ref, ...), custom_call_target="tpu_custom_call" | custom-call | tf_op jit(solution)/shard_map/attend/pallas_call | solution.py:435
  54.1 0.0 collective-permute-done.13.refs_7_
  54.1 2.1 %attend.3 = bf16[64,4096]{1,0:T(8,128)(2,1)} custom-call(f32[4,512,128]{2,1,0:T(8,128)S(1)} %get-tuple-element.47.heads_ref, f32[4,512,128]{2,1,0:T(8,128)S(1)} %get-tuple-element.48.score_ref, f32[4,512,128]{2,1,0:T(8,128)S(1)} %get-tuple-element.49.fresh_k_ref, f32[4,512,128]{2,1,0:T(8,128)S(1)} %get-tuple-element.50.fresh_v_ref, ...), custom_call_target="tpu_custom_call" | custom-call | tf_op jit(solution)/shard_map/attend/pallas_call | solution.py:435
  (5 shorter events, 0.0 us)
Async XLA Ops:
  0.0 3.3 %collective-permute-start = (bf16[2,64,4096]{2,1,0:T(8,128)(2,1)}, bf16[2,64,4096]{2,1,0:T(8,128)(2,1)S(1)}, u32[]{:S(2)}, u32[]{:S(2)}) collective-permute-start(bf16[2,64,4096]{2,1,0:T(8,128)(2,1)} %bitcast.8), channel_id=1, source_target_pairs={{0,1},{1,0},{2,3},{3,2},{4,5},{5,4},{6,7},{7,6},{8,9},{9,8},{10,11... | collective-permute-start | bytes 3145736 | tf_op jit(solution)/shard_map/ppermute | solution.py:506
  0.7 4.0 %collective-permute-start.1 = (bf16[2,64,4096]{2,1,0:T(8,128)(2,1)}, bf16[2,64,4096]{2,1,0:T(8,128)(2,1)S(1)}, u32[]{:S(2)}, u32[]{:S(2)}) collective-permute-start(bf16[2,64,4096]{2,1,0:T(8,128)(2,1)} %up_hbm), channel_id=1, source_target_pairs={{0,1},{1,0},{2,3},{3,2},{4,5},{5,4},{6,7},{7,6},{8,9},{9,8},{10,11... | collective-permute-start | bytes 3145736 | tf_op jit(solution)/shard_map/ppermute | solution.py:506
  2.3 13.0 %collective-permute-start.4 = (bf16[16,8320]{1,0:T(8,128)(2,1)S(1)}, bf16[16,8320]{1,0:T(8,128)(2,1)S(1)}, u32[]{:S(2)}, u32[]{:S(2)}) collective-permute-start(bf16[16,8320]{1,0:T(8,128)(2,1)S(1)} %get-tuple-element.59), channel_id=1, source_target_pairs={{0,8},{1,11},{2,10},{3,9},{4,12},{5,15},{6,14},{7,13},{8,0},{9,3},... | collective-permute-start | bytes 798728 | tf_op jit(solution)/shard_map/ppermute | solution.py:502
  5.0 11.4 %collective-permute-start.2 = (bf16[16,8320]{1,0:T(8,128)(2,1)S(1)}, bf16[16,8320]{1,0:T(8,128)(2,1)S(1)}, u32[]{:S(2)}, u32[]{:S(2)}) collective-permute-start(bf16[16,8320]{1,0:T(8,128)(2,1)S(1)} %get-tuple-element.57), channel_id=1, source_target_pairs={{0,0},{1,3},{2,2},{3,1},{4,4},{5,7},{6,6},{7,5},{8,8},{9,11},{10,1... | collective-permute-start | bytes 798728 | tf_op jit(solution)/shard_map/ppermute | solution.py:502
  8.1 17.2 %collective-permute-start.3 = (bf16[16,8320]{1,0:T(8,128)(2,1)S(1)}, bf16[16,8320]{1,0:T(8,128)(2,1)S(1)}, u32[]{:S(2)}, u32[]{:S(2)}) collective-permute-start(bf16[16,8320]{1,0:T(8,128)(2,1)S(1)} %get-tuple-element.58), channel_id=1, source_target_pairs={{0,4},{1,7},{2,6},{3,5},{4,0},{5,3},{6,2},{7,1},{8,12},{9,15},{10,... | collective-permute-start | bytes 798728 | tf_op jit(solution)/shard_map/ppermute | solution.py:502
  9.4 23.2 %collective-permute-start.8 = (bf16[16,8320]{1,0:T(8,128)(2,1)S(1)}, bf16[16,8320]{1,0:T(8,128)(2,1)S(1)}, u32[]{:S(2)}, u32[]{:S(2)}) collective-permute-start(bf16[16,8320]{1,0:T(8,128)(2,1)S(1)} %get-tuple-element.67), channel_id=1, source_target_pairs={{0,12},{1,15},{2,14},{3,13},{4,8},{5,11},{6,10},{7,9},{8,4},{9,7},... | collective-permute-start | bytes 798728 | tf_op jit(solution)/shard_map/ppermute | solution.py:502
  26.5 14.2 %collective-permute-start.7 = (bf16[2,16,4096]{2,1,0:T(8,128)(2,1)S(1)}, bf16[2,16,4096]{2,1,0:T(8,128)(2,1)S(1)}, u32[]{:S(2)}, u32[]{:S(2)}) collective-permute-start(bf16[2,16,4096]{2,1,0:T(8,128)(2,1)S(1)} %serve.3), channel_id=1, source_target_pairs={{0,8},{1,11},{2,10},{3,9},{4,12},{5,15},{6,14},{7,13},{8,0},{9,3},... | collective-permute-start | bytes 786440 | tf_op jit(solution)/shard_map/ppermute | solution.py:502
  27.5 14.1 %collective-permute-start.6 = (bf16[2,16,4096]{2,1,0:T(8,128)(2,1)S(1)}, bf16[2,16,4096]{2,1,0:T(8,128)(2,1)S(1)}, u32[]{:S(2)}, u32[]{:S(2)}) collective-permute-start(bf16[2,16,4096]{2,1,0:T(8,128)(2,1)S(1)} %get-tuple-element.65), channel_id=1, source_target_pairs={{0,4},{1,7},{2,6},{3,5},{4,0},{5,3},{6,2},{7,1},{8,12},{9,15},{10,... | collective-permute-start | bytes 786440 | tf_op jit(solution)/shard_map/ppermute | solution.py:502
  29.5 12.2 %collective-permute-start.5 = (bf16[2,16,4096]{2,1,0:T(8,128)(2,1)S(1)}, bf16[2,16,4096]{2,1,0:T(8,128)(2,1)S(1)}, u32[]{:S(2)}, u32[]{:S(2)}) collective-permute-start(bf16[2,16,4096]{2,1,0:T(8,128)(2,1)S(1)} %get-tuple-element.64), channel_id=1, source_target_pairs={{0,0},{1,3},{2,2},{3,1},{4,4},{5,7},{6,6},{7,5},{8,8},{9,11},{10,1... | collective-permute-start | bytes 786440 | tf_op jit(solution)/shard_map/ppermute | solution.py:502
  33.7 16.2 %collective-permute-start.14 = (bf16[2,16,2048]{2,1,0:T(8,128)(2,1)S(1)}, bf16[2,16,2048]{2,1,0:T(8,128)(2,1)S(1)}, u32[]{:S(2)}, u32[]{:S(2)}) collective-permute-start(bf16[2,16,2048]{2,1,0:T(8,128)(2,1)S(1)} %get-tuple-element.70), channel_id=1, source_target_pairs={{0,12},{1,15},{2,14},{3,13},{4,8},{5,11},{6,10},{7,9},{8,4},{9,7},... | collective-permute-start | bytes 393224 | tf_op jit(solution)/shard_map/ppermute | solution.py:502
  34.8 17.8 %collective-permute-start.9 = (bf16[2,16,2048]{2,1,0:T(8,128)(2,1)S(1)}, bf16[2,16,2048]{2,1,0:T(8,128)(2,1)S(1)}, u32[]{:S(2)}, u32[]{:S(2)}) collective-permute-start(bf16[2,16,2048]{2,1,0:T(8,128)(2,1)S(1)} %get-tuple-element.69), channel_id=1, source_target_pairs={{0,12},{1,15},{2,14},{3,13},{4,8},{5,11},{6,10},{7,9},{8,4},{9,7},... | collective-permute-start | bytes 393224 | tf_op jit(solution)/shard_map/ppermute | solution.py:502
  40.7 11.9 %collective-permute-start.12 = (bf16[16,4096]{1,0:T(8,128)(2,1)S(1)}, bf16[16,4096]{1,0:T(8,128)(2,1)S(1)}, u32[]{:S(2)}, u32[]{:S(2)}) collective-permute-start(bf16[16,4096]{1,0:T(8,128)(2,1)S(1)} %theirs.7), channel_id=1, source_target_pairs={{0,1},{1,0},{2,3},{3,2},{4,5},{5,4},{6,7},{7,6},{8,9},{9,8},{10,11... | collective-permute-start | bytes 393224 | tf_op jit(solution)/shard_map/ppermute | solution.py:506
  41.6 11.1 %collective-permute-start.11 = (bf16[16,4096]{1,0:T(8,128)(2,1)S(1)}, bf16[16,4096]{1,0:T(8,128)(2,1)S(1)}, u32[]{:S(2)}, u32[]{:S(2)}) collective-permute-start(bf16[16,4096]{1,0:T(8,128)(2,1)S(1)} %theirs.6), channel_id=1, source_target_pairs={{0,1},{1,0},{2,3},{3,2},{4,5},{5,4},{6,7},{7,6},{8,9},{9,8},{10,11... | collective-permute-start | bytes 393224 | tf_op jit(solution)/shard_map/ppermute | solution.py:506
  41.7 11.0 %collective-permute-start.10 = (bf16[16,4096]{1,0:T(8,128)(2,1)S(1)}, bf16[16,4096]{1,0:T(8,128)(2,1)S(1)}, u32[]{:S(2)}, u32[]{:S(2)}) collective-permute-start(bf16[16,4096]{1,0:T(8,128)(2,1)S(1)} %theirs.5), channel_id=1, source_target_pairs={{0,1},{1,0},{2,3},{3,2},{4,5},{5,4},{6,7},{7,6},{8,9},{9,8},{10,11... | collective-permute-start | bytes 393224 | tf_op jit(solution)/shard_map/ppermute | solution.py:506
  49.9 2.7 %collective-permute-start.15 = (bf16[16,2048]{1,0:T(8,128)(2,1)S(1)}, bf16[16,2048]{1,0:T(8,128)(2,1)S(1)}, u32[]{:S(2)}, u32[]{:S(2)}) collective-permute-start(bf16[16,2048]{1,0:T(8,128)(2,1)S(1)} %theirs.9), channel_id=1, source_target_pairs={{0,1},{1,0},{2,3},{3,2},{4,5},{5,4},{6,7},{7,6},{8,9},{9,8},{10,11... | collective-permute-start | bytes 196616 | tf_op jit(solution)/shard_map/ppermute | solution.py:506
  52.6 1.5 %collective-permute-start.13 = (bf16[16,2048]{1,0:T(8,128)(2,1)S(1)}, bf16[16,2048]{1,0:T(8,128)(2,1)S(1)}, u32[]{:S(2)}, u32[]{:S(2)}) collective-permute-start(bf16[16,2048]{1,0:T(8,128)(2,1)S(1)} %theirs.8), channel_id=1, source_target_pairs={{0,1},{1,0},{2,3},{3,2},{4,5},{5,4},{6,7},{7,6},{8,9},{9,8},{10,11... | collective-permute-start | bytes 196616 | tf_op jit(solution)/shard_map/ppermute | solution.py:506

commit v7 on v6

--- a/solution.py
+++ b/solution.py
@@ -533,9 +533,9 @@
     groups = [*pack_near(*ready, far_rows), *far_rows]
     arrived = {g: move(g, groups[g]) for g in [*far, last, *near]}
     early = serve([arrived[g] for g in far], factors)
-    served = serve(after([arrived[g] for g in near], early[0]), factors)
+    served = serve([arrived[g] for g in near], factors)
     returned = {g: move(g, rows) for g, rows in zip(near, served)}
-    returned |= {g: move(g, rows) for g, rows in zip(far, after(early, served[0]))}
+    returned |= {g: move(g, rows) for g, rows in zip(far, early)}
     final = serve(after([arrived[last]], served[0]), factors, parts=2, extra=0)
     final = [move(last, rows) for rows in final]
 

time: 56.4 us -> 56.4 us (level)
  starting transfers between devices: 15.4 us -> 21.5 us
  waiting for transfers between devices: 27.5 us -> 21.5 us
    ppermute x9, waiting for transfers between devices: 26.2 us -> 20.2 us  [move(): parts.append(lax.ppermute(part, ('pool', 'tp'), pairs))]
    ppermute x9, starting transfers between devices: 14 us -> 18 us  [move(): parts.append(lax.ppermute(part, ('pool', 'tp'), pairs))]
    ppermute x7, starting transfers between devices: 1.37 us -> 3.47 us  [swap(): return lax.ppermute(array, 'tp', [(0, 1), (1, 0)])]
where the time goes in v7:
time: 56.4 us; the launch traced here: 56.2 us
  starting transfers between devices  21.5 us (38%)
  waiting for transfers between devices  21.5 us (38%)
  Pallas kernels  13.2 us (23%)
    ppermute x9, waiting for transfers between devices, move(): parts.append(lax.ppermute(part, ('pool', 'tp'), pairs))  20.2 us
    ppermute x9, starting transfers between devices, move(): parts.append(lax.ppermute(part, ('pool', 'tp'), pairs))  18 us
    pallas_call x1, Pallas kernels, prepare(): pl.pallas_call(prepare_kernel, out_shape=[pltpu.VMEM((cached_count, rows,...  4.36 us
    pallas_call x2, Pallas kernels, attend(): pl.pallas_call(functools.partial(attend_kernel, first, [begin for _, begi...  3.59 us
    ppermute x7, starting transfers between devices, swap(): return lax.ppermute(array, 'tp', [(0, 1), (1, 0)])  3.47 us
    pallas_call x3, Pallas kernels, serve(): pl.pallas_call(functools.partial(serve_kernel, len(rows), parts), out_sha...  3.32 us
    pallas_call x1, Pallas kernels, pack(): pl.pallas_call(functools.partial(pack_kernel, pool_count, tp_count, capac...  1.57 us
    ppermute x7, waiting for transfers between devices, swap(): return lax.ppermute(array, 'tp', [(0, 1), (1, 0)])  1.36 us
  transfers between devices with their start and end apart: 16, of which 7 were waited for; matrix products, arithmetic and copies ran while one was open for 0% of the time, Pallas kernels for 20%

profile of v7, /device:TPU:19, one launch (start us, length us, event | category | flops | bytes accessed | tf_op | source)
XLA Modules:
  0.0 56.2 jit_solution(15754853126935561940)
XLA Ops:
  0.0 0.7 %collective-permute-start = (bf16[2,64,4096]{2,1,0:T(8,128)(2,1)}, bf16[2,64,4096]{2,1,0:T(8,128)(2,1)S(1)}, u32[]{:S(2)}, u32[]{:S(2)}) collective-permute-start(bf16[2,64,4096]{2,1,0:T(8,128)(2,1)} %bitcast.8), channel_id=1, source_target_pairs={{0,1},{1,0},{2,3},{3,2},{4,5},{5,4},{6,7},{7,6},{8,9},{9,8},{10,11... | collective-permute-start | bytes 3145736 | tf_op jit(solution)/shard_map/ppermute | solution.py:506
  0.7 0.0 collective-permute-start.1
  0.7 1.6 %pack.1 = (bf16[16,8320]{1,0:T(8,128)(2,1)S(1)}, bf16[16,8320]{1,0:T(8,128)(2,1)S(1)}, bf16[64,128]{1,0:T(8,128)(2,1)S(1)}, s32[2,64]{1,0:T(2,128)S(1)}, bf16[64,8192]{1,0:T(8,128)(2,1)S(1)}) custom-call(s32[1,64]{1,0:T(1,128)} %bitcast.10, s32[1,16]{1,0:T(1,128)} %bitcast.11, bf16[64,8192]{1,0:T(8,128)(2,1)} %hidden_hbm.1), custom_call_target="tpu_custom_call" | custom-call | tf_op jit(solution)/shard_map/pack/pallas_call | solution.py:118
  2.3 1.1 %collective-permute-start.6 = (bf16[16,8320]{1,0:T(8,128)(2,1)S(1)}, bf16[16,8320]{1,0:T(8,128)(2,1)S(1)}, u32[]{:S(2)}, u32[]{:S(2)}) collective-permute-start(bf16[16,8320]{1,0:T(8,128)(2,1)S(1)} %get-tuple-element.60), channel_id=1, source_target_pairs={{0,8},{1,11},{2,10},{3,9},{4,12},{5,15},{6,14},{7,13},{8,0},{9,3},... | collective-permute-start | bytes 798728 | tf_op jit(solution)/shard_map/ppermute | solution.py:502
  3.3 0.0 collective-permute-done.refs_3_.refs_2_
  3.3 1.3 %collective-permute-done.1.refs_5_.refs_4_ = bf16[2,64,4096]{2,1,0:T(8,128)(2,1)S(1)} collective-permute-done((bf16[2,64,4096]{2,1,0:T(8,128)(2,1)}, bf16[2,64,4096]{2,1,0:T(8,128)(2,1)S(1)}, u32[]{:S(2)}, u32[]{:S(2)}) %collective-permute-start.1) | collective-permute-done | bytes 1048608 | tf_op jit(solution)/shard_map/ppermute | solution.py:506
  4.7 0.3 pack_near.1
  5.0 3.2 %collective-permute-start.2 = (bf16[16,8320]{1,0:T(8,128)(2,1)S(1)}, bf16[16,8320]{1,0:T(8,128)(2,1)S(1)}, u32[]{:S(2)}, u32[]{:S(2)}) collective-permute-start(bf16[16,8320]{1,0:T(8,128)(2,1)S(1)} %get-tuple-element.54), channel_id=1, source_target_pairs={{0,0},{1,3},{2,2},{3,1},{4,4},{5,7},{6,6},{7,5},{8,8},{9,11},{10,1... | collective-permute-start | bytes 798728 | tf_op jit(solution)/shard_map/ppermute | solution.py:502
  8.1 1.3 %collective-permute-start.3 = (bf16[16,8320]{1,0:T(8,128)(2,1)S(1)}, bf16[16,8320]{1,0:T(8,128)(2,1)S(1)}, u32[]{:S(2)}, u32[]{:S(2)}) collective-permute-start(bf16[16,8320]{1,0:T(8,128)(2,1)S(1)} %get-tuple-element.55), channel_id=1, source_target_pairs={{0,4},{1,7},{2,6},{3,5},{4,0},{5,3},{6,2},{7,1},{8,12},{9,15},{10,... | collective-permute-start | bytes 798728 | tf_op jit(solution)/shard_map/ppermute | solution.py:502
  9.4 0.0 collective-permute-start.8
  9.4 4.4 %prepare.1 = (f32[4,512,128]{2,1,0:T(8,128)S(1)}, f32[4,512,128]{2,1,0:T(8,128)S(1)}, f32[4,512,128]{2,1,0:T(8,128)S(1)}, f32[4,512,128]{2,1,0:T(8,128)S(1)}, bf...) custom-call(bf16[64,4096]{1,0:T(8,128)(2,1)} %base_hbm, ...), custom_call_target="tpu_custom_call" | custom-call | bytes 10485760 | tf_op jit(solution)/shard_map/prepare/pallas_call | solution.py:300
  13.8 1.5 %collective-permute-done.6.refs_0_ = bf16[16,8320]{1,0:T(8,128)(2,1)S(1)} collective-permute-done((bf16[16,8320]{1,0:T(8,128)(2,1)S(1)}, bf16[16,8320]{1,0:T(8,128)(2,1)S(1)}, u32[]{:S(2)}, u32[]{:S(2)}) %collective-permute-start.6) | collective-permute-done | bytes 266272 | tf_op jit(solution)/shard_map/ppermute | solution.py:502
  15.3 1.1 %serve.4 = bf16[2,16,4096]{2,1,0:T(8,128)(2,1)S(1)} custom-call(bf16[16,8320]{1,0:T(8,128)(2,1)S(1)} %collective-permute-done.6.refs_0_, bf16[2,64,4096]{2,1,0:T(8,128)(2,1)S(1)} %get-tuple-element.56.refs_2_.refs_1_, bf16[2,64,4096]{2,1,0:T(8,128)(2,1)S(1)} %collective-permute-done.refs_3_.refs_2_, ...), custom_call_target="tpu_custom_call" | custom-call | tf_op jit(solution)/shard_map/serve/pallas_call | solution.py:202
  16.4 4.0 %collective-permute-start.7 = (bf16[2,16,4096]{2,1,0:T(8,128)(2,1)S(1)}, bf16[2,16,4096]{2,1,0:T(8,128)(2,1)S(1)}, u32[]{:S(2)}, u32[]{:S(2)}) collective-permute-start(bf16[2,16,4096]{2,1,0:T(8,128)(2,1)S(1)} %serve.4), channel_id=1, source_target_pairs={{0,8},{1,11},{2,10},{3,9},{4,12},{5,15},{6,14},{7,13},{8,0},{9,3},... | collective-permute-start | bytes 786440 | tf_op jit(solution)/shard_map/ppermute | solution.py:502
  20.4 0.0 collective-permute-done.2.refs_0_
  20.4 4.9 %collective-permute-done.3.refs_1_ = bf16[16,8320]{1,0:T(8,128)(2,1)S(1)} collective-permute-done((bf16[16,8320]{1,0:T(8,128)(2,1)S(1)}, bf16[16,8320]{1,0:T(8,128)(2,1)S(1)}, u32[]{:S(2)}, u32[]{:S(2)}) %collective-permute-start.3) | collective-permute-done | bytes 266272 | tf_op jit(solution)/shard_map/ppermute | solution.py:502
  25.4 1.1 %serve.3 = (bf16[2,16,4096]{2,1,0:T(8,128)(2,1)S(1)}, bf16[2,16,4096]{2,1,0:T(8,128)(2,1)S(1)}) custom-call(bf16[16,8320]{1,0:T(8,128)(2,1)S(1)} %collective-permute-done.2.refs_0_, bf16[16,8320]{1,0:T(8,128)(2,1)S(1)} %collective-permute-done.3.refs_1_, bf16[2,64,4096]{2,1,0:T(8,128)(2,1)S(1)} %get-tuple-element.56.refs_2_.refs_1_, ...), custom_call_target="tpu_custom_call" | custom-call | tf_op jit(solution)/shard_map/serve/pallas_call | solution.py:202
  26.5 2.9 %collective-permute-start.5 = (bf16[2,16,4096]{2,1,0:T(8,128)(2,1)S(1)}, bf16[2,16,4096]{2,1,0:T(8,128)(2,1)S(1)}, u32[]{:S(2)}, u32[]{:S(2)}) collective-permute-start(bf16[2,16,4096]{2,1,0:T(8,128)(2,1)S(1)} %get-tuple-element.59), channel_id=1, source_target_pairs={{0,4},{1,7},{2,6},{3,5},{4,0},{5,3},{6,2},{7,1},{8,12},{9,15},{10,... | collective-permute-start | bytes 786440 | tf_op jit(solution)/shard_map/ppermute | solution.py:502
  29.4 3.1 %collective-permute-start.4 = (bf16[2,16,4096]{2,1,0:T(8,128)(2,1)S(1)}, bf16[2,16,4096]{2,1,0:T(8,128)(2,1)S(1)}, u32[]{:S(2)}, u32[]{:S(2)}) collective-permute-start(bf16[2,16,4096]{2,1,0:T(8,128)(2,1)S(1)} %get-tuple-element.58), channel_id=1, source_target_pairs={{0,0},{1,3},{2,2},{3,1},{4,4},{5,7},{6,6},{7,5},{8,8},{9,11},{10,1... | collective-permute-start | bytes 786440 | tf_op jit(solution)/shard_map/ppermute | solution.py:502
  32.5 2.5 %collective-permute-done.8.refs_0_ = bf16[16,8320]{1,0:T(8,128)(2,1)S(1)} collective-permute-done((bf16[16,8320]{1,0:T(8,128)(2,1)S(1)}, bf16[16,8320]{1,0:T(8,128)(2,1)S(1)}, u32[]{:S(2)}, u32[]{:S(2)}) %collective-permute-start.8) | collective-permute-done | bytes 266272 | tf_op jit(solution)/shard_map/ppermute | solution.py:502
  35.0 1.1 %serve.5 = (bf16[2,16,2048]{2,1,0:T(8,128)(2,1)S(1)}, bf16[2,16,2048]{2,1,0:T(8,128)(2,1)S(1)}) custom-call(bf16[16,8320]{1,0:T(8,128)(2,1)S(1)} %collective-permute-done.8.refs_0_, bf16[2,64,4096]{2,1,0:T(8,128)(2,1)S(1)} %get-tuple-element.56.refs_2_.refs_1_, bf16[2,64,4096]{2,1,0:T(8,128)(2,1)S(1)} %collective-permute-done.refs_3_.refs_2_, ...), custom_call_target="tpu_custom_call" | custom-call | tf_op jit(solution)/shard_map/serve/pallas_call | solution.py:202
  36.1 0.7 %collective-permute-start.14 = (bf16[2,16,2048]{2,1,0:T(8,128)(2,1)S(1)}, bf16[2,16,2048]{2,1,0:T(8,128)(2,1)S(1)}, u32[]{:S(2)}, u32[]{:S(2)}) collective-permute-start(bf16[2,16,2048]{2,1,0:T(8,128)(2,1)S(1)} %get-tuple-element.64), channel_id=1, source_target_pairs={{0,12},{1,15},{2,14},{3,13},{4,8},{5,11},{6,10},{7,9},{8,4},{9,7},... | collective-permute-start | bytes 393224 | tf_op jit(solution)/shard_map/ppermute | solution.py:502
  36.8 1.7 %collective-permute-start.9 = (bf16[2,16,2048]{2,1,0:T(8,128)(2,1)S(1)}, bf16[2,16,2048]{2,1,0:T(8,128)(2,1)S(1)}, u32[]{:S(2)}, u32[]{:S(2)}) collective-permute-start(bf16[2,16,2048]{2,1,0:T(8,128)(2,1)S(1)} %get-tuple-element.63), channel_id=1, source_target_pairs={{0,12},{1,15},{2,14},{3,13},{4,8},{5,11},{6,10},{7,9},{8,4},{9,7},... | collective-permute-start | bytes 393224 | tf_op jit(solution)/shard_map/ppermute | solution.py:502
  38.6 5.0 %collective-permute-done.7.rows_ref.refs_2_ = bf16[2,16,4096]{2,1,0:T(8,128)(2,1)S(1)} collective-permute-done((bf16[2,16,4096]{2,1,0:T(8,128)(2,1)S(1)}, bf16[2,16,4096]{2,1,0:T(8,128)(2,1)S(1)}, u32[]{:S(2)}, u32[]{:S(2)}) %collective-permute-start.7) | collective-permute-done | bytes 262176 | tf_op jit(solution)/shard_map/ppermute | solution.py:502
  43.6 0.5 collective-permute-start.12
  44.0 0.0 collective-permute-done.5.rows_ref.refs_1_
  44.1 0.2 collective-permute-start.11
  44.2 0.0 collective-permute-done.4.rows_ref.refs_0_
  44.2 0.5 collective-permute-start.10
  44.7 4.2 %collective-permute-done.14.rows_ref.refs_3_ = bf16[2,16,2048]{2,1,0:T(8,128)(2,1)S(1)} collective-permute-done((bf16[2,16,2048]{2,1,0:T(8,128)(2,1)S(1)}, bf16[2,16,2048]{2,1,0:T(8,128)(2,1)S(1)}, u32[]{:S(2)}, u32[]{:S(2)}) %collective-permute-start.14) | collective-permute-done | bytes 131104 | tf_op jit(solution)/shard_map/ppermute | solution.py:502
  49.0 0.8 %collective-permute-start.15 = (bf16[16,2048]{1,0:T(8,128)(2,1)S(1)}, bf16[16,2048]{1,0:T(8,128)(2,1)S(1)}, u32[]{:S(2)}, u32[]{:S(2)}) collective-permute-start(bf16[16,2048]{1,0:T(8,128)(2,1)S(1)} %theirs.9), channel_id=1, source_target_pairs={{0,1},{1,0},{2,3},{3,2},{4,5},{5,4},{6,7},{7,6},{8,9},{9,8},{10,11... | collective-permute-start | bytes 196616 | tf_op jit(solution)/shard_map/ppermute | solution.py:506
  49.8 2.0 %collective-permute-done.9.rows_ref.refs_3_ = bf16[2,16,2048]{2,1,0:T(8,128)(2,1)S(1)} collective-permute-done((bf16[2,16,2048]{2,1,0:T(8,128)(2,1)S(1)}, bf16[2,16,2048]{2,1,0:T(8,128)(2,1)S(1)}, u32[]{:S(2)}, u32[]{:S(2)}) %collective-permute-start.9) | collective-permute-done | bytes 131104 | tf_op jit(solution)/shard_map/ppermute | solution.py:502
  51.8 0.8 %collective-permute-start.13 = (bf16[16,2048]{1,0:T(8,128)(2,1)S(1)}, bf16[16,2048]{1,0:T(8,128)(2,1)S(1)}, u32[]{:S(2)}, u32[]{:S(2)}) collective-permute-start(bf16[16,2048]{1,0:T(8,128)(2,1)S(1)} %theirs.8), channel_id=1, source_target_pairs={{0,1},{1,0},{2,3},{3,2},{4,5},{5,4},{6,7},{7,6},{8,9},{9,8},{10,11... | collective-permute-start | bytes 196616 | tf_op jit(solution)/shard_map/ppermute | solution.py:506
  52.6 0.0 collective-permute-done.12.refs_6_
  52.6 0.0 collective-permute-done.15.refs_7_
  52.6 0.0 collective-permute-done.11.refs_5_
  52.6 0.0 collective-permute-done.10.refs_4_
  52.6 1.4 %attend.2.refs_8_ = bf16[2,64,1024]{2,1,0:T(8,128)(2,1)S(1)} custom-call(f32[4,512,128]{2,1,0:T(8,128)S(1)} %get-tuple-element.44.heads_ref, f32[4,512,128]{2,1,0:T(8,128)S(1)} %get-tuple-element.45.score_ref, f32[4,512,128]{2,1,0:T(8,128)S(1)} %get-tuple-element.46.fresh_k_ref, f32[4,512,128]{2,1,0:T(8,128)S(1)} %get-tuple-element.47.fresh_v_ref, ...), custom_call_target="tpu_custom_call" | custom-call | tf_op jit(solution)/shard_map/attend/pallas_call | solution.py:435
  54.1 0.0 collective-permute-done.13.refs_7_
  54.1 2.1 %attend.3 = bf16[64,4096]{1,0:T(8,128)(2,1)} custom-call(f32[4,512,128]{2,1,0:T(8,128)S(1)} %get-tuple-element.44.heads_ref, f32[4,512,128]{2,1,0:T(8,128)S(1)} %get-tuple-element.45.score_ref, f32[4,512,128]{2,1,0:T(8,128)S(1)} %get-tuple-element.46.fresh_k_ref, f32[4,512,128]{2,1,0:T(8,128)S(1)} %get-tuple-element.47.fresh_v_ref, ...), custom_call_target="tpu_custom_call" | custom-call | tf_op jit(solution)/shard_map/attend/pallas_call | solution.py:435
  (5 shorter events, 0.0 us)
Async XLA Ops:
  0.0 3.3 %collective-permute-start = (bf16[2,64,4096]{2,1,0:T(8,128)(2,1)}, bf16[2,64,4096]{2,1,0:T(8,128)(2,1)S(1)}, u32[]{:S(2)}, u32[]{:S(2)}) collective-permute-start(bf16[2,64,4096]{2,1,0:T(8,128)(2,1)} %bitcast.8), channel_id=1, source_target_pairs={{0,1},{1,0},{2,3},{3,2},{4,5},{5,4},{6,7},{7,6},{8,9},{9,8},{10,11... | collective-permute-start | bytes 3145736 | tf_op jit(solution)/shard_map/ppermute | solution.py:506
  0.7 4.0 %collective-permute-start.1 = (bf16[2,64,4096]{2,1,0:T(8,128)(2,1)}, bf16[2,64,4096]{2,1,0:T(8,128)(2,1)S(1)}, u32[]{:S(2)}, u32[]{:S(2)}) collective-permute-start(bf16[2,64,4096]{2,1,0:T(8,128)(2,1)} %up_hbm), channel_id=1, source_target_pairs={{0,1},{1,0},{2,3},{3,2},{4,5},{5,4},{6,7},{7,6},{8,9},{9,8},{10,11... | collective-permute-start | bytes 3145736 | tf_op jit(solution)/shard_map/ppermute | solution.py:506
  2.3 13.0 %collective-permute-start.6 = (bf16[16,8320]{1,0:T(8,128)(2,1)S(1)}, bf16[16,8320]{1,0:T(8,128)(2,1)S(1)}, u32[]{:S(2)}, u32[]{:S(2)}) collective-permute-start(bf16[16,8320]{1,0:T(8,128)(2,1)S(1)} %get-tuple-element.60), channel_id=1, source_target_pairs={{0,8},{1,11},{2,10},{3,9},{4,12},{5,15},{6,14},{7,13},{8,0},{9,3},... | collective-permute-start | bytes 798728 | tf_op jit(solution)/shard_map/ppermute | solution.py:502
  5.0 15.5 %collective-permute-start.2 = (bf16[16,8320]{1,0:T(8,128)(2,1)S(1)}, bf16[16,8320]{1,0:T(8,128)(2,1)S(1)}, u32[]{:S(2)}, u32[]{:S(2)}) collective-permute-start(bf16[16,8320]{1,0:T(8,128)(2,1)S(1)} %get-tuple-element.54), channel_id=1, source_target_pairs={{0,0},{1,3},{2,2},{3,1},{4,4},{5,7},{6,6},{7,5},{8,8},{9,11},{10,1... | collective-permute-start | bytes 798728 | tf_op jit(solution)/shard_map/ppermute | solution.py:502
  8.1 17.2 %collective-permute-start.3 = (bf16[16,8320]{1,0:T(8,128)(2,1)S(1)}, bf16[16,8320]{1,0:T(8,128)(2,1)S(1)}, u32[]{:S(2)}, u32[]{:S(2)}) collective-permute-start(bf16[16,8320]{1,0:T(8,128)(2,1)S(1)} %get-tuple-element.55), channel_id=1, source_target_pairs={{0,4},{1,7},{2,6},{3,5},{4,0},{5,3},{6,2},{7,1},{8,12},{9,15},{10,... | collective-permute-start | bytes 798728 | tf_op jit(solution)/shard_map/ppermute | solution.py:502
  9.4 25.6 %collective-permute-start.8 = (bf16[16,8320]{1,0:T(8,128)(2,1)S(1)}, bf16[16,8320]{1,0:T(8,128)(2,1)S(1)}, u32[]{:S(2)}, u32[]{:S(2)}) collective-permute-start(bf16[16,8320]{1,0:T(8,128)(2,1)S(1)} %get-tuple-element.61), channel_id=1, source_target_pairs={{0,12},{1,15},{2,14},{3,13},{4,8},{5,11},{6,10},{7,9},{8,4},{9,7},... | collective-permute-start | bytes 798728 | tf_op jit(solution)/shard_map/ppermute | solution.py:502
  16.4 27.2 %collective-permute-start.7 = (bf16[2,16,4096]{2,1,0:T(8,128)(2,1)S(1)}, bf16[2,16,4096]{2,1,0:T(8,128)(2,1)S(1)}, u32[]{:S(2)}, u32[]{:S(2)}) collective-permute-start(bf16[2,16,4096]{2,1,0:T(8,128)(2,1)S(1)} %serve.4), channel_id=1, source_target_pairs={{0,8},{1,11},{2,10},{3,9},{4,12},{5,15},{6,14},{7,13},{8,0},{9,3},... | collective-permute-start | bytes 786440 | tf_op jit(solution)/shard_map/ppermute | solution.py:502
  26.5 17.5 %collective-permute-start.5 = (bf16[2,16,4096]{2,1,0:T(8,128)(2,1)S(1)}, bf16[2,16,4096]{2,1,0:T(8,128)(2,1)S(1)}, u32[]{:S(2)}, u32[]{:S(2)}) collective-permute-start(bf16[2,16,4096]{2,1,0:T(8,128)(2,1)S(1)} %get-tuple-element.59), channel_id=1, source_target_pairs={{0,4},{1,7},{2,6},{3,5},{4,0},{5,3},{6,2},{7,1},{8,12},{9,15},{10,... | collective-permute-start | bytes 786440 | tf_op jit(solution)/shard_map/ppermute | solution.py:502
  29.4 14.8 %collective-permute-start.4 = (bf16[2,16,4096]{2,1,0:T(8,128)(2,1)S(1)}, bf16[2,16,4096]{2,1,0:T(8,128)(2,1)S(1)}, u32[]{:S(2)}, u32[]{:S(2)}) collective-permute-start(bf16[2,16,4096]{2,1,0:T(8,128)(2,1)S(1)} %get-tuple-element.58), channel_id=1, source_target_pairs={{0,0},{1,3},{2,2},{3,1},{4,4},{5,7},{6,6},{7,5},{8,8},{9,11},{10,1... | collective-permute-start | bytes 786440 | tf_op jit(solution)/shard_map/ppermute | solution.py:502
  36.1 12.8 %collective-permute-start.14 = (bf16[2,16,2048]{2,1,0:T(8,128)(2,1)S(1)}, bf16[2,16,2048]{2,1,0:T(8,128)(2,1)S(1)}, u32[]{:S(2)}, u32[]{:S(2)}) collective-permute-start(bf16[2,16,2048]{2,1,0:T(8,128)(2,1)S(1)} %get-tuple-element.64), channel_id=1, source_target_pairs={{0,12},{1,15},{2,14},{3,13},{4,8},{5,11},{6,10},{7,9},{8,4},{9,7},... | collective-permute-start | bytes 393224 | tf_op jit(solution)/shard_map/ppermute | solution.py:502
  36.8 15.0 %collective-permute-start.9 = (bf16[2,16,2048]{2,1,0:T(8,128)(2,1)S(1)}, bf16[2,16,2048]{2,1,0:T(8,128)(2,1)S(1)}, u32[]{:S(2)}, u32[]{:S(2)}) collective-permute-start(bf16[2,16,2048]{2,1,0:T(8,128)(2,1)S(1)} %get-tuple-element.63), channel_id=1, source_target_pairs={{0,12},{1,15},{2,14},{3,13},{4,8},{5,11},{6,10},{7,9},{8,4},{9,7},... | collective-permute-start | bytes 393224 | tf_op jit(solution)/shard_map/ppermute | solution.py:502
  43.6 9.1 %collective-permute-start.12 = (bf16[16,4096]{1,0:T(8,128)(2,1)S(1)}, bf16[16,4096]{1,0:T(8,128)(2,1)S(1)}, u32[]{:S(2)}, u32[]{:S(2)}) collective-permute-start(bf16[16,4096]{1,0:T(8,128)(2,1)S(1)} %theirs.7), channel_id=1, source_target_pairs={{0,1},{1,0},{2,3},{3,2},{4,5},{5,4},{6,7},{7,6},{8,9},{9,8},{10,11... | collective-permute-start | bytes 393224 | tf_op jit(solution)/shard_map/ppermute | solution.py:506
  44.1 8.6 %collective-permute-start.11 = (bf16[16,4096]{1,0:T(8,128)(2,1)S(1)}, bf16[16,4096]{1,0:T(8,128)(2,1)S(1)}, u32[]{:S(2)}, u32[]{:S(2)}) collective-permute-start(bf16[16,4096]{1,0:T(8,128)(2,1)S(1)} %theirs.6), channel_id=1, source_target_pairs={{0,1},{1,0},{2,3},{3,2},{4,5},{5,4},{6,7},{7,6},{8,9},{9,8},{10,11... | collective-permute-start | bytes 393224 | tf_op jit(solution)/shard_map/ppermute | solution.py:506
  44.2 8.4 %collective-permute-start.10 = (bf16[16,4096]{1,0:T(8,128)(2,1)S(1)}, bf16[16,4096]{1,0:T(8,128)(2,1)S(1)}, u32[]{:S(2)}, u32[]{:S(2)}) collective-permute-start(bf16[16,4096]{1,0:T(8,128)(2,1)S(1)} %theirs.5), channel_id=1, source_target_pairs={{0,1},{1,0},{2,3},{3,2},{4,5},{5,4},{6,7},{7,6},{8,9},{9,8},{10,11... | collective-permute-start | bytes 393224 | tf_op jit(solution)/shard_map/ppermute | solution.py:506
  49.0 3.6 %collective-permute-start.15 = (bf16[16,2048]{1,0:T(8,128)(2,1)S(1)}, bf16[16,2048]{1,0:T(8,128)(2,1)S(1)}, u32[]{:S(2)}, u32[]{:S(2)}) collective-permute-start(bf16[16,2048]{1,0:T(8,128)(2,1)S(1)} %theirs.9), channel_id=1, source_target_pairs={{0,1},{1,0},{2,3},{3,2},{4,5},{5,4},{6,7},{7,6},{8,9},{9,8},{10,11... | collective-permute-start | bytes 196616 | tf_op jit(solution)/shard_map/ppermute | solution.py:506
  51.8 2.3 %collective-permute-start.13 = (bf16[16,2048]{1,0:T(8,128)(2,1)S(1)}, bf16[16,2048]{1,0:T(8,128)(2,1)S(1)}, u32[]{:S(2)}, u32[]{:S(2)}) collective-permute-start(bf16[16,2048]{1,0:T(8,128)(2,1)S(1)} %theirs.8), channel_id=1, source_target_pairs={{0,1},{1,0},{2,3},{3,2},{4,5},{5,4},{6,7},{7,6},{8,9},{9,8},{10,11... | collective-permute-start | bytes 196616 | tf_op jit(solution)/shard_map/ppermute | solution.py:506
